TPU v7x, 256 devices: a whole 4x4x8 slice. The times are simulated.
256 devices in a mesh: tm: 32 (over y, z_hi, core), space: 8 (over z_lo, x).
Axes of the slice: x: 4, y: 4, z: 8 (z_hi: 4, z_lo: 2; z = z_hi * 2 + z_lo), core: 2. Of those that a mesh axis runs over, the one named last changes fastest.
Arguments:
- prev_starts: float32 [32, 4, 4, 64, 128], P('tm', None, None, 'space'), may hold values from -6 to 6
- plan: int32 [32, 2], P('tm'), may hold values from 0 to 7
- cell_type: int32 [4, 64, 128], P(None, 'space'), may hold values from 0 to 2
- coarse_matrix: float32 [4, 4, 4, 64, 128], P(None, None, None, 'space'), may hold values from -0.02 to 0.94, as said below
- rate_values: float32 [8], replicated, may hold values from 0.5 to 3
- enc_weight: float32 [4, 128], replicated, may hold values from -3 to 3
- type_table: float32 [3, 128], replicated, may hold values from -3 to 3
- force_vector: float32 [128], replicated, may hold values from -6 to 6
- norm_gain: float32 [6, 128], replicated, may hold values from 0.5 to 1.5
- self_weight: bfloat16 [6, 128, 128], replicated, may hold values from -0.5 to 0.5
- neigh_weight: bfloat16 [6, 128, 128], replicated, may hold values from -0.21875 to 0.21875
- out_weight: bfloat16 [6, 128, 128], replicated, may hold values from -0.5 to 0.5
- layer_bias: float32 [6, 128], replicated, may hold values from -3 to 3
- dec_gain: float32 [128], replicated, may hold values from 0.5 to 1.5
- dec_weight: bfloat16 [4, 128], replicated, may hold values from -0.25 to 0.25
Outputs:
- corrected_ends: float32 [32, 4, 4, 64, 128], P('tm', None, None, 'space')
Inputs may be any that keep to these rules, and one draw needn't show every extreme that they name: `coarse_matrix`: diagonal entries are positive and in each cell the absolute entries of a row sum to at most 1.
All inputs are finite; a program needn't handle non-finite values.
Results may differ from a plain program's by a relative error of at most 0.0065.
Values may be sent and summed in bfloat16 or wider, within the bound.
No kernel may reach another device: no remote copies, remote signals or barrier semaphores. Data moves between devices by JAX's collectives and lax.ppermute only.
A program may use at most 64 MiB of HBM per device.

v0:
```python
import jax
import jax.numpy as jnp
from jax import lax
from jax.sharding import PartitionSpec as P

CHAN = 4
TYPES = 3
RATES = 8
LAYERS = 6
STEPS = 2


EPS = 1e-05


def with_halo(cells, sides, width):
    for axis, dim in sides:
        count = lax.axis_size(axis)
        ends = count - 1
        head = lax.slice_in_dim(cells, 0, width, axis=dim)
        tail = lax.slice_in_dim(cells, cells.shape[dim] - width, cells.shape[dim], axis=dim)
        cells = jnp.concatenate(
            [
                lax.ppermute(tail, axis, [(i, (i + 1) % count) for i in range(ends)]),
                cells,
                lax.ppermute(head, axis, [((i + 1) % count, i) for i in range(ends)]),
            ],
            axis=dim,
        )
    return cells


def passed_along(value, axis, steps):
    count = lax.axis_size(axis)
    first, last = (max(0, -steps), min(count, count - steps))
    return lax.ppermute(value, axis, [(source, source + steps) for source in range(first, last)])


def normed(hidden, gain_row):
    widened = hidden.astype(jnp.float32)
    row_mean = jnp.mean(widened, axis=-1, keepdims=True)
    row_var = jnp.mean(jnp.square(widened - row_mean), axis=-1, keepdims=True)
    return (widened - row_mean) * lax.rsqrt(row_var + EPS) * gain_row


def neighbours(padded):
    centre = padded[:, 1:-1]
    summed = padded[:, :-2].astype(jnp.float32) + padded[:, 2:].astype(jnp.float32)
    along_y = jnp.pad(centre, ((0, 0), (0, 0), (1, 1), (0, 0)))
    summed = summed + along_y[:, :, :-2].astype(jnp.float32) + along_y[:, :, 2:].astype(jnp.float32)
    along_z = jnp.pad(centre, ((1, 1), (0, 0), (0, 0), (0, 0)))
    summed = summed + along_z[:-2].astype(jnp.float32) + along_z[2:].astype(jnp.float32)
    return summed.astype(jnp.bfloat16)


def advance(hidden_mid, padded, self_w, neigh_w, out_w, bias_row):
    neigh_sum = neighbours(padded)
    centre = padded[:, 1:-1]
    preact = jnp.dot(centre, self_w, preferred_element_type=jnp.float32)
    preact = preact + jnp.dot(neigh_sum, neigh_w, preferred_element_type=jnp.float32) + bias_row
    message = jax.nn.silu(preact).astype(jnp.bfloat16)
    return (
        hidden_mid.astype(jnp.float32) + jnp.dot(message, out_w, preferred_element_type=jnp.float32)
    ).astype(jnp.bfloat16)


def encode(window_state, cell_type, rate_value, enc_weight, type_table, force_vector):
    hidden = window_state[0][..., None] * enc_weight[0]
    for channel in range(1, CHAN):
        hidden = hidden + window_state[channel][..., None] * enc_weight[channel]
    for kind_index in range(TYPES):
        hidden = (
            hidden
            + (cell_type == kind_index).astype(jnp.float32)[..., None] * type_table[kind_index]
        )
    well_sign = (cell_type == 1).astype(jnp.float32) - (cell_type == 2).astype(jnp.float32)
    hidden = hidden + (well_sign * rate_value)[..., None] * force_vector
    return hidden.astype(jnp.bfloat16)


def lookup_rate(sched_row, step_index, rate_values):
    picks = jnp.arange(RATES, dtype=jnp.int32) == sched_row[step_index]
    return jnp.sum(jnp.where(picks, rate_values, 0.0))


def decode(hidden, dec_gain, dec_weight):
    decoded = normed(hidden, dec_gain).astype(jnp.bfloat16)
    return jnp.einsum("ch,zxyh->czxy", dec_weight, decoded, preferred_element_type=jnp.float32)


def matvec(matrix, vector):
    return jnp.sum(matrix * vector[None], axis=1)


def per_device(
    prev_starts,
    plan,
    cell_type,
    coarse_matrix,
    rate_values,
    enc_weight,
    type_table,
    force_vector,
    norm_gain,
    self_weight,
    neigh_weight,
    out_weight,
    layer_bias,
    dec_gain,
    dec_weight,
):
    window_state = prev_starts[0]
    sched_row = plan[0]
    for step_index in range(STEPS):
        rate_value = lookup_rate(sched_row, step_index, rate_values)
        hidden = encode(window_state, cell_type, rate_value, enc_weight, type_table, force_vector)
        for layer_index in range(LAYERS):
            normalized = normed(hidden, norm_gain[layer_index]).astype(jnp.bfloat16)
            padded = with_halo(normalized, (("space", 1),), 1)
            hidden = advance(
                hidden,
                padded,
                self_weight[layer_index],
                neigh_weight[layer_index],
                out_weight[layer_index],
                layer_bias[layer_index],
            )
        window_state = window_state + decode(hidden, dec_gain, dec_weight)
    fine_end = window_state
    start_state = prev_starts[0]
    is_first = lax.axis_index("tm") == 0

    def turn(turn_index, current):
        result = jnp.where(
            is_first, fine_end, fine_end + matvec(coarse_matrix, current - start_state)
        )
        return passed_along(result, "tm", 1)

    current = lax.fori_loop(0, lax.axis_size("tm") - 1, turn, start_state)
    corrected = jnp.where(
        is_first, fine_end, fine_end + matvec(coarse_matrix, current - start_state)
    )
    return corrected[None]


def solution(mesh):
    return jax.shard_map(
        per_device,
        mesh=mesh,
        in_specs=(
            P("tm", None, None, "space", None),
            P("tm", None),
            P(None, "space", None),
            P(None, None, None, "space", None),
            P(),
            P(),
            P(),
            P(),
            P(),
            P(),
            P(),
            P(),
            P(),
            P(),
            P(),
        ),
        out_specs=P("tm", None, None, "space", None),
        check_vma=False,
    )
```

profile of v0, /device:TPU:20, one launch (start us, length us, event | category | flops | bytes accessed | tf_op | source)
XLA Modules:
  0.0 517.8 jit_solution(5644477335516144192)
XLA Ops:
  244.1 272.8 %while.10 = (s32[]{:T(128)}, f32[4,4,8,128]{3,2,1,0:T(8,128)S(1)}, pred[]{:T(512)}, f32[4,4,8,128]{3,2,1,0:T(8,128)S(1)}, f32[4,4,4,8,128]{4,3,2,1,0:T(8,128)S(1)}, /*index=5*/f32[4,4,8,128]{3,2,1,0:T(8,128)S(1)}, s32[]{:T(128)}) while((s32[]{:T(128)}, f32[4,4,8,128]{3,2,1,0:T(8,128)S(1)}, pred[]{:T(512)}, f32[4,4,8,128]{3,2,1,0:T(8,128)S(1)}, ...), condition=%wide.region_32.33_spmd, body=%wide.region_30.32_spmd.sunk | while | flops 163842 | bytes 1048694 | solution.py:139
  246.1 7.4 %collective-permute-done = f32[4,4,8,128]{3,2,1,0:T(8,128)S(1)} collective-permute-done((f32[4,4,8,128]{3,2,1,0:T(8,128)S(1)}, f32[4,4,8,128]{3,2,1,0:T(8,128)S(1)}, u32[]{:S(2)}, u32[]{:S(2)}) %collective-permute-start) | collective-permute-done | bytes 65568 | tf_op jit(solution)/shard_map/while/body/eval_jaxpr/ppermute | solution.py:36
  255.5 6.8 %collective-permute-done = f32[4,4,8,128]{3,2,1,0:T(8,128)S(1)} collective-permute-done((f32[4,4,8,128]{3,2,1,0:T(8,128)S(1)}, f32[4,4,8,128]{3,2,1,0:T(8,128)S(1)}, u32[]{:S(2)}, u32[]{:S(2)}) %collective-permute-start) | collective-permute-done | bytes 65568 | tf_op jit(solution)/shard_map/while/body/eval_jaxpr/ppermute | solution.py:36
  264.2 6.7 %collective-permute-done = f32[4,4,8,128]{3,2,1,0:T(8,128)S(1)} collective-permute-done((f32[4,4,8,128]{3,2,1,0:T(8,128)S(1)}, f32[4,4,8,128]{3,2,1,0:T(8,128)S(1)}, u32[]{:S(2)}, u32[]{:S(2)}) %collective-permute-start) | collective-permute-done | bytes 65568 | tf_op jit(solution)/shard_map/while/body/eval_jaxpr/ppermute | solution.py:36
  273.0 7.5 %collective-permute-done = f32[4,4,8,128]{3,2,1,0:T(8,128)S(1)} collective-permute-done((f32[4,4,8,128]{3,2,1,0:T(8,128)S(1)}, f32[4,4,8,128]{3,2,1,0:T(8,128)S(1)}, u32[]{:S(2)}, u32[]{:S(2)}) %collective-permute-start) | collective-permute-done | bytes 65568 | tf_op jit(solution)/shard_map/while/body/eval_jaxpr/ppermute | solution.py:36
  282.4 7.4 %collective-permute-done = f32[4,4,8,128]{3,2,1,0:T(8,128)S(1)} collective-permute-done((f32[4,4,8,128]{3,2,1,0:T(8,128)S(1)}, f32[4,4,8,128]{3,2,1,0:T(8,128)S(1)}, u32[]{:S(2)}, u32[]{:S(2)}) %collective-permute-start) | collective-permute-done | bytes 65568 | tf_op jit(solution)/shard_map/while/body/eval_jaxpr/ppermute | solution.py:36
  291.8 6.8 %collective-permute-done = f32[4,4,8,128]{3,2,1,0:T(8,128)S(1)} collective-permute-done((f32[4,4,8,128]{3,2,1,0:T(8,128)S(1)}, f32[4,4,8,128]{3,2,1,0:T(8,128)S(1)}, u32[]{:S(2)}, u32[]{:S(2)}) %collective-permute-start) | collective-permute-done | bytes 65568 | tf_op jit(solution)/shard_map/while/body/eval_jaxpr/ppermute | solution.py:36
  300.6 7.4 %collective-permute-done = f32[4,4,8,128]{3,2,1,0:T(8,128)S(1)} collective-permute-done((f32[4,4,8,128]{3,2,1,0:T(8,128)S(1)}, f32[4,4,8,128]{3,2,1,0:T(8,128)S(1)}, u32[]{:S(2)}, u32[]{:S(2)}) %collective-permute-start) | collective-permute-done | bytes 65568 | tf_op jit(solution)/shard_map/while/body/eval_jaxpr/ppermute | solution.py:36
  310.0 7.4 %collective-permute-done = f32[4,4,8,128]{3,2,1,0:T(8,128)S(1)} collective-permute-done((f32[4,4,8,128]{3,2,1,0:T(8,128)S(1)}, f32[4,4,8,128]{3,2,1,0:T(8,128)S(1)}, u32[]{:S(2)}, u32[]{:S(2)}) %collective-permute-start) | collective-permute-done | bytes 65568 | tf_op jit(solution)/shard_map/while/body/eval_jaxpr/ppermute | solution.py:36
  319.4 6.7 %collective-permute-done = f32[4,4,8,128]{3,2,1,0:T(8,128)S(1)} collective-permute-done((f32[4,4,8,128]{3,2,1,0:T(8,128)S(1)}, f32[4,4,8,128]{3,2,1,0:T(8,128)S(1)}, u32[]{:S(2)}, u32[]{:S(2)}) %collective-permute-start) | collective-permute-done | bytes 65568 | tf_op jit(solution)/shard_map/while/body/eval_jaxpr/ppermute | solution.py:36
  328.1 6.7 %collective-permute-done = f32[4,4,8,128]{3,2,1,0:T(8,128)S(1)} collective-permute-done((f32[4,4,8,128]{3,2,1,0:T(8,128)S(1)}, f32[4,4,8,128]{3,2,1,0:T(8,128)S(1)}, u32[]{:S(2)}, u32[]{:S(2)}) %collective-permute-start) | collective-permute-done | bytes 65568 | tf_op jit(solution)/shard_map/while/body/eval_jaxpr/ppermute | solution.py:36
  336.8 6.7 %collective-permute-done = f32[4,4,8,128]{3,2,1,0:T(8,128)S(1)} collective-permute-done((f32[4,4,8,128]{3,2,1,0:T(8,128)S(1)}, f32[4,4,8,128]{3,2,1,0:T(8,128)S(1)}, u32[]{:S(2)}, u32[]{:S(2)}) %collective-permute-start) | collective-permute-done | bytes 65568 | tf_op jit(solution)/shard_map/while/body/eval_jaxpr/ppermute | solution.py:36
  345.4 6.7 %collective-permute-done = f32[4,4,8,128]{3,2,1,0:T(8,128)S(1)} collective-permute-done((f32[4,4,8,128]{3,2,1,0:T(8,128)S(1)}, f32[4,4,8,128]{3,2,1,0:T(8,128)S(1)}, u32[]{:S(2)}, u32[]{:S(2)}) %collective-permute-start) | collective-permute-done | bytes 65568 | tf_op jit(solution)/shard_map/while/body/eval_jaxpr/ppermute | solution.py:36
  354.1 6.7 %collective-permute-done = f32[4,4,8,128]{3,2,1,0:T(8,128)S(1)} collective-permute-done((f32[4,4,8,128]{3,2,1,0:T(8,128)S(1)}, f32[4,4,8,128]{3,2,1,0:T(8,128)S(1)}, u32[]{:S(2)}, u32[]{:S(2)}) %collective-permute-start) | collective-permute-done | bytes 65568 | tf_op jit(solution)/shard_map/while/body/eval_jaxpr/ppermute | solution.py:36
  362.8 6.7 %collective-permute-done = f32[4,4,8,128]{3,2,1,0:T(8,128)S(1)} collective-permute-done((f32[4,4,8,128]{3,2,1,0:T(8,128)S(1)}, f32[4,4,8,128]{3,2,1,0:T(8,128)S(1)}, u32[]{:S(2)}, u32[]{:S(2)}) %collective-permute-start) | collective-permute-done | bytes 65568 | tf_op jit(solution)/shard_map/while/body/eval_jaxpr/ppermute | solution.py:36
  371.5 6.7 %collective-permute-done = f32[4,4,8,128]{3,2,1,0:T(8,128)S(1)} collective-permute-done((f32[4,4,8,128]{3,2,1,0:T(8,128)S(1)}, f32[4,4,8,128]{3,2,1,0:T(8,128)S(1)}, u32[]{:S(2)}, u32[]{:S(2)}) %collective-permute-start) | collective-permute-done | bytes 65568 | tf_op jit(solution)/shard_map/while/body/eval_jaxpr/ppermute | solution.py:36
  380.1 6.7 %collective-permute-done = f32[4,4,8,128]{3,2,1,0:T(8,128)S(1)} collective-permute-done((f32[4,4,8,128]{3,2,1,0:T(8,128)S(1)}, f32[4,4,8,128]{3,2,1,0:T(8,128)S(1)}, u32[]{:S(2)}, u32[]{:S(2)}) %collective-permute-start) | collective-permute-done | bytes 65568 | tf_op jit(solution)/shard_map/while/body/eval_jaxpr/ppermute | solution.py:36
  388.8 6.7 %collective-permute-done = f32[4,4,8,128]{3,2,1,0:T(8,128)S(1)} collective-permute-done((f32[4,4,8,128]{3,2,1,0:T(8,128)S(1)}, f32[4,4,8,128]{3,2,1,0:T(8,128)S(1)}, u32[]{:S(2)}, u32[]{:S(2)}) %collective-permute-start) | collective-permute-done | bytes 65568 | tf_op jit(solution)/shard_map/while/body/eval_jaxpr/ppermute | solution.py:36
  397.5 6.7 %collective-permute-done = f32[4,4,8,128]{3,2,1,0:T(8,128)S(1)} collective-permute-done((f32[4,4,8,128]{3,2,1,0:T(8,128)S(1)}, f32[4,4,8,128]{3,2,1,0:T(8,128)S(1)}, u32[]{:S(2)}, u32[]{:S(2)}) %collective-permute-start) | collective-permute-done | bytes 65568 | tf_op jit(solution)/shard_map/while/body/eval_jaxpr/ppermute | solution.py:36
  406.2 6.7 %collective-permute-done = f32[4,4,8,128]{3,2,1,0:T(8,128)S(1)} collective-permute-done((f32[4,4,8,128]{3,2,1,0:T(8,128)S(1)}, f32[4,4,8,128]{3,2,1,0:T(8,128)S(1)}, u32[]{:S(2)}, u32[]{:S(2)}) %collective-permute-start) | collective-permute-done | bytes 65568 | tf_op jit(solution)/shard_map/while/body/eval_jaxpr/ppermute | solution.py:36
  414.8 6.7 %collective-permute-done = f32[4,4,8,128]{3,2,1,0:T(8,128)S(1)} collective-permute-done((f32[4,4,8,128]{3,2,1,0:T(8,128)S(1)}, f32[4,4,8,128]{3,2,1,0:T(8,128)S(1)}, u32[]{:S(2)}, u32[]{:S(2)}) %collective-permute-start) | collective-permute-done | bytes 65568 | tf_op jit(solution)/shard_map/while/body/eval_jaxpr/ppermute | solution.py:36
  423.5 6.7 %collective-permute-done = f32[4,4,8,128]{3,2,1,0:T(8,128)S(1)} collective-permute-done((f32[4,4,8,128]{3,2,1,0:T(8,128)S(1)}, f32[4,4,8,128]{3,2,1,0:T(8,128)S(1)}, u32[]{:S(2)}, u32[]{:S(2)}) %collective-permute-start) | collective-permute-done | bytes 65568 | tf_op jit(solution)/shard_map/while/body/eval_jaxpr/ppermute | solution.py:36
  432.2 6.7 %collective-permute-done = f32[4,4,8,128]{3,2,1,0:T(8,128)S(1)} collective-permute-done((f32[4,4,8,128]{3,2,1,0:T(8,128)S(1)}, f32[4,4,8,128]{3,2,1,0:T(8,128)S(1)}, u32[]{:S(2)}, u32[]{:S(2)}) %collective-permute-start) | collective-permute-done | bytes 65568 | tf_op jit(solution)/shard_map/while/body/eval_jaxpr/ppermute | solution.py:36
  440.8 6.7 %collective-permute-done = f32[4,4,8,128]{3,2,1,0:T(8,128)S(1)} collective-permute-done((f32[4,4,8,128]{3,2,1,0:T(8,128)S(1)}, f32[4,4,8,128]{3,2,1,0:T(8,128)S(1)}, u32[]{:S(2)}, u32[]{:S(2)}) %collective-permute-start) | collective-permute-done | bytes 65568 | tf_op jit(solution)/shard_map/while/body/eval_jaxpr/ppermute | solution.py:36
  449.5 6.7 %collective-permute-done = f32[4,4,8,128]{3,2,1,0:T(8,128)S(1)} collective-permute-done((f32[4,4,8,128]{3,2,1,0:T(8,128)S(1)}, f32[4,4,8,128]{3,2,1,0:T(8,128)S(1)}, u32[]{:S(2)}, u32[]{:S(2)}) %collective-permute-start) | collective-permute-done | bytes 65568 | tf_op jit(solution)/shard_map/while/body/eval_jaxpr/ppermute | solution.py:36
  458.2 6.7 %collective-permute-done = f32[4,4,8,128]{3,2,1,0:T(8,128)S(1)} collective-permute-done((f32[4,4,8,128]{3,2,1,0:T(8,128)S(1)}, f32[4,4,8,128]{3,2,1,0:T(8,128)S(1)}, u32[]{:S(2)}, u32[]{:S(2)}) %collective-permute-start) | collective-permute-done | bytes 65568 | tf_op jit(solution)/shard_map/while/body/eval_jaxpr/ppermute | solution.py:36
  466.9 6.7 %collective-permute-done = f32[4,4,8,128]{3,2,1,0:T(8,128)S(1)} collective-permute-done((f32[4,4,8,128]{3,2,1,0:T(8,128)S(1)}, f32[4,4,8,128]{3,2,1,0:T(8,128)S(1)}, u32[]{:S(2)}, u32[]{:S(2)}) %collective-permute-start) | collective-permute-done | bytes 65568 | tf_op jit(solution)/shard_map/while/body/eval_jaxpr/ppermute | solution.py:36
  475.5 6.7 %collective-permute-done = f32[4,4,8,128]{3,2,1,0:T(8,128)S(1)} collective-permute-done((f32[4,4,8,128]{3,2,1,0:T(8,128)S(1)}, f32[4,4,8,128]{3,2,1,0:T(8,128)S(1)}, u32[]{:S(2)}, u32[]{:S(2)}) %collective-permute-start) | collective-permute-done | bytes 65568 | tf_op jit(solution)/shard_map/while/body/eval_jaxpr/ppermute | solution.py:36
  484.2 6.7 %collective-permute-done = f32[4,4,8,128]{3,2,1,0:T(8,128)S(1)} collective-permute-done((f32[4,4,8,128]{3,2,1,0:T(8,128)S(1)}, f32[4,4,8,128]{3,2,1,0:T(8,128)S(1)}, u32[]{:S(2)}, u32[]{:S(2)}) %collective-permute-start) | collective-permute-done | bytes 65568 | tf_op jit(solution)/shard_map/while/body/eval_jaxpr/ppermute | solution.py:36
  492.9 6.7 %collective-permute-done = f32[4,4,8,128]{3,2,1,0:T(8,128)S(1)} collective-permute-done((f32[4,4,8,128]{3,2,1,0:T(8,128)S(1)}, f32[4,4,8,128]{3,2,1,0:T(8,128)S(1)}, u32[]{:S(2)}, u32[]{:S(2)}) %collective-permute-start) | collective-permute-done | bytes 65568 | tf_op jit(solution)/shard_map/while/body/eval_jaxpr/ppermute | solution.py:36
  501.6 6.7 %collective-permute-done = f32[4,4,8,128]{3,2,1,0:T(8,128)S(1)} collective-permute-done((f32[4,4,8,128]{3,2,1,0:T(8,128)S(1)}, f32[4,4,8,128]{3,2,1,0:T(8,128)S(1)}, u32[]{:S(2)}, u32[]{:S(2)}) %collective-permute-start) | collective-permute-done | bytes 65568 | tf_op jit(solution)/shard_map/while/body/eval_jaxpr/ppermute | solution.py:36
  510.2 6.7 %collective-permute-done = f32[4,4,8,128]{3,2,1,0:T(8,128)S(1)} collective-permute-done((f32[4,4,8,128]{3,2,1,0:T(8,128)S(1)}, f32[4,4,8,128]{3,2,1,0:T(8,128)S(1)}, u32[]{:S(2)}, u32[]{:S(2)}) %collective-permute-start) | collective-permute-done | bytes 65568 | tf_op jit(solution)/shard_map/while/body/eval_jaxpr/ppermute | solution.py:36
  (397 shorter events, 304.6 us)
Async XLA Ops:
  36.4 9.4 %collective-permute-start.3 = (bf16[4,1,128,128]{3,2,1,0:T(8,128)(2,1)S(1)}, bf16[4,1,128,128]{3,2,1,0:T(8,128)(2,1)S(1)}, u32[]{:S(2)}, u32[]{:S(2)}) collective-permute-start(bf16[4,1,128,128]{3,2,1,0:T(8,128)(2,1)S(1)} %get-tuple-element.88), channel_id=1, source_target_pairs={{0,1},{1,2},{2,3},{3,4},{4,5},{5,6},{6,7},{8,9},{9,10},{10,11},{11... | collective-permute-start | bytes 393224 | tf_op jit(solution)/shard_map/ppermute | solution.py:24
  107.5 9.6 %collective-permute-start.11 = (bf16[4,1,128,128]{3,2,1,0:T(8,128)(2,1)S(1)}, bf16[4,1,128,128]{3,2,1,0:T(8,128)(2,1)S(1)}, u32[]{:S(2)}, u32[]{:S(2)}) collective-permute-start(bf16[4,1,128,128]{3,2,1,0:T(8,128)(2,1)S(1)} %get-tuple-element.80), channel_id=1, source_target_pairs={{0,1},{1,2},{2,3},{3,4},{4,5},{5,6},{6,7},{8,9},{9,10},{10,11},{11... | collective-permute-start | bytes 393224 | tf_op jit(solution)/shard_map/ppermute | solution.py:24
  113.2 9.4 %collective-permute-start.12 = (bf16[4,1,128,128]{3,2,1,0:T(8,128)(2,1)S(1)}, bf16[4,1,128,128]{3,2,1,0:T(8,128)(2,1)S(1)}, u32[]{:S(2)}, u32[]{:S(2)}) collective-permute-start(bf16[4,1,128,128]{3,2,1,0:T(8,128)(2,1)S(1)} %get-tuple-element.81), channel_id=1, source_target_pairs={{1,0},{2,1},{3,2},{4,3},{5,4},{6,5},{7,6},{9,8},{10,9},{11,10},{12... | collective-permute-start | bytes 393224 | tf_op jit(solution)/shard_map/ppermute | solution.py:26
  138.4 10.5 %collective-permute-start.13 = (bf16[4,1,128,128]{3,2,1,0:T(8,128)(2,1)S(1)}, bf16[4,1,128,128]{3,2,1,0:T(8,128)(2,1)S(1)}, u32[]{:S(2)}, u32[]{:S(2)}) collective-permute-start(bf16[4,1,128,128]{3,2,1,0:T(8,128)(2,1)S(1)} %get-tuple-element.78), channel_id=1, source_target_pairs={{0,1},{1,2},{2,3},{3,4},{4,5},{5,6},{6,7},{8,9},{9,10},{10,11},{11... | collective-permute-start | bytes 393224 | tf_op jit(solution)/shard_map/ppermute | solution.py:24
  174.9 8.7 %collective-permute-start.17 = (bf16[4,1,128,128]{3,2,1,0:T(8,128)(2,1)S(1)}, bf16[4,1,128,128]{3,2,1,0:T(8,128)(2,1)S(1)}, u32[]{:S(2)}, u32[]{:S(2)}) collective-permute-start(bf16[4,1,128,128]{3,2,1,0:T(8,128)(2,1)S(1)} %get-tuple-element.74), channel_id=1, source_target_pairs={{0,1},{1,2},{2,3},{3,4},{4,5},{5,6},{6,7},{8,9},{9,10},{10,11},{11... | collective-permute-start | bytes 393224 | tf_op jit(solution)/shard_map/ppermute | solution.py:24
  226.6 8.7 %collective-permute-start.23 = (bf16[4,1,128,128]{3,2,1,0:T(8,128)(2,1)S(1)}, bf16[4,1,128,128]{3,2,1,0:T(8,128)(2,1)S(1)}, u32[]{:S(2)}, u32[]{:S(2)}) collective-permute-start(bf16[4,1,128,128]{3,2,1,0:T(8,128)(2,1)S(1)} %get-tuple-element.68), channel_id=1, source_target_pairs={{0,1},{1,2},{2,3},{3,4},{4,5},{5,6},{6,7},{8,9},{9,10},{10,11},{11... | collective-permute-start | bytes 393224 | tf_op jit(solution)/shard_map/ppermute | solution.py:24
  244.2 9.3 %collective-permute-start = (f32[4,4,8,128]{3,2,1,0:T(8,128)S(1)}, f32[4,4,8,128]{3,2,1,0:T(8,128)S(1)}, u32[]{:S(2)}, u32[]{:S(2)}) collective-permute-start(f32[4,4,8,128]{3,2,1,0:T(8,128)S(1)} %add_select_fusion.3), channel_id=1, source_target_pairs={{0,8},{8,16},{16,24},{24,32},{32,40},{40,48},{48,56},{56,64},{64,7... | collective-permute-start | bytes 196616 | tf_op jit(solution)/shard_map/while/body/eval_jaxpr/ppermute | solution.py:36
  253.5 8.7 %collective-permute-start = (f32[4,4,8,128]{3,2,1,0:T(8,128)S(1)}, f32[4,4,8,128]{3,2,1,0:T(8,128)S(1)}, u32[]{:S(2)}, u32[]{:S(2)}) collective-permute-start(f32[4,4,8,128]{3,2,1,0:T(8,128)S(1)} %add_select_fusion.3), channel_id=1, source_target_pairs={{0,8},{8,16},{16,24},{24,32},{32,40},{40,48},{48,56},{56,64},{64,7... | collective-permute-start | bytes 196616 | tf_op jit(solution)/shard_map/while/body/eval_jaxpr/ppermute | solution.py:36
  262.3 8.7 %collective-permute-start = (f32[4,4,8,128]{3,2,1,0:T(8,128)S(1)}, f32[4,4,8,128]{3,2,1,0:T(8,128)S(1)}, u32[]{:S(2)}, u32[]{:S(2)}) collective-permute-start(f32[4,4,8,128]{3,2,1,0:T(8,128)S(1)} %add_select_fusion.3), channel_id=1, source_target_pairs={{0,8},{8,16},{16,24},{24,32},{32,40},{40,48},{48,56},{56,64},{64,7... | collective-permute-start | bytes 196616 | tf_op jit(solution)/shard_map/while/body/eval_jaxpr/ppermute | solution.py:36
  271.0 9.4 %collective-permute-start = (f32[4,4,8,128]{3,2,1,0:T(8,128)S(1)}, f32[4,4,8,128]{3,2,1,0:T(8,128)S(1)}, u32[]{:S(2)}, u32[]{:S(2)}) collective-permute-start(f32[4,4,8,128]{3,2,1,0:T(8,128)S(1)} %add_select_fusion.3), channel_id=1, source_target_pairs={{0,8},{8,16},{16,24},{24,32},{32,40},{40,48},{48,56},{56,64},{64,7... | collective-permute-start | bytes 196616 | tf_op jit(solution)/shard_map/while/body/eval_jaxpr/ppermute | solution.py:36
  280.5 9.3 %collective-permute-start = (f32[4,4,8,128]{3,2,1,0:T(8,128)S(1)}, f32[4,4,8,128]{3,2,1,0:T(8,128)S(1)}, u32[]{:S(2)}, u32[]{:S(2)}) collective-permute-start(f32[4,4,8,128]{3,2,1,0:T(8,128)S(1)} %add_select_fusion.3), channel_id=1, source_target_pairs={{0,8},{8,16},{16,24},{24,32},{32,40},{40,48},{48,56},{56,64},{64,7... | collective-permute-start | bytes 196616 | tf_op jit(solution)/shard_map/while/body/eval_jaxpr/ppermute | solution.py:36
  289.9 8.7 %collective-permute-start = (f32[4,4,8,128]{3,2,1,0:T(8,128)S(1)}, f32[4,4,8,128]{3,2,1,0:T(8,128)S(1)}, u32[]{:S(2)}, u32[]{:S(2)}) collective-permute-start(f32[4,4,8,128]{3,2,1,0:T(8,128)S(1)} %add_select_fusion.3), channel_id=1, source_target_pairs={{0,8},{8,16},{16,24},{24,32},{32,40},{40,48},{48,56},{56,64},{64,7... | collective-permute-start | bytes 196616 | tf_op jit(solution)/shard_map/while/body/eval_jaxpr/ppermute | solution.py:36
  298.7 9.3 %collective-permute-start = (f32[4,4,8,128]{3,2,1,0:T(8,128)S(1)}, f32[4,4,8,128]{3,2,1,0:T(8,128)S(1)}, u32[]{:S(2)}, u32[]{:S(2)}) collective-permute-start(f32[4,4,8,128]{3,2,1,0:T(8,128)S(1)} %add_select_fusion.3), channel_id=1, source_target_pairs={{0,8},{8,16},{16,24},{24,32},{32,40},{40,48},{48,56},{56,64},{64,7... | collective-permute-start | bytes 196616 | tf_op jit(solution)/shard_map/while/body/eval_jaxpr/ppermute | solution.py:36
  308.0 9.3 %collective-permute-start = (f32[4,4,8,128]{3,2,1,0:T(8,128)S(1)}, f32[4,4,8,128]{3,2,1,0:T(8,128)S(1)}, u32[]{:S(2)}, u32[]{:S(2)}) collective-permute-start(f32[4,4,8,128]{3,2,1,0:T(8,128)S(1)} %add_select_fusion.3), channel_id=1, source_target_pairs={{0,8},{8,16},{16,24},{24,32},{32,40},{40,48},{48,56},{56,64},{64,7... | collective-permute-start | bytes 196616 | tf_op jit(solution)/shard_map/while/body/eval_jaxpr/ppermute | solution.py:36
  317.4 8.7 %collective-permute-start = (f32[4,4,8,128]{3,2,1,0:T(8,128)S(1)}, f32[4,4,8,128]{3,2,1,0:T(8,128)S(1)}, u32[]{:S(2)}, u32[]{:S(2)}) collective-permute-start(f32[4,4,8,128]{3,2,1,0:T(8,128)S(1)} %add_select_fusion.3), channel_id=1, source_target_pairs={{0,8},{8,16},{16,24},{24,32},{32,40},{40,48},{48,56},{56,64},{64,7... | collective-permute-start | bytes 196616 | tf_op jit(solution)/shard_map/while/body/eval_jaxpr/ppermute | solution.py:36
  326.2 8.6 %collective-permute-start = (f32[4,4,8,128]{3,2,1,0:T(8,128)S(1)}, f32[4,4,8,128]{3,2,1,0:T(8,128)S(1)}, u32[]{:S(2)}, u32[]{:S(2)}) collective-permute-start(f32[4,4,8,128]{3,2,1,0:T(8,128)S(1)} %add_select_fusion.3), channel_id=1, source_target_pairs={{0,8},{8,16},{16,24},{24,32},{32,40},{40,48},{48,56},{56,64},{64,7... | collective-permute-start | bytes 196616 | tf_op jit(solution)/shard_map/while/body/eval_jaxpr/ppermute | solution.py:36
  334.8 8.6 %collective-permute-start = (f32[4,4,8,128]{3,2,1,0:T(8,128)S(1)}, f32[4,4,8,128]{3,2,1,0:T(8,128)S(1)}, u32[]{:S(2)}, u32[]{:S(2)}) collective-permute-start(f32[4,4,8,128]{3,2,1,0:T(8,128)S(1)} %add_select_fusion.3), channel_id=1, source_target_pairs={{0,8},{8,16},{16,24},{24,32},{32,40},{40,48},{48,56},{56,64},{64,7... | collective-permute-start | bytes 196616 | tf_op jit(solution)/shard_map/while/body/eval_jaxpr/ppermute | solution.py:36
  343.5 8.6 %collective-permute-start = (f32[4,4,8,128]{3,2,1,0:T(8,128)S(1)}, f32[4,4,8,128]{3,2,1,0:T(8,128)S(1)}, u32[]{:S(2)}, u32[]{:S(2)}) collective-permute-start(f32[4,4,8,128]{3,2,1,0:T(8,128)S(1)} %add_select_fusion.3), channel_id=1, source_target_pairs={{0,8},{8,16},{16,24},{24,32},{32,40},{40,48},{48,56},{56,64},{64,7... | collective-permute-start | bytes 196616 | tf_op jit(solution)/shard_map/while/body/eval_jaxpr/ppermute | solution.py:36
  352.2 8.6 %collective-permute-start = (f32[4,4,8,128]{3,2,1,0:T(8,128)S(1)}, f32[4,4,8,128]{3,2,1,0:T(8,128)S(1)}, u32[]{:S(2)}, u32[]{:S(2)}) collective-permute-start(f32[4,4,8,128]{3,2,1,0:T(8,128)S(1)} %add_select_fusion.3), channel_id=1, source_target_pairs={{0,8},{8,16},{16,24},{24,32},{32,40},{40,48},{48,56},{56,64},{64,7... | collective-permute-start | bytes 196616 | tf_op jit(solution)/shard_map/while/body/eval_jaxpr/ppermute | solution.py:36
  360.9 8.6 %collective-permute-start = (f32[4,4,8,128]{3,2,1,0:T(8,128)S(1)}, f32[4,4,8,128]{3,2,1,0:T(8,128)S(1)}, u32[]{:S(2)}, u32[]{:S(2)}) collective-permute-start(f32[4,4,8,128]{3,2,1,0:T(8,128)S(1)} %add_select_fusion.3), channel_id=1, source_target_pairs={{0,8},{8,16},{16,24},{24,32},{32,40},{40,48},{48,56},{56,64},{64,7... | collective-permute-start | bytes 196616 | tf_op jit(solution)/shard_map/while/body/eval_jaxpr/ppermute | solution.py:36
  369.5 8.6 %collective-permute-start = (f32[4,4,8,128]{3,2,1,0:T(8,128)S(1)}, f32[4,4,8,128]{3,2,1,0:T(8,128)S(1)}, u32[]{:S(2)}, u32[]{:S(2)}) collective-permute-start(f32[4,4,8,128]{3,2,1,0:T(8,128)S(1)} %add_select_fusion.3), channel_id=1, source_target_pairs={{0,8},{8,16},{16,24},{24,32},{32,40},{40,48},{48,56},{56,64},{64,7... | collective-permute-start | bytes 196616 | tf_op jit(solution)/shard_map/while/body/eval_jaxpr/ppermute | solution.py:36
  378.2 8.6 %collective-permute-start = (f32[4,4,8,128]{3,2,1,0:T(8,128)S(1)}, f32[4,4,8,128]{3,2,1,0:T(8,128)S(1)}, u32[]{:S(2)}, u32[]{:S(2)}) collective-permute-start(f32[4,4,8,128]{3,2,1,0:T(8,128)S(1)} %add_select_fusion.3), channel_id=1, source_target_pairs={{0,8},{8,16},{16,24},{24,32},{32,40},{40,48},{48,56},{56,64},{64,7... | collective-permute-start | bytes 196616 | tf_op jit(solution)/shard_map/while/body/eval_jaxpr/ppermute | solution.py:36
  386.9 8.6 %collective-permute-start = (f32[4,4,8,128]{3,2,1,0:T(8,128)S(1)}, f32[4,4,8,128]{3,2,1,0:T(8,128)S(1)}, u32[]{:S(2)}, u32[]{:S(2)}) collective-permute-start(f32[4,4,8,128]{3,2,1,0:T(8,128)S(1)} %add_select_fusion.3), channel_id=1, source_target_pairs={{0,8},{8,16},{16,24},{24,32},{32,40},{40,48},{48,56},{56,64},{64,7... | collective-permute-start | bytes 196616 | tf_op jit(solution)/shard_map/while/body/eval_jaxpr/ppermute | solution.py:36
  395.5 8.6 %collective-permute-start = (f32[4,4,8,128]{3,2,1,0:T(8,128)S(1)}, f32[4,4,8,128]{3,2,1,0:T(8,128)S(1)}, u32[]{:S(2)}, u32[]{:S(2)}) collective-permute-start(f32[4,4,8,128]{3,2,1,0:T(8,128)S(1)} %add_select_fusion.3), channel_id=1, source_target_pairs={{0,8},{8,16},{16,24},{24,32},{32,40},{40,48},{48,56},{56,64},{64,7... | collective-permute-start | bytes 196616 | tf_op jit(solution)/shard_map/while/body/eval_jaxpr/ppermute | solution.py:36
  404.2 8.6 %collective-permute-start = (f32[4,4,8,128]{3,2,1,0:T(8,128)S(1)}, f32[4,4,8,128]{3,2,1,0:T(8,128)S(1)}, u32[]{:S(2)}, u32[]{:S(2)}) collective-permute-start(f32[4,4,8,128]{3,2,1,0:T(8,128)S(1)} %add_select_fusion.3), channel_id=1, source_target_pairs={{0,8},{8,16},{16,24},{24,32},{32,40},{40,48},{48,56},{56,64},{64,7... | collective-permute-start | bytes 196616 | tf_op jit(solution)/shard_map/while/body/eval_jaxpr/ppermute | solution.py:36
  412.9 8.6 %collective-permute-start = (f32[4,4,8,128]{3,2,1,0:T(8,128)S(1)}, f32[4,4,8,128]{3,2,1,0:T(8,128)S(1)}, u32[]{:S(2)}, u32[]{:S(2)}) collective-permute-start(f32[4,4,8,128]{3,2,1,0:T(8,128)S(1)} %add_select_fusion.3), channel_id=1, source_target_pairs={{0,8},{8,16},{16,24},{24,32},{32,40},{40,48},{48,56},{56,64},{64,7... | collective-permute-start | bytes 196616 | tf_op jit(solution)/shard_map/while/body/eval_jaxpr/ppermute | solution.py:36
  421.6 8.6 %collective-permute-start = (f32[4,4,8,128]{3,2,1,0:T(8,128)S(1)}, f32[4,4,8,128]{3,2,1,0:T(8,128)S(1)}, u32[]{:S(2)}, u32[]{:S(2)}) collective-permute-start(f32[4,4,8,128]{3,2,1,0:T(8,128)S(1)} %add_select_fusion.3), channel_id=1, source_target_pairs={{0,8},{8,16},{16,24},{24,32},{32,40},{40,48},{48,56},{56,64},{64,7... | collective-permute-start | bytes 196616 | tf_op jit(solution)/shard_map/while/body/eval_jaxpr/ppermute | solution.py:36
  430.2 8.6 %collective-permute-start = (f32[4,4,8,128]{3,2,1,0:T(8,128)S(1)}, f32[4,4,8,128]{3,2,1,0:T(8,128)S(1)}, u32[]{:S(2)}, u32[]{:S(2)}) collective-permute-start(f32[4,4,8,128]{3,2,1,0:T(8,128)S(1)} %add_select_fusion.3), channel_id=1, source_target_pairs={{0,8},{8,16},{16,24},{24,32},{32,40},{40,48},{48,56},{56,64},{64,7... | collective-permute-start | bytes 196616 | tf_op jit(solution)/shard_map/while/body/eval_jaxpr/ppermute | solution.py:36
  438.9 8.6 %collective-permute-start = (f32[4,4,8,128]{3,2,1,0:T(8,128)S(1)}, f32[4,4,8,128]{3,2,1,0:T(8,128)S(1)}, u32[]{:S(2)}, u32[]{:S(2)}) collective-permute-start(f32[4,4,8,128]{3,2,1,0:T(8,128)S(1)} %add_select_fusion.3), channel_id=1, source_target_pairs={{0,8},{8,16},{16,24},{24,32},{32,40},{40,48},{48,56},{56,64},{64,7... | collective-permute-start | bytes 196616 | tf_op jit(solution)/shard_map/while/body/eval_jaxpr/ppermute | solution.py:36
  447.6 8.6 %collective-permute-start = (f32[4,4,8,128]{3,2,1,0:T(8,128)S(1)}, f32[4,4,8,128]{3,2,1,0:T(8,128)S(1)}, u32[]{:S(2)}, u32[]{:S(2)}) collective-permute-start(f32[4,4,8,128]{3,2,1,0:T(8,128)S(1)} %add_select_fusion.3), channel_id=1, source_target_pairs={{0,8},{8,16},{16,24},{24,32},{32,40},{40,48},{48,56},{56,64},{64,7... | collective-permute-start | bytes 196616 | tf_op jit(solution)/shard_map/while/body/eval_jaxpr/ppermute | solution.py:36
  473.6 8.6 %collective-permute-start = (f32[4,4,8,128]{3,2,1,0:T(8,128)S(1)}, f32[4,4,8,128]{3,2,1,0:T(8,128)S(1)}, u32[]{:S(2)}, u32[]{:S(2)}) collective-permute-start(f32[4,4,8,128]{3,2,1,0:T(8,128)S(1)} %add_select_fusion.3), channel_id=1, source_target_pairs={{0,8},{8,16},{16,24},{24,32},{32,40},{40,48},{48,56},{56,64},{64,7... | collective-permute-start | bytes 196616 | tf_op jit(solution)/shard_map/while/body/eval_jaxpr/ppermute | solution.py:36
  490.9 8.6 %collective-permute-start = (f32[4,4,8,128]{3,2,1,0:T(8,128)S(1)}, f32[4,4,8,128]{3,2,1,0:T(8,128)S(1)}, u32[]{:S(2)}, u32[]{:S(2)}) collective-permute-start(f32[4,4,8,128]{3,2,1,0:T(8,128)S(1)} %add_select_fusion.3), channel_id=1, source_target_pairs={{0,8},{8,16},{16,24},{24,32},{32,40},{40,48},{48,56},{56,64},{64,7... | collective-permute-start | bytes 196616 | tf_op jit(solution)/shard_map/while/body/eval_jaxpr/ppermute | solution.py:36
  (81 other events, 884.6 us)
where the time goes:
time: 527 us; the launch traced here: 518 us
  waiting for transfers between devices  243 us (46%)
  starting transfers between devices  138 us (26%)
  matrix products  72 us (14%)
  other arithmetic  54.4 us (10%)
  local copies, waits for them, and re-layouts  8.45 us (2%)
    ppermute x31, waiting for transfers between devices, passed_along(): lax.ppermute(value, axis, [(source, source + steps) for source in range(f...  211 us
    ppermute x31, starting transfers between devices, passed_along(): lax.ppermute(value, axis, [(source, source + steps) for source in range(f...  59.5 us
    ppermute x12, starting transfers between devices, with_halo(): lax.ppermute(tail, axis, [(i, (i + 1) % count) for i in range(ends)])  52.9 us
    dot_general x12, matrix products, advance(): jnp.dot(message, out_w, preferred_element_type=jnp.float32)  43.7 us
    ppermute x12, waiting for transfers between devices, with_halo(): lax.ppermute(head, axis, [((i + 1) % count, i) for i in range(ends)])  31.1 us
    dot_general x12, matrix products, advance(): preact = jnp.dot(centre, self_w, preferred_element_type=jnp.float32)  25.5 us
    ppermute x12, starting transfers between devices, with_halo(): lax.ppermute(head, axis, [((i + 1) % count, i) for i in range(ends)])  25 us
    reduce_sum x14, other arithmetic, normed(): row_var = jnp.mean(jnp.square(widened - row_mean), axis=-1, keepdims=True)  18.2 us
  transfers between devices with their start and end apart: 55, of which 43 were waited for; matrix products, arithmetic and copies ran while one was open for 5% of the time, Pallas kernels for 0%

commit v1 on v0

v1 whole, which is shorter than its diff:
```python
import functools

import jax
import jax.numpy as jnp
import numpy as np
from jax import lax
from jax.experimental import pallas as pl
from jax.experimental.pallas import tpu as pltpu
from jax.sharding import PartitionSpec as P

HID = 128
CHAN = 4
NZ = 4
TYPES = 3
RATES = 8
LAYERS = 6
STEPS = 2
NY = 128

EPS = 1e-05

GROUPS, GROUP = 8, 16
PADDED = (GROUPS + 2) * GROUP
BLOCK = 8
FRAME = 3 * BLOCK
FEATURES = 3 * CHAN + 2 * TYPES

F32, BF16 = jnp.float32, jnp.bfloat16

_row = np.arange(NY)
TO_GROUPS = np.zeros((NY, NY), np.float32)
TO_GROUPS[_row, (_row % GROUP) * GROUPS + _row // GROUP] = 1.0


def dot(a, b, **kw):
    return jnp.dot(a, b, preferred_element_type=F32, **kw)


def dot_nt(a, b):
    return lax.dot_general(a, b, (((1,), (1,)), ((), ())), preferred_element_type=F32)


def halves(value):
    high = value.astype(BF16)
    return high, (value - high.astype(F32)).astype(BF16)


def fine_step(
    where_ref, own_ref, first_ref, second_ref, kind_ref, kind_first_ref, kind_second_ref,
    enc_ref, in_ref, out_ref, bias_ref, gain_ref, dec_ref, order_ref, back_ref,
    state_ref, send_ref,
    hidden_ref, norm_ref, message_ref,
):
    position = where_ref[0]
    last = where_ref[1]
    odd = position % 2 == 1
    at_left = position == 0
    at_right = position == last

    def store_normalized(layer, x, z, hidden):
        slot = layer % 2
        square = jnp.sum(hidden * hidden, axis=-1, keepdims=True) * (1.0 / HID)
        normal = hidden * lax.rsqrt(square + EPS) * gain_ref[layer]
        norm_ref[slot, x, z, GROUP : GROUP + NY, :] = normal.astype(BF16)
        line = lax.broadcasted_iota(jnp.int32, (GROUP, HID), 0)
        before = pltpu.roll(normal[NY - GROUP :], 1, 0)
        before = jnp.where(line == 0, 0.0, before)
        norm_ref[slot, x, z, :GROUP, :] = before.astype(BF16)
        after = pltpu.roll(normal[:GROUP], GROUP - 1, 0)
        after = jnp.where(line == GROUP - 1, 0.0, after)
        norm_ref[slot, x, z, GROUP + NY :, :] = after.astype(BF16)

    @pl.when(at_left)
    def _():
        norm_ref[:, BLOCK - 1] = jnp.zeros((2, NZ, PADDED, HID), BF16)

    @pl.when(at_right)
    def _():
        norm_ref[:, 2 * BLOCK] = jnp.zeros((2, NZ, PADDED, HID), BF16)

    def encode(block, states, kinds, z):
        rows = []
        highs = [state.astype(BF16).astype(F32) for state in states]
        rows.extend(highs)
        rows.extend(state - high for state, high in zip(states, highs))
        rows.extend(highs)
        marks = [(kinds == kind).astype(F32) for kind in range(TYPES)]
        rows.extend(marks)
        rows.extend(marks)
        table = jnp.concatenate(rows, axis=0).astype(BF16)
        turned = dot_nt(order_ref[...], table).astype(BF16)
        for x in range(BLOCK):
            hidden = dot(turned, enc_ref[:, x * HID : (x + 1) * HID])
            hidden_ref[block * BLOCK + x, z] = hidden
            store_normalized(0, block * BLOCK + x, z, hidden)

    for z in range(NZ):
        encode(
            1,
            [own_ref[c, z] for c in range(CHAN)],
            kind_ref[z],
            z,
        )

    def neighbour(block, take_first):
        for z in range(NZ):
            states = []
            for c in range(CHAN):
                at = pl.ds((c * NZ + z) * BLOCK, BLOCK)
                states.append(jnp.where(take_first, first_ref[at, :], second_ref[at, :]))
            at = pl.ds(z * BLOCK, BLOCK)
            kinds = jnp.where(take_first, kind_first_ref[at, :], kind_second_ref[at, :])
            encode(block, states, kinds, z)

    @pl.when(jnp.logical_not(at_left))
    def _():
        neighbour(0, odd)

    @pl.when(jnp.logical_not(at_right))
    def _():
        neighbour(2, jnp.logical_not(odd))

    def rows_of(layer):
        reach = LAYERS - 1 - layer
        low = jnp.where(at_left, BLOCK, BLOCK - reach)
        high = jnp.where(at_right, 2 * BLOCK, 2 * BLOCK + reach)
        extra = (high - low) % 2
        low = jnp.where(at_left, low, low - extra)
        high = jnp.where(at_left, high + extra, high)
        return low, high

    def messages(layer, x):
        slot = layer % 2
        centre = slice(GROUP, GROUP + NY)
        rows = []
        for d in range(2):
            for z in range(NZ):
                mid = norm_ref[slot, x + d, z, centre, :]
                total = norm_ref[slot, x + d - 1, z, centre, :] + norm_ref[slot, x + d + 1, z, centre, :]
                total = total + (
                    norm_ref[slot, x + d, z, :NY, :] + norm_ref[slot, x + d, z, 2 * GROUP :, :]
                )
                beside = [norm_ref[slot, x + d, w, centre, :] for w in (z - 1, z + 1) if 0 <= w < NZ]
                total = total + functools.reduce(lambda a, b: a + b, beside)
                rows.append(jnp.concatenate([mid, total], axis=-1))
        bias = bias_ref[layer]
        found = []
        for pair in rows:
            half = dot(pair, in_ref[layer]) + bias
            found.append((half * jnp.tanh(half) + half).astype(BF16))
        return found

    def keep(found):
        for at, message in enumerate(found):
            message_ref[at] = message

    def update(layer, x, held):
        for z in range(NZ):
            for d in range(2):
                message = held[d * NZ + z]
                moved = dot(jnp.concatenate([message, message], axis=-1), out_ref[layer])
                hidden = hidden_ref[x + d, z] + moved
                hidden_ref[x + d, z] = hidden
                store_normalized(layer + 1, x + d, z, hidden)

    def count(layer):
        low, high = rows_of(layer)
        return (high - low) // 2

    total = sum(count(layer) for layer in range(LAYERS))

    def advance(_, place):
        layer, x = place
        high = rows_of(layer)[1]
        ends = x + 2 >= high
        next_layer = jnp.where(ends, layer + 1, layer)
        next_x = jnp.where(ends, rows_of(layer + 1)[0], x + 2)
        held = [message_ref[at] for at in range(2 * NZ)]
        found = messages(next_layer, next_x)
        update(layer, x, held)
        keep(found)
        return next_layer, next_x

    start = (jnp.int32(0), rows_of(0)[0])
    keep(messages(*start))
    layer, x = lax.fori_loop(0, total - 1, advance, start)
    update(layer, x, [message_ref[at] for at in range(2 * NZ)])

    found = []
    for z in range(NZ):
        both = jnp.zeros((CHAN * BLOCK, NY), F32)
        for x in range(0, BLOCK, 2):
            pair = jnp.concatenate(
                [norm_ref[0, BLOCK + x + d, z, GROUP : GROUP + NY, :] for d in range(2)], axis=-1
            )
            both = both + dot_nt(dec_ref[x // 2], pair)
        found.append(both)
    change = dot(jnp.concatenate(found, axis=0), back_ref[...], precision=lax.Precision.HIGHEST)
    for c in range(CHAN):
        for z in range(NZ):
            at = (z * CHAN + c) * BLOCK
            state_ref[c, z] = own_ref[c, z] + change[at : at + BLOCK]
    send_ref[...] = state_ref[...].reshape(CHAN * NZ * BLOCK, NY).astype(BF16)


def run_fine_step(*args):
    vmem = pl.BlockSpec(memory_space=pltpu.VMEM)
    return pl.pallas_call(
        fine_step,
        out_shape=(
            jax.ShapeDtypeStruct((CHAN, NZ, BLOCK, NY), F32),
            jax.ShapeDtypeStruct((CHAN * NZ * BLOCK, NY), BF16),
        ),
        in_specs=[pl.BlockSpec(memory_space=pltpu.SMEM)] + [vmem] * 14,
        out_specs=(vmem, vmem),
        scratch_shapes=[
            pltpu.VMEM((FRAME, NZ, NY, HID), F32),
            pltpu.VMEM((2, FRAME, NZ, PADDED, HID), BF16),
            pltpu.VMEM((2 * NZ, NY, HID), BF16),
        ],
        compiler_params=pltpu.CompilerParams(vmem_limit_bytes=40 * 2**20),
        cost_estimate=pl.CostEstimate(flops=10**10, bytes_accessed=2**21, transcendentals=10**7),
        name="fine_step",
    )(*args)


def lookup_rate(sched_row, step_index, rate_values):
    picks = jnp.arange(RATES, dtype=jnp.int32) == sched_row[step_index]
    return jnp.sum(jnp.where(picks, rate_values, 0.0))


def centred(rows):
    return rows - jnp.mean(rows, axis=-1, keepdims=True)


def encoder(rate_value, enc_weight, type_table, force_vector):
    well = jnp.array([0.0, 1.0, -1.0], F32)[:, None] * rate_value * force_vector
    high, low = halves(centred(enc_weight))
    kind_high, kind_low = halves(centred(type_table + well))
    table = jnp.concatenate([high, high, low, kind_high, kind_low], axis=0)
    eye = jnp.eye(BLOCK, dtype=BF16)
    wide = table[:, None, None, :] * eye[None, :, :, None]
    return wide.reshape(FEATURES * BLOCK, BLOCK * HID)


def decoder(dec_weight):
    eye = jnp.eye(BLOCK, dtype=BF16)
    wide = dec_weight[:, None, None, :] * eye[None, :, :, None]
    wide = wide.reshape(CHAN * BLOCK, BLOCK // 2, 2 * HID)
    return wide.transpose(1, 0, 2)


def layer_weights(norm_gain, self_weight, neigh_weight, out_weight, layer_bias, dec_gain):
    enter = jnp.concatenate([self_weight, neigh_weight], axis=1) * jnp.asarray(0.5, BF16)
    leave = jnp.concatenate(halves(centred(out_weight.astype(F32))), axis=1)
    gains = jnp.concatenate([norm_gain, dec_gain[None]], axis=0)
    return enter, leave, (layer_bias * 0.5)[:, None, :], gains[:, None, :]


def exchange(value):
    count = lax.axis_size("space")
    first = [(i, i ^ 1) for i in range(count)]
    second = [(i, i + 1) for i in range(1, count - 1, 2)] + [(i + 1, i) for i in range(1, count - 1, 2)]
    return lax.ppermute(value, "space", first), lax.ppermute(value, "space", second)


def matvec(matrix, vector):
    return jnp.sum(matrix * vector[None], axis=1)


def matmat(left, right):
    return jnp.sum(left[:, :, None] * right[None], axis=1)


def per_device(
    prev_starts, plan, cell_type, coarse_matrix, rate_values, enc_weight, type_table, force_vector,
    norm_gain, self_weight, neigh_weight, out_weight, layer_bias, dec_gain, dec_weight,
):
    own = prev_starts[0]
    sched_row = plan[0]
    position = lax.axis_index("space")
    where = jnp.stack([position, lax.axis_size("space") - 1]).astype(jnp.int32)
    rows = CHAN * NZ * BLOCK

    outgoing = jnp.concatenate(
        [own.reshape(rows, NY).astype(BF16), cell_type.reshape(NZ * BLOCK, NY).astype(BF16)], axis=0
    )
    first, second = exchange(outgoing)
    kinds = [cell_type] + [side[rows:].astype(jnp.int32) for side in (first, second)]
    sides = [side[:rows].astype(F32) for side in (first, second)]

    enter, leave, bias, gains = layer_weights(
        norm_gain, self_weight, neigh_weight, out_weight, layer_bias, dec_gain
    )
    dec = decoder(dec_weight)
    order = jnp.asarray(TO_GROUPS, BF16)
    back = jnp.asarray(TO_GROUPS, F32)

    state = own
    for step_index in range(STEPS):
        rate_value = lookup_rate(sched_row, step_index, rate_values)
        enc = encoder(rate_value, enc_weight, type_table, force_vector)
        state, outgoing = run_fine_step(
            where, state, *sides, *kinds, enc, enter, leave, bias, gains, dec, order, back
        )
        if step_index + 1 < STEPS:
            sides = [side.astype(F32) for side in exchange(outgoing)]

    window = lax.axis_index("tm")
    total = jnp.where(window == 0, state, state - matvec(coarse_matrix, own))
    corrected = total
    power, reach = coarse_matrix, coarse_matrix
    count = lax.axis_size("tm")
    distance = 1
    while distance < count:
        came = lax.ppermute(total, "tm", [(i, i ^ distance) for i in range(count)])
        upper = (window // distance) % 2 == 1
        corrected = corrected + jnp.where(upper, matvec(reach, came), 0.0)
        if 2 * distance < count:
            lower_total = jnp.where(upper, came, total)
            upper_total = jnp.where(upper, total, came)
            total = upper_total + matvec(power, lower_total)
            reach = jnp.where(upper, matmat(power, reach), reach)
            power = matmat(power, power)
        distance *= 2
    return corrected[None]


def solution(mesh):
    return jax.shard_map(
        per_device,
        mesh=mesh,
        in_specs=(
            P("tm", None, None, "space", None),
            P("tm", None),
            P(None, "space", None),
            P(None, None, None, "space", None),
        )
        + (P(),) * 11,
        out_specs=P("tm", None, None, "space", None),
        check_vma=False,
    )
```

time: 527 us -> 111 us (0.21)
  the two profiles are of different devices: /device:TPU:20 before, /device:TPU:56 now
where the time goes in v1:
time: 111 us; the launch traced here: 110 us
  Pallas kernels  54.5 us (49%)
  starting transfers between devices  22.5 us (20%)
  waiting for transfers between devices  18 us (16%)
  other arithmetic  7.66 us (7%)
  local copies, waits for them, and re-layouts  7.22 us (7%)
    pallas_call x2, Pallas kernels, run_fine_step(): pl.pallas_call(fine_step, out_shape=(jax.ShapeDtypeStruct((CHAN, NZ, BLOC...  54.5 us
    ppermute x5, waiting for transfers between devices, per_device(): came = lax.ppermute(total, 'tm', [(i, i ^ distance) for i in range(count)])  13.9 us
    ppermute x5, starting transfers between devices, per_device(): came = lax.ppermute(total, 'tm', [(i, i ^ distance) for i in range(count)])  12.4 us
    ppermute x2, starting transfers between devices, exchange(): lax.ppermute(value, 'space', second)  7.94 us
    unnamed x34, local copies, waits for them, and re-layouts  5.48 us
    ppermute x2, waiting for transfers between devices, exchange(): lax.ppermute(value, 'space', second)  4.09 us
  transfers between devices with their start and end apart: 9, of which 6 were waited for; matrix products, arithmetic and copies ran while one was open for 7% of the time, Pallas kernels for 0%

profile of v1, /device:TPU:56, one launch (start us, length us, event | category | flops | bytes accessed | tf_op | source)
XLA Modules:
  0.0 110.5 jit_solution(13494329697384470312)
XLA Ops:
  0.0 0.9 convert_element_type.85
  0.9 4.2 %collective-permute-start.1 = (bf16[160,128]{1,0:T(8,128)(2,1)S(1)}, bf16[160,128]{1,0:T(8,128)(2,1)S(1)}, u32[]{:S(2)}, u32[]{:S(2)}) collective-permute-start(bf16[160,128]{1,0:T(8,128)(2,1)S(1)} %pad_maximum_fusion.1), channel_id=1, source_target_pairs={{1,2},{3,4},{5,6},{2,1},{4,3},{6,5},{9,10},{11,12},{13,14},{10,9},... | collective-permute-start | bytes 122888 | tf_op jit(solution)/shard_map/ppermute | solution.py:264
  5.1 0.8 collective-permute-start
  5.9 1.3 %fusion.8 = (s32[1,1]{1,0:T(1,128)}, s32[1,1]{1,0:T(1,128)}) fusion(s32[1,2]{1,0:T(1,128)} %param.20), kind=kLoop, calls=%fused_computation.71 | loop fusion | bytes 16 | tf_op jit(solution)/shard_map/slice | solution.py:228
  7.2 0.9 reduce_sum.206
  8.4 0.2 fusion.1
  8.6 0.5 copy-done.13
  9.2 0.6 copy-done.10
  9.8 0.7 copy-done.14
  10.5 1.9 %fusion.7 = (f32[]{:T(128)}, f32[]{:T(128)}) fusion(f32[8]{0:T(128)S(1)} %copy-done.14, s32[]{:T(128)} %bitcast.8, s32[]{:T(128)} %bitcast.4), kind=kLoop, calls=%fused_computation.64 | loop fusion | flops 46 | bytes 48 | tf_op jit(solution)/shard_map/reduce_sum | solution.py:229
  12.4 0.7 copy-done.16
  13.0 1.3 %broadcast_multiply_fusion.6 = (f32[3]{0:T(128)S(1)}, f32[3]{0:T(128)S(1)}) fusion(f32[3]{0:T(128)S(1)} %copy-done.16, f32[]{:T(128)} %get-tuple-element.22, f32[]{:T(128)} %get-tuple-element.21), kind=kLoop, calls=%fused_computation.69 | loop fusion | flops 6 | bytes 44 | tf_op jit(solution)/shard_map/mul | solution.py:237
  14.3 0.7 copy-done.8
  15.0 0.2 fusion.5
  15.6 0.5 copy-done.11
  16.4 0.8 copy-done.6
  17.7 0.7 copy-done.3
  18.5 26.9 %fine_step.2 = (f32[4,4,8,128]{3,2,1,0:T(8,128)S(1)}, bf16[128,128]{1,0:T(8,128)(2,1)S(1)}) custom-call(s32[2]{0:T(128)S(1)} %pad_add_fusion.where_ref, f32[4,4,8,128]{3,2,1,0:T(8,128)S(1)} %bitcast.19, f32[128,128]{1,0:T(8,128)S(1)} %slice_convert_fusion.1.first_ref, f32[128,128]{1,0:T(8,128)S(1)} %slice_convert_fusion.second_ref, ...), custom_call_target="tpu_custom_call" | custom-call | flops 10000000000 | bytes 2097152 | tf_op jit(solution)/shard_map/fine_step/pallas_call | solution.py:208
  45.4 1.4 %collective-permute-start.2 = (bf16[128,128]{1,0:T(8,128)(2,1)S(1)}, bf16[128,128]{1,0:T(8,128)(2,1)S(1)}, u32[]{:S(2)}, u32[]{:S(2)}) collective-permute-start(bf16[128,128]{1,0:T(8,128)(2,1)S(1)} %get-tuple-element.9), channel_id=1, source_target_pairs={{0,1},{1,0},{2,3},{3,2},{4,5},{5,4},{6,7},{7,6},{8,9},{9,8},{10,11... | collective-permute-start | bytes 98312 | tf_op jit(solution)/shard_map/ppermute | solution.py:264
  46.8 3.7 %collective-permute-start.3 = (bf16[128,128]{1,0:T(8,128)(2,1)S(1)}, bf16[128,128]{1,0:T(8,128)(2,1)S(1)}, u32[]{:S(2)}, u32[]{:S(2)}) collective-permute-start(bf16[128,128]{1,0:T(8,128)(2,1)S(1)} %get-tuple-element.9), channel_id=1, source_target_pairs={{1,2},{3,4},{5,6},{2,1},{4,3},{6,5},{9,10},{11,12},{13,14},{10,9},... | collective-permute-start | bytes 98312 | tf_op jit(solution)/shard_map/ppermute | solution.py:264
  50.6 4.1 %collective-permute-done.3 = bf16[128,128]{1,0:T(8,128)(2,1)S(1)} collective-permute-done((bf16[128,128]{1,0:T(8,128)(2,1)S(1)}, bf16[128,128]{1,0:T(8,128)(2,1)S(1)}, u32[]{:S(2)}, u32[]{:S(2)}) %collective-permute-start.3) | collective-permute-done | bytes 32800 | tf_op jit(solution)/shard_map/ppermute | solution.py:264
  54.7 27.7 %fine_step.3 = (f32[4,4,8,128]{3,2,1,0:T(8,128)S(1)}, bf16[128,128]{1,0:T(8,128)(2,1)}) custom-call(s32[2]{0:T(128)S(1)} %pad_add_fusion.where_ref, f32[4,4,8,128]{3,2,1,0:T(8,128)S(1)} %get-tuple-element.8.own_ref, f32[128,128]{1,0:T(8,128)S(1)} %convert_element_type.104.first_ref, f32[128,128]{1,0:T(8,128)S(1)} %convert_element_type.105.second_ref, ...), custom_call_target="tpu_custom_call" | custom-call | flops 10000000000 | bytes 2097152 | tf_op jit(solution)/shard_map/fine_step/pallas_call | solution.py:208
  82.5 1.2 %collective-permute-done.4 = f32[4,4,8,128]{3,2,1,0:T(8,128)S(1)} collective-permute-done((f32[4,4,8,128]{3,2,1,0:T(8,128)S(1)}, f32[4,4,8,128]{3,2,1,0:T(8,128)S(1)}, u32[]{:S(2)}, u32[]{:S(2)}) %collective-permute-start.4) | collective-permute-done | bytes 65568 | tf_op jit(solution)/shard_map/ppermute | solution.py:316
  83.8 3.6 %collective-permute-start.5 = (f32[4,4,8,128]{3,2,1,0:T(8,128)S(1)}, f32[4,4,8,128]{3,2,1,0:T(8,128)S(1)}, u32[]{:S(2)}, u32[]{:S(2)}) collective-permute-start(f32[4,4,8,128]{3,2,1,0:T(8,128)S(1)} %select_add_fusion.3), channel_id=1, source_target_pairs={{0,16},{8,24},{16,0},{24,8},{32,48},{40,56},{48,32},{56,40},{64,80... | collective-permute-start | bytes 196616 | tf_op jit(solution)/shard_map/ppermute | solution.py:316
  87.6 2.2 %collective-permute-done.5 = f32[4,4,8,128]{3,2,1,0:T(8,128)S(1)} collective-permute-done((f32[4,4,8,128]{3,2,1,0:T(8,128)S(1)}, f32[4,4,8,128]{3,2,1,0:T(8,128)S(1)}, u32[]{:S(2)}, u32[]{:S(2)}) %collective-permute-start.5) | collective-permute-done | bytes 65568 | tf_op jit(solution)/shard_map/ppermute | solution.py:316
  90.0 6.5 %collective-permute-start.6 = (f32[4,4,8,128]{3,2,1,0:T(8,128)S(1)}, f32[4,4,8,128]{3,2,1,0:T(8,128)S(1)}, u32[]{:S(2)}, u32[]{:S(2)}) collective-permute-start(f32[4,4,8,128]{3,2,1,0:T(8,128)S(1)} %select_add_fusion.2), channel_id=1, source_target_pairs={{0,32},{8,40},{16,48},{24,56},{32,0},{40,8},{48,16},{56,24},{64,96... | collective-permute-start | bytes 196616 | tf_op jit(solution)/shard_map/ppermute | solution.py:316
  96.6 2.6 %collective-permute-done.6 = f32[4,4,8,128]{3,2,1,0:T(8,128)S(1)} collective-permute-done((f32[4,4,8,128]{3,2,1,0:T(8,128)S(1)}, f32[4,4,8,128]{3,2,1,0:T(8,128)S(1)}, u32[]{:S(2)}, u32[]{:S(2)}) %collective-permute-start.6) | collective-permute-done | bytes 65568 | tf_op jit(solution)/shard_map/ppermute | solution.py:316
  99.5 0.8 collective-permute-start.7
  100.3 3.5 %collective-permute-done.7 = f32[4,4,8,128]{3,2,1,0:T(8,128)S(1)} collective-permute-done((f32[4,4,8,128]{3,2,1,0:T(8,128)S(1)}, f32[4,4,8,128]{3,2,1,0:T(8,128)S(1)}, u32[]{:S(2)}, u32[]{:S(2)}) %collective-permute-start.7) | collective-permute-done | bytes 65568 | tf_op jit(solution)/shard_map/ppermute | solution.py:316
  103.9 1.3 %collective-permute-start.8 = (f32[4,4,8,128]{3,2,1,0:T(8,128)S(1)}, f32[4,4,8,128]{3,2,1,0:T(8,128)S(1)}, u32[]{:S(2)}, u32[]{:S(2)}) collective-permute-start(f32[4,4,8,128]{3,2,1,0:T(8,128)S(1)} %select_add_fusion), channel_id=1, source_target_pairs={{0,128},{8,136},{16,144},{24,152},{32,160},{40,168},{48,176},{56,1... | collective-permute-start | bytes 196616 | tf_op jit(solution)/shard_map/ppermute | solution.py:316
  105.3 4.4 %collective-permute-done.8 = f32[4,4,8,128]{3,2,1,0:T(8,128)S(1)} collective-permute-done((f32[4,4,8,128]{3,2,1,0:T(8,128)S(1)}, f32[4,4,8,128]{3,2,1,0:T(8,128)S(1)}, u32[]{:S(2)}, u32[]{:S(2)}) %collective-permute-start.8) | collective-permute-done | bytes 65568 | tf_op jit(solution)/shard_map/ppermute | solution.py:316
  109.8 0.7 add_bitcast_fusion
  (79 shorter events, 2.6 us)
Async XLA Ops:
  0.0 0.9 copy-start.1
  0.0 8.3 %copy-start.5 = (bf16[6,128,128]{2,1,0:T(8,128)(2,1)S(1)}, bf16[6,128,128]{2,1,0:T(8,128)(2,1)}, u32[]{:S(2)}) copy-start(bf16[6,128,128]{2,1,0:T(8,128)(2,1)} %param.30) | copy-start | bytes 589828
  0.9 16.6 %collective-permute-start.1 = (bf16[160,128]{1,0:T(8,128)(2,1)S(1)}, bf16[160,128]{1,0:T(8,128)(2,1)S(1)}, u32[]{:S(2)}, u32[]{:S(2)}) collective-permute-start(bf16[160,128]{1,0:T(8,128)(2,1)S(1)} %pad_maximum_fusion.1), channel_id=1, source_target_pairs={{1,2},{3,4},{5,6},{2,1},{4,3},{6,5},{9,10},{11,12},{13,14},{10,9},... | collective-permute-start | bytes 122888 | tf_op jit(solution)/shard_map/ppermute | solution.py:264
  5.1 12.5 %collective-permute-start = (bf16[160,128]{1,0:T(8,128)(2,1)S(1)}, bf16[160,128]{1,0:T(8,128)(2,1)S(1)}, u32[]{:S(2)}, u32[]{:S(2)}) collective-permute-start(bf16[160,128]{1,0:T(8,128)(2,1)S(1)} %pad_maximum_fusion.1), channel_id=1, source_target_pairs={{0,1},{1,0},{2,3},{3,2},{4,5},{5,4},{6,7},{7,6},{8,9},{9,8},{10,11... | collective-permute-start | bytes 122888 | tf_op jit(solution)/shard_map/ppermute | solution.py:264
  7.2 0.9 copy-start.9
  8.4 0.7 copy-start.13
  9.1 0.7 copy-start.10
  9.8 0.7 copy-start.14
  12.4 0.7 copy-start.16
  14.3 0.7 copy-start.8
  14.3 0.7 copy-start.12
  15.4 0.7 copy-start.11
  15.6 0.7 copy-start.15
  16.3 0.9 copy-start.6
  16.3 1.0 copy-start.7
  17.6 0.8 copy-start.3
  17.6 0.8 copy-start
  17.6 0.9 copy-start.2
  18.5 32.1 %copy-start.4 = (f32[4,4,4,8,128]{4,3,2,1,0:T(8,128)S(1)}, f32[4,4,4,8,128]{4,3,2,1,0:T(8,128)}, u32[]{:S(2)}) copy-start(f32[4,4,4,8,128]{4,3,2,1,0:T(8,128)} %param.22) | copy-start | bytes 786436
  45.4 5.2 %collective-permute-start.2 = (bf16[128,128]{1,0:T(8,128)(2,1)S(1)}, bf16[128,128]{1,0:T(8,128)(2,1)S(1)}, u32[]{:S(2)}, u32[]{:S(2)}) collective-permute-start(bf16[128,128]{1,0:T(8,128)(2,1)S(1)} %get-tuple-element.9), channel_id=1, source_target_pairs={{0,1},{1,0},{2,3},{3,2},{4,5},{5,4},{6,7},{7,6},{8,9},{9,8},{10,11... | collective-permute-start | bytes 98312 | tf_op jit(solution)/shard_map/ppermute | solution.py:264
  46.8 7.9 %collective-permute-start.3 = (bf16[128,128]{1,0:T(8,128)(2,1)S(1)}, bf16[128,128]{1,0:T(8,128)(2,1)S(1)}, u32[]{:S(2)}, u32[]{:S(2)}) collective-permute-start(bf16[128,128]{1,0:T(8,128)(2,1)S(1)} %get-tuple-element.9), channel_id=1, source_target_pairs={{1,2},{3,4},{5,6},{2,1},{4,3},{6,5},{9,10},{11,12},{13,14},{10,9},... | collective-permute-start | bytes 98312 | tf_op jit(solution)/shard_map/ppermute | solution.py:264
  82.4 1.3 %collective-permute-start.4 = (f32[4,4,8,128]{3,2,1,0:T(8,128)S(1)}, f32[4,4,8,128]{3,2,1,0:T(8,128)S(1)}, u32[]{:S(2)}, u32[]{:S(2)}) collective-permute-start(f32[4,4,8,128]{3,2,1,0:T(8,128)S(1)} %subtract_select_fusion), channel_id=1, source_target_pairs={{0,8},{8,0},{16,24},{24,16},{32,40},{40,32},{48,56},{56,48},{64,72... | collective-permute-start | bytes 196616 | tf_op jit(solution)/shard_map/ppermute | solution.py:316
  83.8 6.0 %collective-permute-start.5 = (f32[4,4,8,128]{3,2,1,0:T(8,128)S(1)}, f32[4,4,8,128]{3,2,1,0:T(8,128)S(1)}, u32[]{:S(2)}, u32[]{:S(2)}) collective-permute-start(f32[4,4,8,128]{3,2,1,0:T(8,128)S(1)} %select_add_fusion.3), channel_id=1, source_target_pairs={{0,16},{8,24},{16,0},{24,8},{32,48},{40,56},{48,32},{56,40},{64,80... | collective-permute-start | bytes 196616 | tf_op jit(solution)/shard_map/ppermute | solution.py:316
  90.0 9.2 %collective-permute-start.6 = (f32[4,4,8,128]{3,2,1,0:T(8,128)S(1)}, f32[4,4,8,128]{3,2,1,0:T(8,128)S(1)}, u32[]{:S(2)}, u32[]{:S(2)}) collective-permute-start(f32[4,4,8,128]{3,2,1,0:T(8,128)S(1)} %select_add_fusion.2), channel_id=1, source_target_pairs={{0,32},{8,40},{16,48},{24,56},{32,0},{40,8},{48,16},{56,24},{64,96... | collective-permute-start | bytes 196616 | tf_op jit(solution)/shard_map/ppermute | solution.py:316
  99.5 4.4 %collective-permute-start.7 = (f32[4,4,8,128]{3,2,1,0:T(8,128)S(1)}, f32[4,4,8,128]{3,2,1,0:T(8,128)S(1)}, u32[]{:S(2)}, u32[]{:S(2)}) collective-permute-start(f32[4,4,8,128]{3,2,1,0:T(8,128)S(1)} %select_add_fusion.1), channel_id=1, source_target_pairs={{0,64},{8,72},{16,80},{24,88},{32,96},{40,104},{48,112},{56,120},{... | collective-permute-start | bytes 196616 | tf_op jit(solution)/shard_map/ppermute | solution.py:316
  103.9 5.9 %collective-permute-start.8 = (f32[4,4,8,128]{3,2,1,0:T(8,128)S(1)}, f32[4,4,8,128]{3,2,1,0:T(8,128)S(1)}, u32[]{:S(2)}, u32[]{:S(2)}) collective-permute-start(f32[4,4,8,128]{3,2,1,0:T(8,128)S(1)} %select_add_fusion), channel_id=1, source_target_pairs={{0,128},{8,136},{16,144},{24,152},{32,160},{40,168},{48,176},{56,1... | collective-permute-start | bytes 196616 | tf_op jit(solution)/shard_map/ppermute | solution.py:316

commit v2 on v1

--- a/solution.py
+++ b/solution.py
@@ -41,8 +41,8 @@
 
 
 def halves(value):
-    high = value.astype(BF16)
-    return high, (value - high.astype(F32)).astype(BF16)
+    high = lax.reduce_precision(value, 8, 7)
+    return high.astype(BF16), (value - high).astype(BF16)
 
 
 def fine_step(

time: 111 us -> 111 us (level)
  no operation moved by 1% of the time
where the time goes in v2:
time: 111 us; the launch traced here: 110 us
  Pallas kernels  54.5 us (49%)
  starting transfers between devices  22.5 us (20%)
  waiting for transfers between devices  18 us (16%)
  other arithmetic  7.66 us (7%)
  local copies, waits for them, and re-layouts  7.22 us (7%)
    pallas_call x2, Pallas kernels, run_fine_step(): pl.pallas_call(fine_step, out_shape=(jax.ShapeDtypeStruct((CHAN, NZ, BLOC...  54.5 us
    ppermute x5, waiting for transfers between devices, per_device(): came = lax.ppermute(total, 'tm', [(i, i ^ distance) for i in range(count)])  13.9 us
    ppermute x5, starting transfers between devices, per_device(): came = lax.ppermute(total, 'tm', [(i, i ^ distance) for i in range(count)])  12.4 us
    ppermute x2, starting transfers between devices, exchange(): lax.ppermute(value, 'space', second)  7.93 us
    unnamed x34, local copies, waits for them, and re-layouts  5.48 us
    ppermute x2, waiting for transfers between devices, exchange(): lax.ppermute(value, 'space', second)  4.1 us
  transfers between devices with their start and end apart: 9, of which 6 were waited for; matrix products, arithmetic and copies ran while one was open for 7% of the time, Pallas kernels for 0%

profile of v2, /device:TPU:56, one launch (start us, length us, event | category | flops | bytes accessed | tf_op | source)
XLA Modules:
  0.0 110.5 jit_solution(8778801581355279036)
XLA Ops:
  0.0 0.9 convert_element_type.72
  0.9 4.2 %collective-permute-start.1 = (bf16[160,128]{1,0:T(8,128)(2,1)S(1)}, bf16[160,128]{1,0:T(8,128)(2,1)S(1)}, u32[]{:S(2)}, u32[]{:S(2)}) collective-permute-start(bf16[160,128]{1,0:T(8,128)(2,1)S(1)} %pad_maximum_fusion.1), channel_id=1, source_target_pairs={{1,2},{3,4},{5,6},{2,1},{4,3},{6,5},{9,10},{11,12},{13,14},{10,9},... | collective-permute-start | bytes 122888 | tf_op jit(solution)/shard_map/ppermute | solution.py:264
  5.1 0.8 collective-permute-start
  5.9 1.3 %fusion.9 = (s32[1,1]{1,0:T(1,128)}, s32[1,1]{1,0:T(1,128)}) fusion(s32[1,2]{1,0:T(1,128)} %param.20), kind=kLoop, calls=%fused_computation.74 | loop fusion | bytes 16 | tf_op jit(solution)/shard_map/slice | solution.py:228
  7.2 0.9 reduce_sum.206
  8.4 0.2 reduce-precision_convert_fusion
  8.6 0.5 copy-done.13
  9.2 0.6 copy-done.10
  9.8 0.7 copy-done.14
  10.5 1.9 %fusion.8 = (f32[]{:T(128)}, f32[]{:T(128)}) fusion(f32[8]{0:T(128)S(1)} %copy-done.14, s32[]{:T(128)} %bitcast.8, s32[]{:T(128)} %bitcast.4), kind=kLoop, calls=%fused_computation.67 | loop fusion | flops 46 | bytes 48 | tf_op jit(solution)/shard_map/reduce_sum | solution.py:229
  12.4 0.7 copy-done.16
  13.0 1.3 %broadcast_multiply_fusion.6 = (f32[3]{0:T(128)S(1)}, f32[3]{0:T(128)S(1)}) fusion(f32[3]{0:T(128)S(1)} %copy-done.16, f32[]{:T(128)} %get-tuple-element.22, f32[]{:T(128)} %get-tuple-element.21), kind=kLoop, calls=%fused_computation.72 | loop fusion | flops 6 | bytes 44 | tf_op jit(solution)/shard_map/mul | solution.py:237
  14.3 0.7 copy-done.8
  15.0 0.2 fusion.6
  15.6 0.5 copy-done.11
  16.4 0.8 copy-done.6
  17.7 0.7 copy-done.3
  18.5 26.9 %fine_step.2 = (f32[4,4,8,128]{3,2,1,0:T(8,128)S(1)}, bf16[128,128]{1,0:T(8,128)(2,1)S(1)}) custom-call(s32[2]{0:T(128)S(1)} %pad_add_fusion.where_ref, f32[4,4,8,128]{3,2,1,0:T(8,128)S(1)} %bitcast.19, f32[128,128]{1,0:T(8,128)S(1)} %slice_convert_fusion.1.first_ref, f32[128,128]{1,0:T(8,128)S(1)} %slice_convert_fusion.second_ref, ...), custom_call_target="tpu_custom_call" | custom-call | flops 10000000000 | bytes 2097152 | tf_op jit(solution)/shard_map/fine_step/pallas_call | solution.py:208
  45.4 1.4 %collective-permute-start.2 = (bf16[128,128]{1,0:T(8,128)(2,1)S(1)}, bf16[128,128]{1,0:T(8,128)(2,1)S(1)}, u32[]{:S(2)}, u32[]{:S(2)}) collective-permute-start(bf16[128,128]{1,0:T(8,128)(2,1)S(1)} %get-tuple-element.9), channel_id=1, source_target_pairs={{0,1},{1,0},{2,3},{3,2},{4,5},{5,4},{6,7},{7,6},{8,9},{9,8},{10,11... | collective-permute-start | bytes 98312 | tf_op jit(solution)/shard_map/ppermute | solution.py:264
  46.8 3.7 %collective-permute-start.3 = (bf16[128,128]{1,0:T(8,128)(2,1)S(1)}, bf16[128,128]{1,0:T(8,128)(2,1)S(1)}, u32[]{:S(2)}, u32[]{:S(2)}) collective-permute-start(bf16[128,128]{1,0:T(8,128)(2,1)S(1)} %get-tuple-element.9), channel_id=1, source_target_pairs={{1,2},{3,4},{5,6},{2,1},{4,3},{6,5},{9,10},{11,12},{13,14},{10,9},... | collective-permute-start | bytes 98312 | tf_op jit(solution)/shard_map/ppermute | solution.py:264
  50.6 4.1 %collective-permute-done.3 = bf16[128,128]{1,0:T(8,128)(2,1)S(1)} collective-permute-done((bf16[128,128]{1,0:T(8,128)(2,1)S(1)}, bf16[128,128]{1,0:T(8,128)(2,1)S(1)}, u32[]{:S(2)}, u32[]{:S(2)}) %collective-permute-start.3) | collective-permute-done | bytes 32800 | tf_op jit(solution)/shard_map/ppermute | solution.py:264
  54.7 27.7 %fine_step.3 = (f32[4,4,8,128]{3,2,1,0:T(8,128)S(1)}, bf16[128,128]{1,0:T(8,128)(2,1)}) custom-call(s32[2]{0:T(128)S(1)} %pad_add_fusion.where_ref, f32[4,4,8,128]{3,2,1,0:T(8,128)S(1)} %get-tuple-element.8.own_ref, f32[128,128]{1,0:T(8,128)S(1)} %convert_element_type.88.first_ref, f32[128,128]{1,0:T(8,128)S(1)} %convert_element_type.89.second_ref, ...), custom_call_target="tpu_custom_call" | custom-call | flops 10000000000 | bytes 2097152 | tf_op jit(solution)/shard_map/fine_step/pallas_call | solution.py:208
  82.5 1.2 %collective-permute-done.4 = f32[4,4,8,128]{3,2,1,0:T(8,128)S(1)} collective-permute-done((f32[4,4,8,128]{3,2,1,0:T(8,128)S(1)}, f32[4,4,8,128]{3,2,1,0:T(8,128)S(1)}, u32[]{:S(2)}, u32[]{:S(2)}) %collective-permute-start.4) | collective-permute-done | bytes 65568 | tf_op jit(solution)/shard_map/ppermute | solution.py:316
  83.8 3.6 %collective-permute-start.5 = (f32[4,4,8,128]{3,2,1,0:T(8,128)S(1)}, f32[4,4,8,128]{3,2,1,0:T(8,128)S(1)}, u32[]{:S(2)}, u32[]{:S(2)}) collective-permute-start(f32[4,4,8,128]{3,2,1,0:T(8,128)S(1)} %select_add_fusion.3), channel_id=1, source_target_pairs={{0,16},{8,24},{16,0},{24,8},{32,48},{40,56},{48,32},{56,40},{64,80... | collective-permute-start | bytes 196616 | tf_op jit(solution)/shard_map/ppermute | solution.py:316
  87.6 2.2 %collective-permute-done.5 = f32[4,4,8,128]{3,2,1,0:T(8,128)S(1)} collective-permute-done((f32[4,4,8,128]{3,2,1,0:T(8,128)S(1)}, f32[4,4,8,128]{3,2,1,0:T(8,128)S(1)}, u32[]{:S(2)}, u32[]{:S(2)}) %collective-permute-start.5) | collective-permute-done | bytes 65568 | tf_op jit(solution)/shard_map/ppermute | solution.py:316
  90.0 6.5 %collective-permute-start.6 = (f32[4,4,8,128]{3,2,1,0:T(8,128)S(1)}, f32[4,4,8,128]{3,2,1,0:T(8,128)S(1)}, u32[]{:S(2)}, u32[]{:S(2)}) collective-permute-start(f32[4,4,8,128]{3,2,1,0:T(8,128)S(1)} %select_add_fusion.2), channel_id=1, source_target_pairs={{0,32},{8,40},{16,48},{24,56},{32,0},{40,8},{48,16},{56,24},{64,96... | collective-permute-start | bytes 196616 | tf_op jit(solution)/shard_map/ppermute | solution.py:316
  96.6 2.6 %collective-permute-done.6 = f32[4,4,8,128]{3,2,1,0:T(8,128)S(1)} collective-permute-done((f32[4,4,8,128]{3,2,1,0:T(8,128)S(1)}, f32[4,4,8,128]{3,2,1,0:T(8,128)S(1)}, u32[]{:S(2)}, u32[]{:S(2)}) %collective-permute-start.6) | collective-permute-done | bytes 65568 | tf_op jit(solution)/shard_map/ppermute | solution.py:316
  99.5 0.8 collective-permute-start.7
  100.3 3.5 %collective-permute-done.7 = f32[4,4,8,128]{3,2,1,0:T(8,128)S(1)} collective-permute-done((f32[4,4,8,128]{3,2,1,0:T(8,128)S(1)}, f32[4,4,8,128]{3,2,1,0:T(8,128)S(1)}, u32[]{:S(2)}, u32[]{:S(2)}) %collective-permute-start.7) | collective-permute-done | bytes 65568 | tf_op jit(solution)/shard_map/ppermute | solution.py:316
  103.9 1.3 %collective-permute-start.8 = (f32[4,4,8,128]{3,2,1,0:T(8,128)S(1)}, f32[4,4,8,128]{3,2,1,0:T(8,128)S(1)}, u32[]{:S(2)}, u32[]{:S(2)}) collective-permute-start(f32[4,4,8,128]{3,2,1,0:T(8,128)S(1)} %select_add_fusion), channel_id=1, source_target_pairs={{0,128},{8,136},{16,144},{24,152},{32,160},{40,168},{48,176},{56,1... | collective-permute-start | bytes 196616 | tf_op jit(solution)/shard_map/ppermute | solution.py:316
  105.3 4.4 %collective-permute-done.8 = f32[4,4,8,128]{3,2,1,0:T(8,128)S(1)} collective-permute-done((f32[4,4,8,128]{3,2,1,0:T(8,128)S(1)}, f32[4,4,8,128]{3,2,1,0:T(8,128)S(1)}, u32[]{:S(2)}, u32[]{:S(2)}) %collective-permute-start.8) | collective-permute-done | bytes 65568 | tf_op jit(solution)/shard_map/ppermute | solution.py:316
  109.8 0.7 add_bitcast_fusion
  (79 shorter events, 2.6 us)
Async XLA Ops:
  0.0 0.9 copy-start.1
  0.0 8.3 %copy-start.5 = (bf16[6,128,128]{2,1,0:T(8,128)(2,1)S(1)}, bf16[6,128,128]{2,1,0:T(8,128)(2,1)}, u32[]{:S(2)}) copy-start(bf16[6,128,128]{2,1,0:T(8,128)(2,1)} %param.30) | copy-start | bytes 589828
  0.9 16.6 %collective-permute-start.1 = (bf16[160,128]{1,0:T(8,128)(2,1)S(1)}, bf16[160,128]{1,0:T(8,128)(2,1)S(1)}, u32[]{:S(2)}, u32[]{:S(2)}) collective-permute-start(bf16[160,128]{1,0:T(8,128)(2,1)S(1)} %pad_maximum_fusion.1), channel_id=1, source_target_pairs={{1,2},{3,4},{5,6},{2,1},{4,3},{6,5},{9,10},{11,12},{13,14},{10,9},... | collective-permute-start | bytes 122888 | tf_op jit(solution)/shard_map/ppermute | solution.py:264
  5.1 12.5 %collective-permute-start = (bf16[160,128]{1,0:T(8,128)(2,1)S(1)}, bf16[160,128]{1,0:T(8,128)(2,1)S(1)}, u32[]{:S(2)}, u32[]{:S(2)}) collective-permute-start(bf16[160,128]{1,0:T(8,128)(2,1)S(1)} %pad_maximum_fusion.1), channel_id=1, source_target_pairs={{0,1},{1,0},{2,3},{3,2},{4,5},{5,4},{6,7},{7,6},{8,9},{9,8},{10,11... | collective-permute-start | bytes 122888 | tf_op jit(solution)/shard_map/ppermute | solution.py:264
  7.2 0.9 copy-start.9
  8.4 0.7 copy-start.13
  9.1 0.7 copy-start.10
  9.8 0.7 copy-start.14
  12.4 0.7 copy-start.16
  14.3 0.7 copy-start.8
  14.3 0.7 copy-start.12
  15.4 0.7 copy-start.11
  15.6 0.7 copy-start.15
  16.3 0.9 copy-start.6
  16.3 1.0 copy-start.7
  17.6 0.8 copy-start.3
  17.6 0.8 copy-start
  17.6 0.9 copy-start.2
  18.5 32.1 %copy-start.4 = (f32[4,4,4,8,128]{4,3,2,1,0:T(8,128)S(1)}, f32[4,4,4,8,128]{4,3,2,1,0:T(8,128)}, u32[]{:S(2)}) copy-start(f32[4,4,4,8,128]{4,3,2,1,0:T(8,128)} %param.22) | copy-start | bytes 786436
  45.4 5.2 %collective-permute-start.2 = (bf16[128,128]{1,0:T(8,128)(2,1)S(1)}, bf16[128,128]{1,0:T(8,128)(2,1)S(1)}, u32[]{:S(2)}, u32[]{:S(2)}) collective-permute-start(bf16[128,128]{1,0:T(8,128)(2,1)S(1)} %get-tuple-element.9), channel_id=1, source_target_pairs={{0,1},{1,0},{2,3},{3,2},{4,5},{5,4},{6,7},{7,6},{8,9},{9,8},{10,11... | collective-permute-start | bytes 98312 | tf_op jit(solution)/shard_map/ppermute | solution.py:264
  46.8 7.9 %collective-permute-start.3 = (bf16[128,128]{1,0:T(8,128)(2,1)S(1)}, bf16[128,128]{1,0:T(8,128)(2,1)S(1)}, u32[]{:S(2)}, u32[]{:S(2)}) collective-permute-start(bf16[128,128]{1,0:T(8,128)(2,1)S(1)} %get-tuple-element.9), channel_id=1, source_target_pairs={{1,2},{3,4},{5,6},{2,1},{4,3},{6,5},{9,10},{11,12},{13,14},{10,9},... | collective-permute-start | bytes 98312 | tf_op jit(solution)/shard_map/ppermute | solution.py:264
  82.4 1.3 %collective-permute-start.4 = (f32[4,4,8,128]{3,2,1,0:T(8,128)S(1)}, f32[4,4,8,128]{3,2,1,0:T(8,128)S(1)}, u32[]{:S(2)}, u32[]{:S(2)}) collective-permute-start(f32[4,4,8,128]{3,2,1,0:T(8,128)S(1)} %subtract_select_fusion), channel_id=1, source_target_pairs={{0,8},{8,0},{16,24},{24,16},{32,40},{40,32},{48,56},{56,48},{64,72... | collective-permute-start | bytes 196616 | tf_op jit(solution)/shard_map/ppermute | solution.py:316
  83.8 6.0 %collective-permute-start.5 = (f32[4,4,8,128]{3,2,1,0:T(8,128)S(1)}, f32[4,4,8,128]{3,2,1,0:T(8,128)S(1)}, u32[]{:S(2)}, u32[]{:S(2)}) collective-permute-start(f32[4,4,8,128]{3,2,1,0:T(8,128)S(1)} %select_add_fusion.3), channel_id=1, source_target_pairs={{0,16},{8,24},{16,0},{24,8},{32,48},{40,56},{48,32},{56,40},{64,80... | collective-permute-start | bytes 196616 | tf_op jit(solution)/shard_map/ppermute | solution.py:316
  90.0 9.2 %collective-permute-start.6 = (f32[4,4,8,128]{3,2,1,0:T(8,128)S(1)}, f32[4,4,8,128]{3,2,1,0:T(8,128)S(1)}, u32[]{:S(2)}, u32[]{:S(2)}) collective-permute-start(f32[4,4,8,128]{3,2,1,0:T(8,128)S(1)} %select_add_fusion.2), channel_id=1, source_target_pairs={{0,32},{8,40},{16,48},{24,56},{32,0},{40,8},{48,16},{56,24},{64,96... | collective-permute-start | bytes 196616 | tf_op jit(solution)/shard_map/ppermute | solution.py:316
  99.5 4.4 %collective-permute-start.7 = (f32[4,4,8,128]{3,2,1,0:T(8,128)S(1)}, f32[4,4,8,128]{3,2,1,0:T(8,128)S(1)}, u32[]{:S(2)}, u32[]{:S(2)}) collective-permute-start(f32[4,4,8,128]{3,2,1,0:T(8,128)S(1)} %select_add_fusion.1), channel_id=1, source_target_pairs={{0,64},{8,72},{16,80},{24,88},{32,96},{40,104},{48,112},{56,120},{... | collective-permute-start | bytes 196616 | tf_op jit(solution)/shard_map/ppermute | solution.py:316
  103.9 5.9 %collective-permute-start.8 = (f32[4,4,8,128]{3,2,1,0:T(8,128)S(1)}, f32[4,4,8,128]{3,2,1,0:T(8,128)S(1)}, u32[]{:S(2)}, u32[]{:S(2)}) collective-permute-start(f32[4,4,8,128]{3,2,1,0:T(8,128)S(1)} %select_add_fusion), channel_id=1, source_target_pairs={{0,128},{8,136},{16,144},{24,152},{32,160},{40,168},{48,176},{56,1... | collective-permute-start | bytes 196616 | tf_op jit(solution)/shard_map/ppermute | solution.py:316

commit v3 on v2

v3 whole, which is shorter than its diff:
```python
import functools

import jax
import jax.numpy as jnp
from jax import lax
from jax.experimental import pallas as pl
from jax.experimental.pallas import tpu as pltpu
from jax.sharding import PartitionSpec as P

HID = 128
CHAN = 4
NZ = 4
TYPES = 3
RATES = 8
LAYERS = 6
STEPS = 2
NY = 128

EPS = 1e-05

GROUPS, GROUP = 8, 16
PADDED = (GROUPS + 2) * GROUP
BLOCK = 8
FRAME = 3 * BLOCK
SPARE = FRAME + 2
HELD = SPARE + 3
FEATURES = 3 * CHAN + 2 * TYPES
ROWS = CHAN * NZ * BLOCK

F32, BF16 = jnp.float32, jnp.bfloat16


def dot(a, b, **kw):
    return jnp.dot(a, b, preferred_element_type=F32, **kw)


def dot_nt(a, b):
    return lax.dot_general(a, b, (((1,), (1,)), ((), ())), preferred_element_type=F32)


def grouped(dtype):
    row = lax.broadcasted_iota(jnp.int32, (NY, NY), 0)
    cell = lax.broadcasted_iota(jnp.int32, (NY, NY), 1)
    return (cell == (row % GROUP) * GROUPS + row // GROUP).astype(dtype)


def fine_step(
    where_ref, own_ref, first_ref, second_ref, kind_ref, kind_first_ref, kind_second_ref,
    enc_ref, in_ref, out_ref, bias_ref, gain_ref, dec_ref,
    state_ref, send_ref,
    hidden_ref, norm_ref, enter_ref,
):
    order = grouped(F32).astype(BF16)
    position = where_ref[0]
    last = where_ref[1]
    odd = position % 2 == 1
    at_left = position == 0
    at_right = position == last

    def strength(hidden):
        return jnp.sum(hidden * hidden, axis=-1, keepdims=True)

    def normalize(layer, hidden, target):
        normal = hidden * lax.rsqrt(strength(hidden) + HID * EPS) * gain_ref[layer]
        line = lax.broadcasted_iota(jnp.int32, (GROUP, HID), 0)
        before = jnp.where(line == 0, 0.0, pltpu.roll(normal[NY - GROUP :], 1, 0))
        after = jnp.where(line == GROUP - 1, 0.0, pltpu.roll(normal[:GROUP], GROUP - 1, 0))
        target[:GROUP, :] = before.astype(BF16)
        target[GROUP : GROUP + NY, :] = normal.astype(BF16)
        target[GROUP + NY :, :] = after.astype(BF16)

    @pl.when(at_left)
    def _():
        norm_ref[:, BLOCK - 1] = jnp.zeros((2, NZ, PADDED, HID), BF16)

    @pl.when(at_right)
    def _():
        norm_ref[:, 2 * BLOCK] = jnp.zeros((2, NZ, PADDED, HID), BF16)

    def encode(block, states, kinds, z):
        rows = []
        highs = [state.astype(BF16).astype(F32) for state in states]
        rows.extend(highs)
        rows.extend(state - high for state, high in zip(states, highs))
        rows.extend(highs)
        marks = [(kinds == float(kind)).astype(F32) for kind in range(TYPES)]
        rows.extend(marks)
        rows.extend(marks)
        table = jnp.concatenate(rows, axis=0).astype(BF16)
        turned = dot_nt(order, table).astype(BF16)
        for x in range(BLOCK):
            hidden = dot(turned, enc_ref[:, x * HID : (x + 1) * HID])
            hidden_ref[block * BLOCK + x, z] = hidden
            normalize(0, hidden, norm_ref.at[0, block * BLOCK + x, z])

    for z in range(NZ):
        encode(
            1,
            [own_ref[c, z] for c in range(CHAN)],
            kind_ref[z].astype(F32),
            z,
        )

    def neighbour(block, take_first):
        states = jnp.where(take_first, first_ref[:ROWS, :], second_ref[:ROWS, :]).astype(F32)
        kinds = jnp.where(take_first, kind_first_ref[ROWS:, :], kind_second_ref[ROWS:, :]).astype(F32)
        for z in range(NZ):
            parts = []
            for c in range(CHAN):
                at = (c * NZ + z) * BLOCK
                parts.append(states[at : at + BLOCK])
            encode(block, parts, kinds[z * BLOCK : (z + 1) * BLOCK], z)

    @pl.when(jnp.logical_not(at_left))
    def _():
        neighbour(0, odd)

    @pl.when(jnp.logical_not(at_right))
    def _():
        neighbour(2, jnp.logical_not(odd))

    def rows_of(layer):
        reach = LAYERS - 1 - layer
        low = jnp.where(at_left, BLOCK, BLOCK - reach)
        high = jnp.where(at_right, 2 * BLOCK, 2 * BLOCK + reach)
        return low, high

    tiles = [(d, z) for d in range(2) for z in range(NZ)]

    def group(start):
        return slice(start * GROUP, (start + 1) * GROUP)

    def gather(layer, x):
        slot = layer % 2
        loaded = {}

        def read(dx, z, start):
            if (dx, z, start) not in loaded:
                loaded[dx, z, start] = norm_ref[slot, x + dx, z, group(start), :]
            return loaded[dx, z, start]

        rows = []
        for start in range(1, GROUPS + 1):
            for d, z in tiles:
                along_x = read(d - 1, z, start) + read(d + 1, z, start)
                along_y = read(d, z, start - 1) + read(d, z, start + 1)
                beside = [read(d, w, start) for w in (z - 1, z + 1) if 0 <= w < NZ]
                along_z = functools.reduce(lambda a, b: a + b, beside)
                rows.append(jnp.concatenate([read(d, z, start), along_x + along_y + along_z], axis=-1))
        return jnp.concatenate(rows, axis=0)

    def turn(_, pairs):
        newest, second, third = pairs
        half = enter_ref[...]
        message = half * jnp.tanh(half) + half
        moved = dot(message, out_ref[second[0], :HID, :])
        entered = dot(gather(*newest), in_ref[newest[0]])
        enter_ref[...] = (entered + bias_ref[newest[0]]).astype(BF16)
        outside = jnp.logical_and(at_right, third[1] + 1 == 2 * BLOCK)
        slot = (third[0] + 1) % 2
        for d, z in tiles:
            row = third[1] if d == 0 else jnp.where(outside, SPARE, third[1] + 1)
            normalize(third[0] + 1, hidden_ref[third[1] + d, z], norm_ref.at[slot, row, z])
        for start in range(GROUPS):
            for at, (d, z) in enumerate(tiles):
                part = moved[group(start * len(tiles) + at)]
                hidden_ref[second[1] + d, z, group(start), :] += part
        layer, x = newest
        ends = x + 2 >= rows_of(layer)[1]
        next_layer = jnp.where(ends, layer + 1, layer)
        next_x = jnp.where(ends, rows_of(layer + 1)[0], x + 2)
        done = next_layer >= LAYERS
        following = (jnp.where(done, 0, next_layer), jnp.where(done, SPARE, next_x))
        return following, newest, second

    def count(layer):
        low, high = rows_of(layer)
        return (high - low + 1) // 2

    total = sum(count(layer) for layer in range(LAYERS))
    none = (jnp.int32(0), jnp.int32(SPARE))
    start = (jnp.int32(0), rows_of(0)[0])
    lax.fori_loop(0, total + 2, turn, (start, none, none))

    found = []
    for z in range(NZ):
        both = jnp.zeros((CHAN * BLOCK, NY), F32)
        for x in range(0, BLOCK, 2):
            pair = jnp.concatenate(
                [norm_ref[0, BLOCK + x + d, z, GROUP : GROUP + NY, :] for d in range(2)], axis=-1
            )
            both = both + dot_nt(dec_ref[x // 2], pair)
        found.append(both)
    change = dot(jnp.concatenate(found, axis=0), grouped(F32), precision=lax.Precision.HIGHEST)
    for c in range(CHAN):
        for z in range(NZ):
            at = (z * CHAN + c) * BLOCK
            state_ref[c, z] = own_ref[c, z] + change[at : at + BLOCK]
    send_ref[...] = state_ref[...].reshape(CHAN * NZ * BLOCK, NY).astype(BF16)


def run_fine_step(*args):
    vmem = pl.BlockSpec(memory_space=pltpu.VMEM)
    return pl.pallas_call(
        fine_step,
        out_shape=(
            jax.ShapeDtypeStruct((CHAN, NZ, BLOCK, NY), F32),
            jax.ShapeDtypeStruct((CHAN * NZ * BLOCK, NY), BF16),
        ),
        in_specs=[pl.BlockSpec(memory_space=pltpu.SMEM)] + [vmem] * 12,
        out_specs=(vmem, vmem),
        scratch_shapes=[
            pltpu.VMEM((HELD, NZ, NY, HID), F32),
            pltpu.VMEM((2, HELD, NZ, PADDED, HID), BF16),
            pltpu.VMEM((2 * NZ * NY, HID), BF16),
        ],
        compiler_params=pltpu.CompilerParams(vmem_limit_bytes=40 * 2**20),
        cost_estimate=pl.CostEstimate(flops=10**10, bytes_accessed=2**21, transcendentals=10**7),
        name="fine_step",
    )(*args)


def centred(rows):
    return rows - jnp.mean(rows, axis=-1, keepdims=True)


def halves(value):
    high = value.astype(BF16)
    return high, (value - high.astype(F32)).astype(BF16)


def prepare(
    plan_ref, rate_ref,
    enc_hbm, type_hbm, force_hbm, gain_hbm, self_hbm, neigh_hbm, out_hbm, bias_hbm, dec_gain_hbm, dec_hbm,
    enc_first_ref, enc_second_ref, in_ref, leave_ref, bias_ref, gains_ref, dec_out_ref,
    enc, kind, force, gain, own, neigh, out, bias, dec_gain, dec, sems,
):
    sources = (enc_hbm, type_hbm, force_hbm, gain_hbm, self_hbm, neigh_hbm, out_hbm, bias_hbm, dec_gain_hbm, dec_hbm)
    targets = (enc, kind, force, gain, own, neigh, out, bias, dec_gain, dec)
    copies = [pltpu.make_async_copy(a, b, sems.at[n]) for n, (a, b) in enumerate(zip(sources, targets))]
    for copy in copies:
        copy.start()
    for copy in copies:
        copy.wait()

    line = lax.broadcasted_iota(jnp.int32, (BLOCK, HID), 0)

    def spread(rows, x):
        return [jnp.where(line == x, row, 0.0) for row in rows]

    weights = halves(centred(enc[...]))
    for step, enc_ref in enumerate((enc_first_ref, enc_second_ref)):
        rate = rate_ref[plan_ref[0, step]]
        push = rate * force[...]
        table = kind[...]
        kinds = halves(centred(jnp.concatenate([table[0:1], table[1:2] + push, table[2:3] - push], axis=0)))
        high, low = [half.astype(F32) for half in weights]
        rows = [part[c : c + 1] for part in (high, high, low) for c in range(CHAN)]
        rows += [part.astype(F32)[k : k + 1] for part in kinds for k in range(TYPES)]
        for x in range(BLOCK):
            enc_ref[:, x * HID : (x + 1) * HID] = jnp.concatenate(spread(rows, x), axis=0).astype(BF16)
    for layer in range(LAYERS):
        half = jnp.asarray(0.5, BF16)
        in_ref[layer, :HID, :] = own[layer] * half
        in_ref[layer, HID:, :] = neigh[layer] * half
        high, low = halves(centred(out[layer].astype(F32)))
        leave_ref[layer, :HID, :] = high
        leave_ref[layer, HID:, :] = low
        bias_ref[layer] = bias[layer : layer + 1, :] * 0.5
        gains_ref[layer] = gain[layer : layer + 1, :] * HID**0.5
    gains_ref[LAYERS] = dec_gain[...] * HID**0.5
    rows = [dec[...].astype(F32)[c : c + 1] for c in range(CHAN)]
    for x in range(BLOCK):
        part = jnp.concatenate(spread(rows, x), axis=0).astype(BF16)
        dec_out_ref[x // 2, :, (x % 2) * HID : (x % 2 + 1) * HID] = part


def run_prepare(plan, rate_values, *arrays):
    vmem = pl.BlockSpec(memory_space=pltpu.VMEM)
    smem = pl.BlockSpec(memory_space=pltpu.SMEM)
    shapes = (
        ((FEATURES * BLOCK, BLOCK * HID), BF16),
        ((FEATURES * BLOCK, BLOCK * HID), BF16),
        ((LAYERS, 2 * HID, HID), BF16),
        ((LAYERS, 2 * HID, HID), BF16),
        ((LAYERS, 1, HID), F32),
        ((LAYERS + 1, 1, HID), F32),
        ((BLOCK // 2, CHAN * BLOCK, 2 * HID), BF16),
    )
    return pl.pallas_call(
        prepare,
        out_shape=tuple(jax.ShapeDtypeStruct(shape, dtype) for shape, dtype in shapes),
        in_specs=[smem] * 2 + [pl.BlockSpec(memory_space=pl.ANY)] * len(arrays),
        out_specs=(vmem,) * len(shapes),
        scratch_shapes=[pltpu.VMEM(array.shape, array.dtype) for array in arrays]
        + [pltpu.SemaphoreType.DMA((len(arrays),))],
        compiler_params=pltpu.CompilerParams(vmem_limit_bytes=16 * 2**20),
        cost_estimate=pl.CostEstimate(flops=10**8, bytes_accessed=2**21, transcendentals=0),
        name="prepare",
    )(plan, rate_values, *arrays)


def exchange(value):
    count = lax.axis_size("space")
    first = [(i, i ^ 1) for i in range(count)]
    second = [(i, i + 1) for i in range(1, count - 1, 2)] + [(i + 1, i) for i in range(1, count - 1, 2)]
    return lax.ppermute(value, "space", first), lax.ppermute(value, "space", second)


def matvec(matrix, vector):
    return jnp.sum(matrix * vector[None], axis=1)


def matmat(left, right):
    return jnp.sum(left[:, :, None] * right[None], axis=1)


def per_device(
    prev_starts, plan, cell_type, coarse_matrix, rate_values, enc_weight, type_table, force_vector,
    norm_gain, self_weight, neigh_weight, out_weight, layer_bias, dec_gain, dec_weight,
):
    own = prev_starts[0]
    position = lax.axis_index("space")
    where = jnp.stack([position, lax.axis_size("space") - 1]).astype(jnp.int32)

    outgoing = jnp.concatenate(
        [own.reshape(ROWS, NY).astype(BF16), cell_type.reshape(NZ * BLOCK, NY).astype(BF16)], axis=0
    )
    kinds = sides = exchange(outgoing)
    enc_first, enc_second, *weights = run_prepare(
        plan, rate_values, enc_weight, type_table, force_vector[None], norm_gain, self_weight,
        neigh_weight, out_weight, layer_bias, dec_gain[None], dec_weight,
    )

    state = own
    for step_index in range(STEPS):
        state, outgoing = run_fine_step(
            where, state, *sides, cell_type, *kinds, (enc_first, enc_second)[step_index], *weights
        )
        if step_index + 1 < STEPS:
            sides = exchange(outgoing)

    window = lax.axis_index("tm")
    total = jnp.where(window == 0, state, state - matvec(coarse_matrix, own))
    corrected = total
    power, reach = coarse_matrix, coarse_matrix
    count = lax.axis_size("tm")
    distance = 1
    while distance < count:
        came = lax.ppermute(total.astype(BF16), "tm", [(i, i ^ distance) for i in range(count)])
        came = came.astype(F32)
        upper = (window // distance) % 2 == 1
        corrected = corrected + jnp.where(upper, matvec(reach, came), 0.0)
        if 2 * distance < count:
            lower_total = jnp.where(upper, came, total)
            upper_total = jnp.where(upper, total, came)
            total = upper_total + matvec(power, lower_total)
            reach = jnp.where(upper, matmat(power, reach), reach)
            power = matmat(power, power)
        distance *= 2
    return corrected[None]


def solution(mesh):
    return jax.shard_map(
        per_device,
        mesh=mesh,
        in_specs=(
            P("tm", None, None, "space", None),
            P("tm", None),
            P(None, "space", None),
            P(None, None, None, "space", None),
        )
        + (P(),) * 11,
        out_specs=P("tm", None, None, "space", None),
        check_vma=False,
    )
```

time: 111 us -> 97.5 us (0.88)
  other arithmetic: 7.66 us -> 2.6 us
  Pallas kernels: 54.5 us -> 50.1 us
  waiting for transfers between devices: 18 us -> 16.3 us
  starting transfers between devices: 22.5 us -> 21.3 us
    pallas_call x2, Pallas kernels: 54.5 us -> 48.4 us  [run_fine_step(): pl.pallas_call(fine_step, out_shape=(jax.ShapeDtypeStruct((CHAN, NZ, BLOC...]
    reduce_sum x4 -> x0, other arithmetic: 3.13 us -> none  [the longest x1 1.91 us: lookup_rate(): return jnp.sum(jnp.where(picks, rate_values, 0.0))]
    ppermute x5, waiting for transfers between devices: 13.9 us -> 11.8 us  [per_device(): lax.ppermute(total.astype(BF16), 'tm', [(i, i ^ distance) for i in range(...]
    pallas_call x0 -> x1, Pallas kernels: none -> 1.75 us  [run_prepare(): pl.pallas_call(prepare, out_shape=tuple((jax.ShapeDtypeStruct(shape, dtyp...]
    mul x5 -> x0, other arithmetic: 1.54 us -> none  [the longest x1 1.27 us: encoder(): well = jnp.array([0.0, 1.0, -1.0], F32)[:, None] * rate_value * force_vector]
    slice x1 -> x0, local copies, waits for them, and re-layouts: 1.32 us -> none  [lookup_rate(): picks = jnp.arange(RATES, dtype=jnp.int32) == sched_row[step_index]]
    unnamed x34 -> x30, local copies, waits for them, and re-layouts: 5.48 us -> 6.55 us
  transfers between devices with their start and end apart: 9 -> 9, of which waited for: 6 -> 6; matrix products, arithmetic and copies ran while one was open for 7% -> 0% of each run, Pallas kernels for 0% -> 2%
where the time goes in v3:
time: 97.5 us; the launch traced here: 97.2 us
  Pallas kernels  50.1 us (51%)
  starting transfers between devices  21.3 us (22%)
  waiting for transfers between devices  16.3 us (17%)
  local copies, waits for them, and re-layouts  6.55 us (7%)
  other arithmetic  2.6 us (3%)
    pallas_call x2, Pallas kernels, run_fine_step(): pl.pallas_call(fine_step, out_shape=(jax.ShapeDtypeStruct((CHAN, NZ, BLOC...  48.4 us
    ppermute x5, waiting for transfers between devices, per_device(): lax.ppermute(total.astype(BF16), 'tm', [(i, i ^ distance) for i in range(...  11.8 us
    ppermute x5, starting transfers between devices, per_device(): lax.ppermute(total.astype(BF16), 'tm', [(i, i ^ distance) for i in range(...  11.6 us
    ppermute x2, starting transfers between devices, exchange(): lax.ppermute(value, 'space', second)  6.91 us
    unnamed x30, local copies, waits for them, and re-layouts  6.55 us
    ppermute x2, waiting for transfers between devices, exchange(): lax.ppermute(value, 'space', second)  4.47 us
    ppermute x2, starting transfers between devices, exchange(): lax.ppermute(value, 'space', first)  2.72 us
  transfers between devices with their start and end apart: 9, of which 6 were waited for; matrix products, arithmetic and copies ran while one was open for 0% of the time, Pallas kernels for 2%

profile of v3, /device:TPU:56, one launch (start us, length us, event | category | flops | bytes accessed | tf_op | source)
XLA Modules:
  0.0 97.2 jit_solution(4601083006913221280)
XLA Ops:
  0.0 0.9 convert_element_type.42
  0.9 1.6 %collective-permute-start = (bf16[160,128]{1,0:T(8,128)(2,1)S(1)}, bf16[160,128]{1,0:T(8,128)(2,1)S(1)}, u32[]{:S(2)}, u32[]{:S(2)}) collective-permute-start(bf16[160,128]{1,0:T(8,128)(2,1)S(1)} %pad_maximum_fusion), channel_id=1, source_target_pairs={{0,1},{1,0},{2,3},{3,2},{4,5},{5,4},{6,7},{7,6},{8,9},{9,8},{10,11... | collective-permute-start | bytes 122888 | tf_op jit(solution)/shard_map/ppermute | solution.py:307
  2.5 3.5 %collective-permute-start.1 = (bf16[160,128]{1,0:T(8,128)(2,1)S(1)}, bf16[160,128]{1,0:T(8,128)(2,1)S(1)}, u32[]{:S(2)}, u32[]{:S(2)}) collective-permute-start(bf16[160,128]{1,0:T(8,128)(2,1)S(1)} %pad_maximum_fusion), channel_id=1, source_target_pairs={{1,2},{3,4},{5,6},{2,1},{4,3},{6,5},{9,10},{11,12},{13,14},{10,9},... | collective-permute-start | bytes 122888 | tf_op jit(solution)/shard_map/ppermute | solution.py:307
  6.1 0.6 copy-done.5
  6.8 0.9 copy-done.2
  7.8 0.9 copy-done.3
  8.7 0.7 copy-done.6
  9.4 0.7 copy-done.8
  10.1 0.7 copy-done.10
  10.7 0.7 copy-done.11
  11.4 0.7 copy-done.12
  12.0 0.7 copy-done.13
  12.7 1.8 %prepare.1 = (bf16[144,1024]{1,0:T(8,128)(2,1)S(1)}, bf16[144,1024]{1,0:T(8,128)(2,1)S(1)}, bf16[6,256,128]{2,1,0:T(8,128)(2,1)S(1)}, bf16[6,256,128]{2,1,0:T(8,...) custom-call(s32[1,2]{1,0:T(1,128)S(1)} %copy-done.10, ...), custom_call_target="tpu_custom_call" | custom-call | flops 100000000 | bytes 2097152 | tf_op jit(solution)/shard_map/prepare/pallas_call | solution.py:290
  14.5 23.9 %fine_step.2 = (f32[4,4,8,128]{3,2,1,0:T(8,128)S(1)}, bf16[128,128]{1,0:T(8,128)(2,1)S(1)}) custom-call(s32[2]{0:T(128)S(1)} %pad_add_fusion.where_ref, f32[4,4,8,128]{3,2,1,0:T(8,128)S(1)} %bitcast.9, bf16[160,128]{1,0:T(8,128)(2,1)S(1)} %collective-permute-done.first_ref.kind_first_ref, ...), custom_call_target="tpu_custom_call" | custom-call | flops 10000000000 | bytes 2097152 | tf_op jit(solution)/shard_map/fine_step/pallas_call | solution.py:204
  38.4 1.1 %collective-permute-start.2 = (bf16[128,128]{1,0:T(8,128)(2,1)S(1)}, bf16[128,128]{1,0:T(8,128)(2,1)S(1)}, u32[]{:S(2)}, u32[]{:S(2)}) collective-permute-start(bf16[128,128]{1,0:T(8,128)(2,1)S(1)} %get-tuple-element.22), channel_id=1, source_target_pairs={{0,1},{1,0},{2,3},{3,2},{4,5},{5,4},{6,7},{7,6},{8,9},{9,8},{10,11... | collective-permute-start | bytes 98312 | tf_op jit(solution)/shard_map/ppermute | solution.py:307
  39.5 3.4 %collective-permute-start.3 = (bf16[128,128]{1,0:T(8,128)(2,1)S(1)}, bf16[128,128]{1,0:T(8,128)(2,1)S(1)}, u32[]{:S(2)}, u32[]{:S(2)}) collective-permute-start(bf16[128,128]{1,0:T(8,128)(2,1)S(1)} %get-tuple-element.22), channel_id=1, source_target_pairs={{1,2},{3,4},{5,6},{2,1},{4,3},{6,5},{9,10},{11,12},{13,14},{10,9},... | collective-permute-start | bytes 98312 | tf_op jit(solution)/shard_map/ppermute | solution.py:307
  43.0 4.5 %collective-permute-done.3.second_ref = bf16[128,128]{1,0:T(8,128)(2,1)S(1)} collective-permute-done((bf16[128,128]{1,0:T(8,128)(2,1)S(1)}, bf16[128,128]{1,0:T(8,128)(2,1)S(1)}, u32[]{:S(2)}, u32[]{:S(2)}) %collective-permute-start.3) | collective-permute-done | bytes 32800 | tf_op jit(solution)/shard_map/ppermute | solution.py:307
  47.4 24.5 %fine_step.3 = (f32[4,4,8,128]{3,2,1,0:T(8,128)S(1)}, bf16[128,128]{1,0:T(8,128)(2,1)}) custom-call(s32[2]{0:T(128)S(1)} %pad_add_fusion.where_ref, f32[4,4,8,128]{3,2,1,0:T(8,128)S(1)} %get-tuple-element.21.own_ref, bf16[128,128]{1,0:T(8,128)(2,1)S(1)} %collective-permute-done.2.first_ref, bf16[128,128]{1,0:T(8,128)(2,1)S(1)} %collective-permute-done.3.second_ref, ...), custom_call_target="tpu_custom_call" | custom-call | flops 10000000000 | bytes 2097152 | tf_op jit(solution)/shard_map/fine_step/pallas_call | solution.py:204
  71.9 0.1 collective-permute-start.4
  72.1 1.2 %collective-permute-done.4 = bf16[4,4,8,128]{3,2,1,0:T(8,128)(2,1)S(1)} collective-permute-done((bf16[4,4,8,128]{3,2,1,0:T(8,128)(2,1)S(1)}, bf16[4,4,8,128]{3,2,1,0:T(8,128)(2,1)S(1)}, u32[]{:S(2)}, u32[]{:S(2)}) %collective-permute-start.4) | collective-permute-done | bytes 32800 | tf_op jit(solution)/shard_map/ppermute | solution.py:350
  73.3 3.4 %collective-permute-start.5 = (bf16[4,4,8,128]{3,2,1,0:T(8,128)(2,1)S(1)}, bf16[4,4,8,128]{3,2,1,0:T(8,128)(2,1)S(1)}, u32[]{:S(2)}, u32[]{:S(2)}) collective-permute-start(bf16[4,4,8,128]{3,2,1,0:T(8,128)(2,1)S(1)} %get-tuple-element.41), channel_id=1, source_target_pairs={{0,16},{8,24},{16,0},{24,8},{32,48},{40,56},{48,32},{56,40},{64,80... | collective-permute-start | bytes 98312 | tf_op jit(solution)/shard_map/ppermute | solution.py:350
  76.9 1.7 %collective-permute-done.5 = bf16[4,4,8,128]{3,2,1,0:T(8,128)(2,1)S(1)} collective-permute-done((bf16[4,4,8,128]{3,2,1,0:T(8,128)(2,1)S(1)}, bf16[4,4,8,128]{3,2,1,0:T(8,128)(2,1)S(1)}, u32[]{:S(2)}, u32[]{:S(2)}) %collective-permute-start.5) | collective-permute-done | bytes 32800 | tf_op jit(solution)/shard_map/ppermute | solution.py:350
  78.7 6.0 %collective-permute-start.6 = (bf16[4,4,8,128]{3,2,1,0:T(8,128)(2,1)S(1)}, bf16[4,4,8,128]{3,2,1,0:T(8,128)(2,1)S(1)}, u32[]{:S(2)}, u32[]{:S(2)}) collective-permute-start(bf16[4,4,8,128]{3,2,1,0:T(8,128)(2,1)S(1)} %get-tuple-element.39), channel_id=1, source_target_pairs={{0,32},{8,40},{16,48},{24,56},{32,0},{40,8},{48,16},{56,24},{64,96... | collective-permute-start | bytes 98312 | tf_op jit(solution)/shard_map/ppermute | solution.py:350
  84.7 0.2 multiply_reduce_fusion.3
  84.9 1.7 %collective-permute-done.6 = bf16[4,4,8,128]{3,2,1,0:T(8,128)(2,1)S(1)} collective-permute-done((bf16[4,4,8,128]{3,2,1,0:T(8,128)(2,1)S(1)}, bf16[4,4,8,128]{3,2,1,0:T(8,128)(2,1)S(1)}, u32[]{:S(2)}, u32[]{:S(2)}) %collective-permute-start.6) | collective-permute-done | bytes 32800 | tf_op jit(solution)/shard_map/ppermute | solution.py:350
  86.7 0.2 multiply_reduce_fusion.1
  86.9 0.8 collective-permute-start.7
  87.8 3.1 %collective-permute-done.7 = bf16[4,4,8,128]{3,2,1,0:T(8,128)(2,1)S(1)} collective-permute-done((bf16[4,4,8,128]{3,2,1,0:T(8,128)(2,1)S(1)}, bf16[4,4,8,128]{3,2,1,0:T(8,128)(2,1)S(1)}, u32[]{:S(2)}, u32[]{:S(2)}) %collective-permute-start.7) | collective-permute-done | bytes 32800 | tf_op jit(solution)/shard_map/ppermute | solution.py:350
  91.0 1.3 %collective-permute-start.8 = (bf16[4,4,8,128]{3,2,1,0:T(8,128)(2,1)S(1)}, bf16[4,4,8,128]{3,2,1,0:T(8,128)(2,1)S(1)}, u32[]{:S(2)}, u32[]{:S(2)}) collective-permute-start(bf16[4,4,8,128]{3,2,1,0:T(8,128)(2,1)S(1)} %add_convert_fusion), channel_id=1, source_target_pairs={{0,128},{8,136},{16,144},{24,152},{32,160},{40,168},{48,176},{56,1... | collective-permute-start | bytes 98312 | tf_op jit(solution)/shard_map/ppermute | solution.py:350
  92.3 0.1 multiply_reduce_fusion
  92.4 4.1 %collective-permute-done.8 = bf16[4,4,8,128]{3,2,1,0:T(8,128)(2,1)S(1)} collective-permute-done((bf16[4,4,8,128]{3,2,1,0:T(8,128)(2,1)S(1)}, bf16[4,4,8,128]{3,2,1,0:T(8,128)(2,1)S(1)}, u32[]{:S(2)}, u32[]{:S(2)}) %collective-permute-start.8) | collective-permute-done | bytes 32800 | tf_op jit(solution)/shard_map/ppermute | solution.py:350
  96.6 0.7 add_bitcast_fusion
  (50 shorter events, 0.8 us)
Async XLA Ops:
  0.0 0.9 copy-start.4
  0.0 6.1 %copy-start.1 = (bf16[6,128,128]{2,1,0:T(8,128)(2,1)S(1)}, bf16[6,128,128]{2,1,0:T(8,128)(2,1)}, u32[]{:S(2)}) copy-start(bf16[6,128,128]{2,1,0:T(8,128)(2,1)} %self_hbm.1) | copy-start | bytes 589828
  0.9 13.5 %collective-permute-start = (bf16[160,128]{1,0:T(8,128)(2,1)S(1)}, bf16[160,128]{1,0:T(8,128)(2,1)S(1)}, u32[]{:S(2)}, u32[]{:S(2)}) collective-permute-start(bf16[160,128]{1,0:T(8,128)(2,1)S(1)} %pad_maximum_fusion), channel_id=1, source_target_pairs={{0,1},{1,0},{2,3},{3,2},{4,5},{5,4},{6,7},{7,6},{8,9},{9,8},{10,11... | collective-permute-start | bytes 122888 | tf_op jit(solution)/shard_map/ppermute | solution.py:307
  2.5 12.0 %collective-permute-start.1 = (bf16[160,128]{1,0:T(8,128)(2,1)S(1)}, bf16[160,128]{1,0:T(8,128)(2,1)S(1)}, u32[]{:S(2)}, u32[]{:S(2)}) collective-permute-start(bf16[160,128]{1,0:T(8,128)(2,1)S(1)} %pad_maximum_fusion), channel_id=1, source_target_pairs={{1,2},{3,4},{5,6},{2,1},{4,3},{6,5},{9,10},{11,12},{13,14},{10,9},... | collective-permute-start | bytes 122888 | tf_op jit(solution)/shard_map/ppermute | solution.py:307
  6.0 0.7 copy-start.5
  6.1 0.7 copy-start.7
  6.1 0.7 copy-start.9
  6.8 0.9 copy-start.2
  7.8 0.9 copy-start.3
  8.7 0.7 copy-start.6
  9.4 0.7 copy-start.8
  10.1 0.7 copy-start.10
  10.7 0.7 copy-start.11
  11.4 0.7 copy-start.12
  12.0 0.7 copy-start.13
  12.7 1.8 %copy-start = (f32[1,4,4,8,128]{4,3,2,1,0:T(8,128)S(1)}, f32[1,4,4,8,128]{4,3,2,1,0:T(8,128)}, u32[]{:S(2)}) copy-start(f32[1,4,4,8,128]{4,3,2,1,0:T(8,128)} %param.15) | copy-start | bytes 196612
  14.5 28.4 %copy-start.14 = (f32[4,4,4,8,128]{4,3,2,1,0:T(8,128)S(1)}, f32[4,4,4,8,128]{4,3,2,1,0:T(8,128)}, u32[]{:S(2)}) copy-start(f32[4,4,4,8,128]{4,3,2,1,0:T(8,128)} %param.18) | copy-start | bytes 786436
  38.4 4.6 %collective-permute-start.2 = (bf16[128,128]{1,0:T(8,128)(2,1)S(1)}, bf16[128,128]{1,0:T(8,128)(2,1)S(1)}, u32[]{:S(2)}, u32[]{:S(2)}) collective-permute-start(bf16[128,128]{1,0:T(8,128)(2,1)S(1)} %get-tuple-element.22), channel_id=1, source_target_pairs={{0,1},{1,0},{2,3},{3,2},{4,5},{5,4},{6,7},{7,6},{8,9},{9,8},{10,11... | collective-permute-start | bytes 98312 | tf_op jit(solution)/shard_map/ppermute | solution.py:307
  39.5 7.9 %collective-permute-start.3 = (bf16[128,128]{1,0:T(8,128)(2,1)S(1)}, bf16[128,128]{1,0:T(8,128)(2,1)S(1)}, u32[]{:S(2)}, u32[]{:S(2)}) collective-permute-start(bf16[128,128]{1,0:T(8,128)(2,1)S(1)} %get-tuple-element.22), channel_id=1, source_target_pairs={{1,2},{3,4},{5,6},{2,1},{4,3},{6,5},{9,10},{11,12},{13,14},{10,9},... | collective-permute-start | bytes 98312 | tf_op jit(solution)/shard_map/ppermute | solution.py:307
  71.9 1.3 %collective-permute-start.4 = (bf16[4,4,8,128]{3,2,1,0:T(8,128)(2,1)S(1)}, bf16[4,4,8,128]{3,2,1,0:T(8,128)(2,1)S(1)}, u32[]{:S(2)}, u32[]{:S(2)}) collective-permute-start(bf16[4,4,8,128]{3,2,1,0:T(8,128)(2,1)S(1)} %get-tuple-element.43), channel_id=1, source_target_pairs={{0,8},{8,0},{16,24},{24,16},{32,40},{40,32},{48,56},{56,48},{64,72... | collective-permute-start | bytes 98312 | tf_op jit(solution)/shard_map/ppermute | solution.py:350
  73.3 5.3 %collective-permute-start.5 = (bf16[4,4,8,128]{3,2,1,0:T(8,128)(2,1)S(1)}, bf16[4,4,8,128]{3,2,1,0:T(8,128)(2,1)S(1)}, u32[]{:S(2)}, u32[]{:S(2)}) collective-permute-start(bf16[4,4,8,128]{3,2,1,0:T(8,128)(2,1)S(1)} %get-tuple-element.41), channel_id=1, source_target_pairs={{0,16},{8,24},{16,0},{24,8},{32,48},{40,56},{48,32},{56,40},{64,80... | collective-permute-start | bytes 98312 | tf_op jit(solution)/shard_map/ppermute | solution.py:350
  78.7 7.9 %collective-permute-start.6 = (bf16[4,4,8,128]{3,2,1,0:T(8,128)(2,1)S(1)}, bf16[4,4,8,128]{3,2,1,0:T(8,128)(2,1)S(1)}, u32[]{:S(2)}, u32[]{:S(2)}) collective-permute-start(bf16[4,4,8,128]{3,2,1,0:T(8,128)(2,1)S(1)} %get-tuple-element.39), channel_id=1, source_target_pairs={{0,32},{8,40},{16,48},{24,56},{32,0},{40,8},{48,16},{56,24},{64,96... | collective-permute-start | bytes 98312 | tf_op jit(solution)/shard_map/ppermute | solution.py:350
  86.9 4.0 %collective-permute-start.7 = (bf16[4,4,8,128]{3,2,1,0:T(8,128)(2,1)S(1)}, bf16[4,4,8,128]{3,2,1,0:T(8,128)(2,1)S(1)}, u32[]{:S(2)}, u32[]{:S(2)}) collective-permute-start(bf16[4,4,8,128]{3,2,1,0:T(8,128)(2,1)S(1)} %get-tuple-element.37), channel_id=1, source_target_pairs={{0,64},{8,72},{16,80},{24,88},{32,96},{40,104},{48,112},{56,120},{... | collective-permute-start | bytes 98312 | tf_op jit(solution)/shard_map/ppermute | solution.py:350
  91.0 5.5 %collective-permute-start.8 = (bf16[4,4,8,128]{3,2,1,0:T(8,128)(2,1)S(1)}, bf16[4,4,8,128]{3,2,1,0:T(8,128)(2,1)S(1)}, u32[]{:S(2)}, u32[]{:S(2)}) collective-permute-start(bf16[4,4,8,128]{3,2,1,0:T(8,128)(2,1)S(1)} %add_convert_fusion), channel_id=1, source_target_pairs={{0,128},{8,136},{16,144},{24,152},{32,160},{40,168},{48,176},{56,1... | collective-permute-start | bytes 98312 | tf_op jit(solution)/shard_map/ppermute | solution.py:350

commit v4 on v3

--- a/solution.py
+++ b/solution.py
@@ -24,8 +24,10 @@
 FRAME = 3 * BLOCK
 SPARE = FRAME + 2
 HELD = SPARE + 3
-FEATURES = 3 * CHAN + 2 * TYPES
+FEATURES = 2 * CHAN + 2 * TYPES
 ROWS = CHAN * NZ * BLOCK
+
+SWAPS = {1: 1, 2: 2, 4: 6, 8: 8, 16: 24}
 
 F32, BF16 = jnp.float32, jnp.bfloat16
 
@@ -77,47 +79,37 @@
     def _():
         norm_ref[:, 2 * BLOCK] = jnp.zeros((2, NZ, PADDED, HID), BF16)
 
-    def encode(block, states, kinds, z):
-        rows = []
-        highs = [state.astype(BF16).astype(F32) for state in states]
-        rows.extend(highs)
-        rows.extend(state - high for state, high in zip(states, highs))
-        rows.extend(highs)
-        marks = [(kinds == float(kind)).astype(F32) for kind in range(TYPES)]
-        rows.extend(marks)
-        rows.extend(marks)
-        table = jnp.concatenate(rows, axis=0).astype(BF16)
-        turned = dot_nt(order, table).astype(BF16)
-        for x in range(BLOCK):
-            hidden = dot(turned, enc_ref[:, x * HID : (x + 1) * HID])
-            hidden_ref[block * BLOCK + x, z] = hidden
-            normalize(0, hidden, norm_ref.at[0, block * BLOCK + x, z])
-
-    for z in range(NZ):
-        encode(
-            1,
-            [own_ref[c, z] for c in range(CHAN)],
-            kind_ref[z].astype(F32),
-            z,
-        )
-
-    def neighbour(block, take_first):
+    def encode(block, states, kinds, xs):
+        turned = []
+        for z in range(NZ):
+            rows = [states[(c * NZ + z) * BLOCK : (c * NZ + z + 1) * BLOCK] for c in range(CHAN)]
+            kind_row = kinds[z * BLOCK : (z + 1) * BLOCK]
+            marks = [(kind_row == float(kind)).astype(F32) for kind in range(TYPES)]
+            table = jnp.concatenate(rows + rows + marks + marks, axis=0).astype(BF16)
+            turned.append(dot_nt(order, table).astype(BF16))
+        turned = jnp.concatenate(turned, axis=0)
+        for first in range(xs.start, xs.stop, 2):
+            found = dot(turned, enc_ref[:, first * HID : (first + 2) * HID])
+            for x in (first, first + 1):
+                for z in range(NZ):
+                    hidden = found[z * NY : (z + 1) * NY, (x - first) * HID : (x - first + 1) * HID]
+                    hidden_ref[block * BLOCK + x, z] = hidden
+                    normalize(0, hidden, norm_ref.at[0, block * BLOCK + x, z])
+
+    encode(1, own_ref[...].reshape(ROWS, NY), kind_ref[...].reshape(NZ * BLOCK, NY).astype(F32), range(BLOCK))
+
+    def neighbour(block, take_first, xs):
         states = jnp.where(take_first, first_ref[:ROWS, :], second_ref[:ROWS, :]).astype(F32)
         kinds = jnp.where(take_first, kind_first_ref[ROWS:, :], kind_second_ref[ROWS:, :]).astype(F32)
-        for z in range(NZ):
-            parts = []
-            for c in range(CHAN):
-                at = (c * NZ + z) * BLOCK
-                parts.append(states[at : at + BLOCK])
-            encode(block, parts, kinds[z * BLOCK : (z + 1) * BLOCK], z)
+        encode(block, states, kinds, xs)
 
     @pl.when(jnp.logical_not(at_left))
     def _():
-        neighbour(0, odd)
+        neighbour(0, odd, range(BLOCK - LAYERS, BLOCK))
 
     @pl.when(jnp.logical_not(at_right))
     def _():
-        neighbour(2, jnp.logical_not(odd))
+        neighbour(2, jnp.logical_not(odd), range(LAYERS))
 
     def rows_of(layer):
         reach = LAYERS - 1 - layer
@@ -153,7 +145,7 @@
         newest, second, third = pairs
         half = enter_ref[...]
         message = half * jnp.tanh(half) + half
-        moved = dot(message, out_ref[second[0], :HID, :])
+        moved = dot(message, out_ref[second[0]])
         entered = dot(gather(*newest), in_ref[newest[0]])
         enter_ref[...] = (entered + bias_ref[newest[0]]).astype(BF16)
         outside = jnp.logical_and(at_right, third[1] + 1 == 2 * BLOCK)
@@ -255,7 +247,7 @@
         table = kind[...]
         kinds = halves(centred(jnp.concatenate([table[0:1], table[1:2] + push, table[2:3] - push], axis=0)))
         high, low = [half.astype(F32) for half in weights]
-        rows = [part[c : c + 1] for part in (high, high, low) for c in range(CHAN)]
+        rows = [part[c : c + 1] for part in (high, low) for c in range(CHAN)]
         rows += [part.astype(F32)[k : k + 1] for part in kinds for k in range(TYPES)]
         for x in range(BLOCK):
             enc_ref[:, x * HID : (x + 1) * HID] = jnp.concatenate(spread(rows, x), axis=0).astype(BF16)
@@ -263,9 +255,7 @@
         half = jnp.asarray(0.5, BF16)
         in_ref[layer, :HID, :] = own[layer] * half
         in_ref[layer, HID:, :] = neigh[layer] * half
-        high, low = halves(centred(out[layer].astype(F32)))
-        leave_ref[layer, :HID, :] = high
-        leave_ref[layer, HID:, :] = low
+        leave_ref[layer] = centred(out[layer].astype(F32)).astype(BF16)
         bias_ref[layer] = bias[layer : layer + 1, :] * 0.5
         gains_ref[layer] = gain[layer : layer + 1, :] * HID**0.5
     gains_ref[LAYERS] = dec_gain[...] * HID**0.5
@@ -282,7 +272,7 @@
         ((FEATURES * BLOCK, BLOCK * HID), BF16),
         ((FEATURES * BLOCK, BLOCK * HID), BF16),
         ((LAYERS, 2 * HID, HID), BF16),
-        ((LAYERS, 2 * HID, HID), BF16),
+        ((LAYERS, HID, HID), BF16),
         ((LAYERS, 1, HID), F32),
         ((LAYERS + 1, 1, HID), F32),
         ((BLOCK // 2, CHAN * BLOCK, 2 * HID), BF16),
@@ -290,7 +280,7 @@
     return pl.pallas_call(
         prepare,
         out_shape=tuple(jax.ShapeDtypeStruct(shape, dtype) for shape, dtype in shapes),
-        in_specs=[smem] * 2 + [pl.BlockSpec(memory_space=pl.ANY)] * len(arrays),
+        in_specs=[smem] * 2 + [pl.BlockSpec(memory_space=pltpu.HBM)] * len(arrays),
         out_specs=(vmem,) * len(shapes),
         scratch_shapes=[pltpu.VMEM(array.shape, array.dtype) for array in arrays]
         + [pltpu.SemaphoreType.DMA((len(arrays),))],
@@ -347,8 +337,8 @@
     count = lax.axis_size("tm")
     distance = 1
     while distance < count:
-        came = lax.ppermute(total.astype(BF16), "tm", [(i, i ^ distance) for i in range(count)])
-        came = came.astype(F32)
+        partners = [(i, i ^ SWAPS[distance]) for i in range(count)]
+        came = lax.ppermute(total.astype(jnp.float16), "tm", partners).astype(F32)
         upper = (window // distance) % 2 == 1
         corrected = corrected + jnp.where(upper, matvec(reach, came), 0.0)
         if 2 * distance < count:

time: 97.5 us -> 89.3 us (0.916)
  local copies, waits for them, and re-layouts: 6.55 us -> 2.54 us
  Pallas kernels: 50.1 us -> 47.3 us
  starting transfers between devices: 21.3 us -> 18.5 us
    unnamed x30, local copies, waits for them, and re-layouts: 6.55 us -> 2.54 us
    pallas_call x2, Pallas kernels: 48.4 us -> 45.6 us  [run_fine_step(): pl.pallas_call(fine_step, out_shape=(jax.ShapeDtypeStruct((CHAN, NZ, BLOC...]
    ppermute x2, starting transfers between devices: 2.72 us -> 1 us  [exchange(): lax.ppermute(value, 'space', first)]
    ppermute x5, starting transfers between devices: 11.6 us -> 10 us  [per_device(): came = lax.ppermute(total.astype(jnp.float16), 'tm', partners).astype(F32)]
  transfers between devices with their start and end apart: 9 -> 9, of which waited for: 6 -> 6; matrix products, arithmetic and copies ran while one was open for 0% -> 1% of each run, Pallas kernels for 2% -> 2%
where the time goes in v4:
time: 89.3 us; the launch traced here: 88.9 us
  Pallas kernels  47.3 us (53%)
  starting transfers between devices  18.5 us (21%)
  waiting for transfers between devices  16.9 us (19%)
  other arithmetic  3.32 us (4%)
  local copies, waits for them, and re-layouts  2.54 us (3%)
    pallas_call x2, Pallas kernels, run_fine_step(): pl.pallas_call(fine_step, out_shape=(jax.ShapeDtypeStruct((CHAN, NZ, BLOC...  45.6 us
    ppermute x5, waiting for transfers between devices, per_device(): came = lax.ppermute(total.astype(jnp.float16), 'tm', partners).astype(F32)  12.3 us
    ppermute x5, starting transfers between devices, per_device(): came = lax.ppermute(total.astype(jnp.float16), 'tm', partners).astype(F32)  10 us
    ppermute x2, starting transfers between devices, exchange(): lax.ppermute(value, 'space', second)  7.47 us
    ppermute x2, waiting for transfers between devices, exchange(): lax.ppermute(value, 'space', second)  4.52 us
    unnamed x30, local copies, waits for them, and re-layouts  2.54 us
  transfers between devices with their start and end apart: 9, of which 6 were waited for; matrix products, arithmetic and copies ran while one was open for 1% of the time, Pallas kernels for 2%

profile of v4, /device:TPU:56, one launch (start us, length us, event | category | flops | bytes accessed | tf_op | source)
XLA Modules:
  0.0 88.9 jit_solution(9323732275489623711)
XLA Ops:
  0.0 0.8 convert_bitcast_fusion
  0.8 0.8 convert_element_type.42
  1.7 4.3 %collective-permute-start.1 = (bf16[160,128]{1,0:T(8,128)(2,1)S(1)}, bf16[160,128]{1,0:T(8,128)(2,1)S(1)}, u32[]{:S(2)}, u32[]{:S(2)}) collective-permute-start(bf16[160,128]{1,0:T(8,128)(2,1)S(1)} %pad_maximum_fusion), channel_id=1, source_target_pairs={{1,2},{3,4},{5,6},{2,1},{4,3},{6,5},{9,10},{11,12},{13,14},{10,9},... | collective-permute-start | bytes 122888 | tf_op jit(solution)/shard_map/ppermute | solution.py:297
  6.0 0.8 collective-permute-start
  6.8 0.1 pad_add_fusion.where_ref
  6.9 0.6 copy-done.7
  7.5 0.0 copy-done.9
  7.5 0.9 %copy-done.2 = bf16[6,128,128]{2,1,0:T(8,128)(2,1)S(1)} copy-done((bf16[6,128,128]{2,1,0:T(8,128)(2,1)S(1)}, bf16[6,128,128]{2,1,0:T(8,128)(2,1)}, u32[]{:S(2)}) %copy-start.2) | copy-done | bytes 196632
  8.5 0.9 %copy-done.3 = bf16[6,128,128]{2,1,0:T(8,128)(2,1)S(1)} copy-done((bf16[6,128,128]{2,1,0:T(8,128)(2,1)S(1)}, bf16[6,128,128]{2,1,0:T(8,128)(2,1)}, u32[]{:S(2)}) %copy-start.3) | copy-done | bytes 196632
  9.4 1.7 %prepare.1 = (bf16[112,1024]{1,0:T(8,128)(2,1)S(1)}, bf16[112,1024]{1,0:T(8,128)(2,1)S(1)}, bf16[6,256,128]{2,1,0:T(8,128)(2,1)S(1)}, bf16[6,128,128]{2,1,0:T(8,...) custom-call(s32[1,2]{1,0:T(1,128)S(1)} %copy-done.10, ...), custom_call_target="tpu_custom_call" | custom-call | flops 100000000 | bytes 2097152 | tf_op jit(solution)/shard_map/prepare/pallas_call | solution.py:280
  11.2 22.5 %fine_step.2 = (f32[4,4,8,128]{3,2,1,0:T(8,128)S(1)}, bf16[128,128]{1,0:T(8,128)(2,1)S(1)}) custom-call(s32[2]{0:T(128)S(1)} %pad_add_fusion.where_ref, f32[4,4,8,128]{3,2,1,0:T(8,128)S(1)} %bitcast.9, bf16[160,128]{1,0:T(8,128)(2,1)S(1)} %collective-permute-done.first_ref.kind_first_ref, ...), custom_call_target="tpu_custom_call" | custom-call | flops 10000000000 | bytes 2097152 | tf_op jit(solution)/shard_map/fine_step/pallas_call | solution.py:196
  33.7 3.1 %collective-permute-start.3 = (bf16[128,128]{1,0:T(8,128)(2,1)S(1)}, bf16[128,128]{1,0:T(8,128)(2,1)S(1)}, u32[]{:S(2)}, u32[]{:S(2)}) collective-permute-start(bf16[128,128]{1,0:T(8,128)(2,1)S(1)} %get-tuple-element.22), channel_id=1, source_target_pairs={{1,2},{3,4},{5,6},{2,1},{4,3},{6,5},{9,10},{11,12},{13,14},{10,9},... | collective-permute-start | bytes 98312 | tf_op jit(solution)/shard_map/ppermute | solution.py:297
  36.8 0.2 collective-permute-start.2
  37.1 4.5 %collective-permute-done.3.second_ref = bf16[128,128]{1,0:T(8,128)(2,1)S(1)} collective-permute-done((bf16[128,128]{1,0:T(8,128)(2,1)S(1)}, bf16[128,128]{1,0:T(8,128)(2,1)S(1)}, u32[]{:S(2)}, u32[]{:S(2)}) %collective-permute-start.3) | collective-permute-done | bytes 32800 | tf_op jit(solution)/shard_map/ppermute | solution.py:297
  41.6 23.1 %fine_step.3 = (f32[4,4,8,128]{3,2,1,0:T(8,128)S(1)}, bf16[128,128]{1,0:T(8,128)(2,1)}) custom-call(s32[2]{0:T(128)S(1)} %pad_add_fusion.where_ref, f32[4,4,8,128]{3,2,1,0:T(8,128)S(1)} %get-tuple-element.21.own_ref, bf16[128,128]{1,0:T(8,128)(2,1)S(1)} %collective-permute-done.2.first_ref, bf16[128,128]{1,0:T(8,128)(2,1)S(1)} %collective-permute-done.3.second_ref, ...), custom_call_target="tpu_custom_call" | custom-call | flops 10000000000 | bytes 2097152 | tf_op jit(solution)/shard_map/fine_step/pallas_call | solution.py:196
  64.7 0.1 collective-permute-start.4
  64.9 1.2 %collective-permute-done.4 = f16[4,4,8,128]{3,2,1,0:T(8,128)(2,1)S(1)} collective-permute-done((f16[4,4,8,128]{3,2,1,0:T(8,128)(2,1)S(1)}, f16[4,4,8,128]{3,2,1,0:T(8,128)(2,1)S(1)}, u32[]{:S(2)}, u32[]{:S(2)}) %collective-permute-start.4) | collective-permute-done | bytes 32800 | tf_op jit(solution)/shard_map/ppermute | solution.py:341
  66.1 3.4 %collective-permute-start.5 = (f16[4,4,8,128]{3,2,1,0:T(8,128)(2,1)S(1)}, f16[4,4,8,128]{3,2,1,0:T(8,128)(2,1)S(1)}, u32[]{:S(2)}, u32[]{:S(2)}) collective-permute-start(f16[4,4,8,128]{3,2,1,0:T(8,128)(2,1)S(1)} %get-tuple-element.41), channel_id=1, source_target_pairs={{0,16},{8,24},{16,0},{24,8},{32,48},{40,56},{48,32},{56,40},{64,80... | collective-permute-start | bytes 98312 | tf_op jit(solution)/shard_map/ppermute | solution.py:341
  69.5 0.1 multiply_reduce_fusion.5
  69.7 1.7 %collective-permute-done.5 = f16[4,4,8,128]{3,2,1,0:T(8,128)(2,1)S(1)} collective-permute-done((f16[4,4,8,128]{3,2,1,0:T(8,128)(2,1)S(1)}, f16[4,4,8,128]{3,2,1,0:T(8,128)(2,1)S(1)}, u32[]{:S(2)}, u32[]{:S(2)}) %collective-permute-start.5) | collective-permute-done | bytes 32800 | tf_op jit(solution)/shard_map/ppermute | solution.py:341
  71.4 0.1 multiply_reduce_fusion.12
  71.5 5.4 %collective-permute-start.6 = (f16[4,4,8,128]{3,2,1,0:T(8,128)(2,1)S(1)}, f16[4,4,8,128]{3,2,1,0:T(8,128)(2,1)S(1)}, u32[]{:S(2)}, u32[]{:S(2)}) collective-permute-start(f16[4,4,8,128]{3,2,1,0:T(8,128)(2,1)S(1)} %get-tuple-element.39), channel_id=1, source_target_pairs={{0,48},{8,56},{16,32},{24,40},{32,16},{40,24},{48,0},{56,8},{64,11... | collective-permute-start | bytes 98312 | tf_op jit(solution)/shard_map/ppermute | solution.py:341
  76.9 0.2 multiply_reduce_fusion.3
  77.1 1.7 %collective-permute-done.6 = f16[4,4,8,128]{3,2,1,0:T(8,128)(2,1)S(1)} collective-permute-done((f16[4,4,8,128]{3,2,1,0:T(8,128)(2,1)S(1)}, f16[4,4,8,128]{3,2,1,0:T(8,128)(2,1)S(1)}, u32[]{:S(2)}, u32[]{:S(2)}) %collective-permute-start.6) | collective-permute-done | bytes 32800 | tf_op jit(solution)/shard_map/ppermute | solution.py:341
  78.9 0.8 collective-permute-start.7
  79.8 0.2 multiply_reduce_fusion.1
  80.0 2.9 %collective-permute-done.7 = f16[4,4,8,128]{3,2,1,0:T(8,128)(2,1)S(1)} collective-permute-done((f16[4,4,8,128]{3,2,1,0:T(8,128)(2,1)S(1)}, f16[4,4,8,128]{3,2,1,0:T(8,128)(2,1)S(1)}, u32[]{:S(2)}, u32[]{:S(2)}) %collective-permute-start.7) | collective-permute-done | bytes 32800 | tf_op jit(solution)/shard_map/ppermute | solution.py:341
  83.0 0.3 collective-permute-start.8
  83.3 0.1 multiply_reduce_fusion
  83.4 4.8 %collective-permute-done.8 = f16[4,4,8,128]{3,2,1,0:T(8,128)(2,1)S(1)} collective-permute-done((f16[4,4,8,128]{3,2,1,0:T(8,128)(2,1)S(1)}, f16[4,4,8,128]{3,2,1,0:T(8,128)(2,1)S(1)}, u32[]{:S(2)}, u32[]{:S(2)}) %collective-permute-start.8) | collective-permute-done | bytes 32800 | tf_op jit(solution)/shard_map/ppermute | solution.py:341
  88.2 0.1 multiply_reduce_fusion.8
  88.2 0.7 add_bitcast_fusion
  (50 shorter events, 0.5 us)
Async XLA Ops:
  0.0 6.9 %copy-start.1 = (bf16[6,128,128]{2,1,0:T(8,128)(2,1)S(1)}, bf16[6,128,128]{2,1,0:T(8,128)(2,1)}, u32[]{:S(2)}) copy-start(bf16[6,128,128]{2,1,0:T(8,128)(2,1)} %self_hbm.1) | copy-start | bytes 589828
  1.6 5.3 %copy-start.10 = (s32[1,2]{1,0:T(1,128)S(1)}, s32[1,2]{1,0:T(1,128)}, u32[]{:S(2)}) copy-start(s32[1,2]{1,0:T(1,128)} %plan_ref.1) | copy-start | bytes 28
  1.6 5.3 %copy-start.11 = (f32[8]{0:T(128)S(1)}, f32[8]{0:T(128)}, u32[]{:S(2)}) copy-start(f32[8]{0:T(128)} %rate_ref.1) | copy-start | bytes 100
  1.6 5.3 %copy-start.12 = (f32[128]{0:T(128)S(1)}, f32[128]{0:T(128)}, u32[]{:S(2)}) copy-start(f32[128]{0:T(128)} %param.22) | copy-start | bytes 1540
  1.6 5.3 %copy-start.13 = (f32[128]{0:T(128)S(1)}, f32[128]{0:T(128)}, u32[]{:S(2)}) copy-start(f32[128]{0:T(128)} %param.28) | copy-start | bytes 1540
  1.7 9.4 %collective-permute-start.1 = (bf16[160,128]{1,0:T(8,128)(2,1)S(1)}, bf16[160,128]{1,0:T(8,128)(2,1)S(1)}, u32[]{:S(2)}, u32[]{:S(2)}) collective-permute-start(bf16[160,128]{1,0:T(8,128)(2,1)S(1)} %pad_maximum_fusion), channel_id=1, source_target_pairs={{1,2},{3,4},{5,6},{2,1},{4,3},{6,5},{9,10},{11,12},{13,14},{10,9},... | collective-permute-start | bytes 122888 | tf_op jit(solution)/shard_map/ppermute | solution.py:297
  6.0 5.1 %collective-permute-start = (bf16[160,128]{1,0:T(8,128)(2,1)S(1)}, bf16[160,128]{1,0:T(8,128)(2,1)S(1)}, u32[]{:S(2)}, u32[]{:S(2)}) collective-permute-start(bf16[160,128]{1,0:T(8,128)(2,1)S(1)} %pad_maximum_fusion), channel_id=1, source_target_pairs={{0,1},{1,0},{2,3},{3,2},{4,5},{5,4},{6,7},{7,6},{8,9},{9,8},{10,11... | collective-permute-start | bytes 122888 | tf_op jit(solution)/shard_map/ppermute | solution.py:297
  6.8 0.7 copy-start.7
  6.8 0.7 copy-start.8
  6.8 0.7 copy-start.6
  6.8 0.7 copy-start.5
  6.9 0.7 copy-start.9
  7.5 0.9 %copy-start.2 = (bf16[6,128,128]{2,1,0:T(8,128)(2,1)S(1)}, bf16[6,128,128]{2,1,0:T(8,128)(2,1)}, u32[]{:S(2)}) copy-start(bf16[6,128,128]{2,1,0:T(8,128)(2,1)} %neigh_hbm.1) | copy-start | bytes 589828
  8.5 0.9 %copy-start.3 = (bf16[6,128,128]{2,1,0:T(8,128)(2,1)S(1)}, bf16[6,128,128]{2,1,0:T(8,128)(2,1)}, u32[]{:S(2)}) copy-start(bf16[6,128,128]{2,1,0:T(8,128)(2,1)} %out_hbm.1) | copy-start | bytes 589828
  9.4 1.7 %copy-start = (f32[1,4,4,8,128]{4,3,2,1,0:T(8,128)S(1)}, f32[1,4,4,8,128]{4,3,2,1,0:T(8,128)}, u32[]{:S(2)}) copy-start(f32[1,4,4,8,128]{4,3,2,1,0:T(8,128)} %param.15) | copy-start | bytes 196612
  9.4 1.7 %copy-start.4 = (s32[4,8,128]{2,1,0:T(8,128)S(1)}, s32[4,8,128]{2,1,0:T(8,128)}, u32[]{:S(2)}) copy-start(s32[4,8,128]{2,1,0:T(8,128)} %kind_ref.3) | copy-start | bytes 49156
  11.1 25.9 %copy-start.14 = (f32[4,4,4,8,128]{4,3,2,1,0:T(8,128)S(1)}, f32[4,4,4,8,128]{4,3,2,1,0:T(8,128)}, u32[]{:S(2)}) copy-start(f32[4,4,4,8,128]{4,3,2,1,0:T(8,128)} %param.18) | copy-start | bytes 786436
  33.7 7.9 %collective-permute-start.3 = (bf16[128,128]{1,0:T(8,128)(2,1)S(1)}, bf16[128,128]{1,0:T(8,128)(2,1)S(1)}, u32[]{:S(2)}, u32[]{:S(2)}) collective-permute-start(bf16[128,128]{1,0:T(8,128)(2,1)S(1)} %get-tuple-element.22), channel_id=1, source_target_pairs={{1,2},{3,4},{5,6},{2,1},{4,3},{6,5},{9,10},{11,12},{13,14},{10,9},... | collective-permute-start | bytes 98312 | tf_op jit(solution)/shard_map/ppermute | solution.py:297
  36.8 4.8 %collective-permute-start.2 = (bf16[128,128]{1,0:T(8,128)(2,1)S(1)}, bf16[128,128]{1,0:T(8,128)(2,1)S(1)}, u32[]{:S(2)}, u32[]{:S(2)}) collective-permute-start(bf16[128,128]{1,0:T(8,128)(2,1)S(1)} %get-tuple-element.22), channel_id=1, source_target_pairs={{0,1},{1,0},{2,3},{3,2},{4,5},{5,4},{6,7},{7,6},{8,9},{9,8},{10,11... | collective-permute-start | bytes 98312 | tf_op jit(solution)/shard_map/ppermute | solution.py:297
  64.7 1.3 %collective-permute-start.4 = (f16[4,4,8,128]{3,2,1,0:T(8,128)(2,1)S(1)}, f16[4,4,8,128]{3,2,1,0:T(8,128)(2,1)S(1)}, u32[]{:S(2)}, u32[]{:S(2)}) collective-permute-start(f16[4,4,8,128]{3,2,1,0:T(8,128)(2,1)S(1)} %get-tuple-element.43), channel_id=1, source_target_pairs={{0,8},{8,0},{16,24},{24,16},{32,40},{40,32},{48,56},{56,48},{64,72... | collective-permute-start | bytes 98312 | tf_op jit(solution)/shard_map/ppermute | solution.py:341
  66.1 5.3 %collective-permute-start.5 = (f16[4,4,8,128]{3,2,1,0:T(8,128)(2,1)S(1)}, f16[4,4,8,128]{3,2,1,0:T(8,128)(2,1)S(1)}, u32[]{:S(2)}, u32[]{:S(2)}) collective-permute-start(f16[4,4,8,128]{3,2,1,0:T(8,128)(2,1)S(1)} %get-tuple-element.41), channel_id=1, source_target_pairs={{0,16},{8,24},{16,0},{24,8},{32,48},{40,56},{48,32},{56,40},{64,80... | collective-permute-start | bytes 98312 | tf_op jit(solution)/shard_map/ppermute | solution.py:341
  71.5 7.3 %collective-permute-start.6 = (f16[4,4,8,128]{3,2,1,0:T(8,128)(2,1)S(1)}, f16[4,4,8,128]{3,2,1,0:T(8,128)(2,1)S(1)}, u32[]{:S(2)}, u32[]{:S(2)}) collective-permute-start(f16[4,4,8,128]{3,2,1,0:T(8,128)(2,1)S(1)} %get-tuple-element.39), channel_id=1, source_target_pairs={{0,48},{8,56},{16,32},{24,40},{32,16},{40,24},{48,0},{56,8},{64,11... | collective-permute-start | bytes 98312 | tf_op jit(solution)/shard_map/ppermute | solution.py:341
  78.9 4.0 %collective-permute-start.7 = (f16[4,4,8,128]{3,2,1,0:T(8,128)(2,1)S(1)}, f16[4,4,8,128]{3,2,1,0:T(8,128)(2,1)S(1)}, u32[]{:S(2)}, u32[]{:S(2)}) collective-permute-start(f16[4,4,8,128]{3,2,1,0:T(8,128)(2,1)S(1)} %get-tuple-element.37), channel_id=1, source_target_pairs={{0,64},{8,72},{16,80},{24,88},{32,96},{40,104},{48,112},{56,120},{... | collective-permute-start | bytes 98312 | tf_op jit(solution)/shard_map/ppermute | solution.py:341
  83.0 5.2 %collective-permute-start.8 = (f16[4,4,8,128]{3,2,1,0:T(8,128)(2,1)S(1)}, f16[4,4,8,128]{3,2,1,0:T(8,128)(2,1)S(1)}, u32[]{:S(2)}, u32[]{:S(2)}) collective-permute-start(f16[4,4,8,128]{3,2,1,0:T(8,128)(2,1)S(1)} %add_convert_fusion), channel_id=1, source_target_pairs={{0,192},{8,200},{16,208},{24,216},{32,224},{40,232},{48,240},{56,2... | collective-permute-start | bytes 98312 | tf_op jit(solution)/shard_map/ppermute | solution.py:341

commit v5 on v4

--- a/solution.py
+++ b/solution.py
@@ -48,7 +48,7 @@
 
 def fine_step(
     where_ref, own_ref, first_ref, second_ref, kind_ref, kind_first_ref, kind_second_ref,
-    enc_ref, in_ref, out_ref, bias_ref, gain_ref, dec_ref,
+    enc_ref, self_ref, neigh_ref, out_ref, bias_ref, gain_ref, dec_ref,
     state_ref, send_ref,
     hidden_ref, norm_ref, enter_ref,
 ):
@@ -126,37 +126,41 @@
         slot = layer % 2
         loaded = {}
 
-        def read(dx, z, start):
-            if (dx, z, start) not in loaded:
-                loaded[dx, z, start] = norm_ref[slot, x + dx, z, group(start), :]
-            return loaded[dx, z, start]
+        def read(dx, z, start, own=None):
+            loaded_key = (dx, z, start, own)
+            if loaded_key not in loaded:
+                loaded[loaded_key] = norm_ref[slot, x + dx, z, group(start), :]
+            return loaded[loaded_key]
 
         rows = []
-        for start in range(1, GROUPS + 1):
-            for d, z in tiles:
-                along_x = read(d - 1, z, start) + read(d + 1, z, start)
-                along_y = read(d, z, start - 1) + read(d, z, start + 1)
-                beside = [read(d, w, start) for w in (z - 1, z + 1) if 0 <= w < NZ]
+        for d, z in tiles:
+            for start in range(1, GROUPS + 1):
+                key = (d, z)
+                mid = read(d, z, start, key)
+                along_x = read(d - 1, z, start, (key, 1)) + read(d + 1, z, start, (key, 1))
+                along_y = read(d, z, start - 1, key) + read(d, z, start + 1, key)
+                beside = [read(d, w, start, (key, 2)) for w in (z - 1, z + 1) if 0 <= w < NZ]
                 along_z = functools.reduce(lambda a, b: a + b, beside)
-                rows.append(jnp.concatenate([read(d, z, start), along_x + along_y + along_z], axis=-1))
+                rows.append(jnp.concatenate([mid, along_x + along_y + along_z], axis=-1))
         return jnp.concatenate(rows, axis=0)
 
     def turn(_, pairs):
         newest, second, third = pairs
         half = enter_ref[...]
         message = half * jnp.tanh(half) + half
-        moved = dot(message, out_ref[second[0]])
-        entered = dot(gather(*newest), in_ref[newest[0]])
-        enter_ref[...] = (entered + bias_ref[newest[0]]).astype(BF16)
+        moved = dot(jnp.concatenate([message, message], axis=-1), out_ref[second[0]])
+        enter = jnp.concatenate([self_ref[newest[0]], neigh_ref[newest[0]]], axis=0)
+        entered = dot(gather(*newest), enter)
+        entered = (entered + bias_ref[newest[0]]).astype(BF16)
+        for at, (d, z) in enumerate(tiles):
+            enter_ref[z * NY : (z + 1) * NY, d * HID : (d + 1) * HID] = entered[at * NY : (at + 1) * NY]
         outside = jnp.logical_and(at_right, third[1] + 1 == 2 * BLOCK)
         slot = (third[0] + 1) % 2
         for d, z in tiles:
             row = third[1] if d == 0 else jnp.where(outside, SPARE, third[1] + 1)
             normalize(third[0] + 1, hidden_ref[third[1] + d, z], norm_ref.at[slot, row, z])
-        for start in range(GROUPS):
-            for at, (d, z) in enumerate(tiles):
-                part = moved[group(start * len(tiles) + at)]
-                hidden_ref[second[1] + d, z, group(start), :] += part
+        for d, z in tiles:
+            hidden_ref[second[1] + d, z] += moved[z * NY : (z + 1) * NY, d * HID : (d + 1) * HID]
         layer, x = newest
         ends = x + 2 >= rows_of(layer)[1]
         next_layer = jnp.where(ends, layer + 1, layer)
@@ -199,12 +203,12 @@
             jax.ShapeDtypeStruct((CHAN, NZ, BLOCK, NY), F32),
             jax.ShapeDtypeStruct((CHAN * NZ * BLOCK, NY), BF16),
         ),
-        in_specs=[pl.BlockSpec(memory_space=pltpu.SMEM)] + [vmem] * 12,
+        in_specs=[pl.BlockSpec(memory_space=pltpu.SMEM)] + [vmem] * 13,
         out_specs=(vmem, vmem),
         scratch_shapes=[
             pltpu.VMEM((HELD, NZ, NY, HID), F32),
             pltpu.VMEM((2, HELD, NZ, PADDED, HID), BF16),
-            pltpu.VMEM((2 * NZ * NY, HID), BF16),
+            pltpu.VMEM((NZ * NY, 2 * HID), BF16),
         ],
         compiler_params=pltpu.CompilerParams(vmem_limit_bytes=40 * 2**20),
         cost_estimate=pl.CostEstimate(flops=10**10, bytes_accessed=2**21, transcendentals=10**7),
@@ -221,14 +225,19 @@
     return high, (value - high.astype(F32)).astype(BF16)
 
 
+def twice(block, none):
+    upper = jnp.concatenate([block, none], axis=1)
+    return jnp.concatenate([upper, jnp.concatenate([none, block], axis=1)], axis=0)
+
+
 def prepare(
     plan_ref, rate_ref,
-    enc_hbm, type_hbm, force_hbm, gain_hbm, self_hbm, neigh_hbm, out_hbm, bias_hbm, dec_gain_hbm, dec_hbm,
-    enc_first_ref, enc_second_ref, in_ref, leave_ref, bias_ref, gains_ref, dec_out_ref,
-    enc, kind, force, gain, own, neigh, out, bias, dec_gain, dec, sems,
+    enc_hbm, type_hbm, force_hbm, gain_hbm, out_hbm, bias_hbm, dec_gain_hbm, dec_hbm,
+    enc_first_ref, enc_second_ref, leave_ref, bias_ref, gains_ref, dec_out_ref,
+    enc, kind, force, gain, out, bias, dec_gain, dec, sems,
 ):
-    sources = (enc_hbm, type_hbm, force_hbm, gain_hbm, self_hbm, neigh_hbm, out_hbm, bias_hbm, dec_gain_hbm, dec_hbm)
-    targets = (enc, kind, force, gain, own, neigh, out, bias, dec_gain, dec)
+    sources = (enc_hbm, type_hbm, force_hbm, gain_hbm, out_hbm, bias_hbm, dec_gain_hbm, dec_hbm)
+    targets = (enc, kind, force, gain, out, bias, dec_gain, dec)
     copies = [pltpu.make_async_copy(a, b, sems.at[n]) for n, (a, b) in enumerate(zip(sources, targets))]
     for copy in copies:
         copy.start()
@@ -252,12 +261,11 @@
         for x in range(BLOCK):
             enc_ref[:, x * HID : (x + 1) * HID] = jnp.concatenate(spread(rows, x), axis=0).astype(BF16)
     for layer in range(LAYERS):
-        half = jnp.asarray(0.5, BF16)
-        in_ref[layer, :HID, :] = own[layer] * half
-        in_ref[layer, HID:, :] = neigh[layer] * half
-        leave_ref[layer] = centred(out[layer].astype(F32)).astype(BF16)
+        none = jnp.zeros((HID, HID), BF16)
+        high, low = halves(centred(out[layer].astype(F32)))
+        leave_ref[layer] = jnp.concatenate([twice(high, none), twice(low, none)], axis=0)
         bias_ref[layer] = bias[layer : layer + 1, :] * 0.5
-        gains_ref[layer] = gain[layer : layer + 1, :] * HID**0.5
+        gains_ref[layer] = gain[layer : layer + 1, :] * (0.5 * HID**0.5)
     gains_ref[LAYERS] = dec_gain[...] * HID**0.5
     rows = [dec[...].astype(F32)[c : c + 1] for c in range(CHAN)]
     for x in range(BLOCK):
@@ -271,8 +279,7 @@
     shapes = (
         ((FEATURES * BLOCK, BLOCK * HID), BF16),
         ((FEATURES * BLOCK, BLOCK * HID), BF16),
-        ((LAYERS, 2 * HID, HID), BF16),
-        ((LAYERS, HID, HID), BF16),
+        ((LAYERS, 4 * HID, 2 * HID), BF16),
         ((LAYERS, 1, HID), F32),
         ((LAYERS + 1, 1, HID), F32),
         ((BLOCK // 2, CHAN * BLOCK, 2 * HID), BF16),
@@ -314,18 +321,19 @@
     where = jnp.stack([position, lax.axis_size("space") - 1]).astype(jnp.int32)
 
     outgoing = jnp.concatenate(
-        [own.reshape(ROWS, NY).astype(BF16), cell_type.reshape(NZ * BLOCK, NY).astype(BF16)], axis=0
-    )
+        [own.reshape(ROWS, NY), cell_type.astype(F32).reshape(NZ * BLOCK, NY)], axis=0
+    ).astype(BF16)
     kinds = sides = exchange(outgoing)
     enc_first, enc_second, *weights = run_prepare(
-        plan, rate_values, enc_weight, type_table, force_vector[None], norm_gain, self_weight,
-        neigh_weight, out_weight, layer_bias, dec_gain[None], dec_weight,
+        plan, rate_values, enc_weight, type_table, force_vector[None], norm_gain,
+        out_weight, layer_bias, dec_gain[None], dec_weight,
     )
 
     state = own
     for step_index in range(STEPS):
         state, outgoing = run_fine_step(
-            where, state, *sides, cell_type, *kinds, (enc_first, enc_second)[step_index], *weights
+            where, state, *sides, cell_type, *kinds, (enc_first, enc_second)[step_index],
+            self_weight, neigh_weight, *weights,
         )
         if step_index + 1 < STEPS:
             sides = exchange(outgoing)

time: 89.3 us -> 99.7 us (1.12)
  local copies, waits for them, and re-layouts: 2.54 us -> 10.4 us
  Pallas kernels: 47.3 us -> 48.8 us
    unnamed x30 -> x36, local copies, waits for them, and re-layouts: 2.54 us -> 10.4 us
    pallas_call x2, Pallas kernels: 45.6 us -> 47.7 us  [run_fine_step(): pl.pallas_call(fine_step, out_shape=(jax.ShapeDtypeStruct((CHAN, NZ, BLOC...]
    ppermute x2, starting transfers between devices: 1 us -> 2.63 us  [exchange(): lax.ppermute(value, 'space', first)]
    convert_element_type x2 -> x0, other arithmetic: 1.61 us -> none  [the longest x1 0.85 us: per_device(): own.reshape(ROWS, NY).astype(BF16)]
  transfers between devices with their start and end apart: 9 -> 9, of which waited for: 6 -> 6; matrix products, arithmetic and copies ran while one was open for 1% -> 0% of each run, Pallas kernels for 2% -> 1%
where the time goes in v5:
time: 99.7 us; the launch traced here: 99.1 us
  Pallas kernels  48.8 us (49%)
  starting transfers between devices  19 us (19%)
  waiting for transfers between devices  17.3 us (17%)
  local copies, waits for them, and re-layouts  10.4 us (10%)
  other arithmetic  3.29 us (3%)
    pallas_call x2, Pallas kernels, run_fine_step(): pl.pallas_call(fine_step, out_shape=(jax.ShapeDtypeStruct((CHAN, NZ, BLOC...  47.7 us
    ppermute x5, waiting for transfers between devices, per_device(): came = lax.ppermute(total.astype(jnp.float16), 'tm', partners).astype(F32)  12.6 us
    unnamed x36, local copies, waits for them, and re-layouts  10.4 us
    ppermute x5, starting transfers between devices, per_device(): came = lax.ppermute(total.astype(jnp.float16), 'tm', partners).astype(F32)  9.74 us
    ppermute x2, starting transfers between devices, exchange(): lax.ppermute(value, 'space', second)  6.66 us
    ppermute x2, waiting for transfers between devices, exchange(): lax.ppermute(value, 'space', second)  4.71 us
    ppermute x2, starting transfers between devices, exchange(): lax.ppermute(value, 'space', first)  2.63 us
  transfers between devices with their start and end apart: 9, of which 6 were waited for; matrix products, arithmetic and copies ran while one was open for 0% of the time, Pallas kernels for 1%

profile of v5, /device:TPU:56, one launch (start us, length us, event | category | flops | bytes accessed | tf_op | source)
XLA Modules:
  0.0 99.1 jit_solution(1657811882400087278)
XLA Ops:
  0.0 0.8 convert.8
  0.8 0.7 fusion
  1.6 1.5 %collective-permute-start = (bf16[160,128]{1,0:T(8,128)(2,1)S(1)}, bf16[160,128]{1,0:T(8,128)(2,1)S(1)}, u32[]{:S(2)}, u32[]{:S(2)}) collective-permute-start(bf16[160,128]{1,0:T(8,128)(2,1)S(1)} %pad_maximum_fusion), channel_id=1, source_target_pairs={{0,1},{1,0},{2,3},{3,2},{4,5},{5,4},{6,7},{7,6},{8,9},{9,8},{10,11... | collective-permute-start | bytes 122888 | tf_op jit(solution)/shard_map/ppermute | solution.py:304
  3.1 3.5 %collective-permute-start.1 = (bf16[160,128]{1,0:T(8,128)(2,1)S(1)}, bf16[160,128]{1,0:T(8,128)(2,1)S(1)}, u32[]{:S(2)}, u32[]{:S(2)}) collective-permute-start(bf16[160,128]{1,0:T(8,128)(2,1)S(1)} %pad_maximum_fusion), channel_id=1, source_target_pairs={{1,2},{3,4},{5,6},{2,1},{4,3},{6,5},{9,10},{11,12},{13,14},{10,9},... | collective-permute-start | bytes 122888 | tf_op jit(solution)/shard_map/ppermute | solution.py:304
  6.7 0.9 copy-done.3
  7.6 0.7 copy-done.8
  8.3 0.7 copy-done.9
  9.0 0.7 copy-done.10
  9.7 0.7 copy-done.11
  10.4 0.7 copy-done.12
  11.7 0.7 copy-done.14
  12.3 0.7 copy-done.15
  13.0 0.7 copy-done.16
  13.7 1.2 %prepare.1 = (bf16[112,1024]{1,0:T(8,128)(2,1)S(1)}, bf16[112,1024]{1,0:T(8,128)(2,1)S(1)}, bf16[6,512,256]{2,1,0:T(8,128)(2,1)S(1)}, f32[6,1,128]{2,1,0:T(1,128...) custom-call(s32[1,2]{1,0:T(1,128)S(1)} %copy-done.13, f32[8]{0:T(128)S(1)} %copy-done.14, ...), custom_call_target="tpu_custom_call" | custom-call | flops 100000000 | bytes 2097152 | tf_op jit(solution)/shard_map/prepare/pallas_call | solution.py:287
  14.9 0.8 copy-done
  15.7 0.7 copy-done.1
  16.4 0.9 copy-done.4
  17.3 0.9 copy-done.6
  18.3 23.3 %fine_step.2 = (f32[4,4,8,128]{3,2,1,0:T(8,128)S(1)}, bf16[128,128]{1,0:T(8,128)(2,1)S(1)}) custom-call(s32[2]{0:T(128)S(1)} %pad_add_fusion.where_ref, f32[4,4,8,128]{3,2,1,0:T(8,128)S(1)} %bitcast.9, bf16[160,128]{1,0:T(8,128)(2,1)S(1)} %collective-permute-done.first_ref.kind_first_ref, ...), custom_call_target="tpu_custom_call" | custom-call | flops 10000000000 | bytes 2097152 | tf_op jit(solution)/shard_map/fine_step/pallas_call | solution.py:200
  41.6 1.1 %collective-permute-start.2 = (bf16[128,128]{1,0:T(8,128)(2,1)S(1)}, bf16[128,128]{1,0:T(8,128)(2,1)S(1)}, u32[]{:S(2)}, u32[]{:S(2)}) collective-permute-start(bf16[128,128]{1,0:T(8,128)(2,1)S(1)} %get-tuple-element.20), channel_id=1, source_target_pairs={{0,1},{1,0},{2,3},{3,2},{4,5},{5,4},{6,7},{7,6},{8,9},{9,8},{10,11... | collective-permute-start | bytes 98312 | tf_op jit(solution)/shard_map/ppermute | solution.py:304
  42.7 3.1 %collective-permute-start.3 = (bf16[128,128]{1,0:T(8,128)(2,1)S(1)}, bf16[128,128]{1,0:T(8,128)(2,1)S(1)}, u32[]{:S(2)}, u32[]{:S(2)}) collective-permute-start(bf16[128,128]{1,0:T(8,128)(2,1)S(1)} %get-tuple-element.20), channel_id=1, source_target_pairs={{1,2},{3,4},{5,6},{2,1},{4,3},{6,5},{9,10},{11,12},{13,14},{10,9},... | collective-permute-start | bytes 98312 | tf_op jit(solution)/shard_map/ppermute | solution.py:304
  45.9 4.7 %collective-permute-done.3.second_ref = bf16[128,128]{1,0:T(8,128)(2,1)S(1)} collective-permute-done((bf16[128,128]{1,0:T(8,128)(2,1)S(1)}, bf16[128,128]{1,0:T(8,128)(2,1)S(1)}, u32[]{:S(2)}, u32[]{:S(2)}) %collective-permute-start.3) | collective-permute-done | bytes 32800 | tf_op jit(solution)/shard_map/ppermute | solution.py:304
  50.7 24.3 %fine_step.3 = (f32[4,4,8,128]{3,2,1,0:T(8,128)S(1)}, bf16[128,128]{1,0:T(8,128)(2,1)}) custom-call(s32[2]{0:T(128)S(1)} %pad_add_fusion.where_ref, f32[4,4,8,128]{3,2,1,0:T(8,128)S(1)} %get-tuple-element.19.own_ref, bf16[128,128]{1,0:T(8,128)(2,1)S(1)} %collective-permute-done.2.first_ref, bf16[128,128]{1,0:T(8,128)(2,1)S(1)} %collective-permute-done.3.second_ref, ...), custom_call_target="tpu_custom_call" | custom-call | flops 10000000000 | bytes 2097152 | tf_op jit(solution)/shard_map/fine_step/pallas_call | solution.py:200
  75.1 1.2 %collective-permute-done.4 = f16[4,4,8,128]{3,2,1,0:T(8,128)(2,1)S(1)} collective-permute-done((f16[4,4,8,128]{3,2,1,0:T(8,128)(2,1)S(1)}, f16[4,4,8,128]{3,2,1,0:T(8,128)(2,1)S(1)}, u32[]{:S(2)}, u32[]{:S(2)}) %collective-permute-start.4) | collective-permute-done | bytes 32800 | tf_op jit(solution)/shard_map/ppermute | solution.py:349
  76.4 3.4 %collective-permute-start.5 = (f16[4,4,8,128]{3,2,1,0:T(8,128)(2,1)S(1)}, f16[4,4,8,128]{3,2,1,0:T(8,128)(2,1)S(1)}, u32[]{:S(2)}, u32[]{:S(2)}) collective-permute-start(f16[4,4,8,128]{3,2,1,0:T(8,128)(2,1)S(1)} %get-tuple-element.39), channel_id=1, source_target_pairs={{0,16},{8,24},{16,0},{24,8},{32,48},{40,56},{48,32},{56,40},{64,80... | collective-permute-start | bytes 98312 | tf_op jit(solution)/shard_map/ppermute | solution.py:349
  80.0 1.7 %collective-permute-done.5 = f16[4,4,8,128]{3,2,1,0:T(8,128)(2,1)S(1)} collective-permute-done((f16[4,4,8,128]{3,2,1,0:T(8,128)(2,1)S(1)}, f16[4,4,8,128]{3,2,1,0:T(8,128)(2,1)S(1)}, u32[]{:S(2)}, u32[]{:S(2)}) %collective-permute-start.5) | collective-permute-done | bytes 32800 | tf_op jit(solution)/shard_map/ppermute | solution.py:349
  81.8 5.1 %collective-permute-start.6 = (f16[4,4,8,128]{3,2,1,0:T(8,128)(2,1)S(1)}, f16[4,4,8,128]{3,2,1,0:T(8,128)(2,1)S(1)}, u32[]{:S(2)}, u32[]{:S(2)}) collective-permute-start(f16[4,4,8,128]{3,2,1,0:T(8,128)(2,1)S(1)} %get-tuple-element.37), channel_id=1, source_target_pairs={{0,48},{8,56},{16,32},{24,40},{32,16},{40,24},{48,0},{56,8},{64,11... | collective-permute-start | bytes 98312 | tf_op jit(solution)/shard_map/ppermute | solution.py:349
  87.1 1.7 %collective-permute-done.6 = f16[4,4,8,128]{3,2,1,0:T(8,128)(2,1)S(1)} collective-permute-done((f16[4,4,8,128]{3,2,1,0:T(8,128)(2,1)S(1)}, f16[4,4,8,128]{3,2,1,0:T(8,128)(2,1)S(1)}, u32[]{:S(2)}, u32[]{:S(2)}) %collective-permute-start.6) | collective-permute-done | bytes 32800 | tf_op jit(solution)/shard_map/ppermute | solution.py:349
  89.1 0.8 collective-permute-start.7
  90.0 3.1 %collective-permute-done.7 = f16[4,4,8,128]{3,2,1,0:T(8,128)(2,1)S(1)} collective-permute-done((f16[4,4,8,128]{3,2,1,0:T(8,128)(2,1)S(1)}, f16[4,4,8,128]{3,2,1,0:T(8,128)(2,1)S(1)}, u32[]{:S(2)}, u32[]{:S(2)}) %collective-permute-start.7) | collective-permute-done | bytes 32800 | tf_op jit(solution)/shard_map/ppermute | solution.py:349
  93.6 4.8 %collective-permute-done.8 = f16[4,4,8,128]{3,2,1,0:T(8,128)(2,1)S(1)} collective-permute-done((f16[4,4,8,128]{3,2,1,0:T(8,128)(2,1)S(1)}, f16[4,4,8,128]{3,2,1,0:T(8,128)(2,1)S(1)}, u32[]{:S(2)}, u32[]{:S(2)}) %collective-permute-start.8) | collective-permute-done | bytes 32800 | tf_op jit(solution)/shard_map/ppermute | solution.py:349
  98.5 0.7 add_bitcast_fusion
  (56 shorter events, 2.2 us)
Async XLA Ops:
  1.6 13.3 %collective-permute-start = (bf16[160,128]{1,0:T(8,128)(2,1)S(1)}, bf16[160,128]{1,0:T(8,128)(2,1)S(1)}, u32[]{:S(2)}, u32[]{:S(2)}) collective-permute-start(bf16[160,128]{1,0:T(8,128)(2,1)S(1)} %pad_maximum_fusion), channel_id=1, source_target_pairs={{0,1},{1,0},{2,3},{3,2},{4,5},{5,4},{6,7},{7,6},{8,9},{9,8},{10,11... | collective-permute-start | bytes 122888 | tf_op jit(solution)/shard_map/ppermute | solution.py:304
  3.1 11.8 %collective-permute-start.1 = (bf16[160,128]{1,0:T(8,128)(2,1)S(1)}, bf16[160,128]{1,0:T(8,128)(2,1)S(1)}, u32[]{:S(2)}, u32[]{:S(2)}) collective-permute-start(bf16[160,128]{1,0:T(8,128)(2,1)S(1)} %pad_maximum_fusion), channel_id=1, source_target_pairs={{1,2},{3,4},{5,6},{2,1},{4,3},{6,5},{9,10},{11,12},{13,14},{10,9},... | collective-permute-start | bytes 122888 | tf_op jit(solution)/shard_map/ppermute | solution.py:304
  6.7 0.9 copy-start.3
  7.6 0.7 copy-start.8
  8.3 0.7 copy-start.9
  9.0 0.7 copy-start.10
  9.7 0.7 copy-start.11
  10.4 0.7 copy-start.12
  11.0 0.7 copy-start.13
  11.7 0.7 copy-start.14
  12.3 0.7 copy-start.15
  13.0 0.7 copy-start.16
  14.8 0.8 copy-start
  15.7 0.7 copy-start.1
  16.4 0.9 copy-start.4
  17.3 0.9 copy-start.6
  18.3 27.6 %copy-start.17 = (f32[4,4,4,8,128]{4,3,2,1,0:T(8,128)S(1)}, f32[4,4,4,8,128]{4,3,2,1,0:T(8,128)}, u32[]{:S(2)}) copy-start(f32[4,4,4,8,128]{4,3,2,1,0:T(8,128)} %param.18) | copy-start | bytes 786436
  18.3 32.4 %copy-start.2 = (s32[4,8,128]{2,1,0:T(8,128)S(1)}, s32[4,8,128]{2,1,0:T(8,128)}, u32[]{:S(2)}) copy-start(s32[4,8,128]{2,1,0:T(8,128)} %kind_ref.3) | copy-start | bytes 49156
  18.3 32.4 %copy-start.5 = (bf16[6,128,128]{2,1,0:T(8,128)(2,1)S(1)}, bf16[6,128,128]{2,1,0:T(8,128)(2,1)}, u32[]{:S(2)}) copy-start(bf16[6,128,128]{2,1,0:T(8,128)(2,1)} %self_ref.3) | copy-start | bytes 589828
  18.3 32.4 %copy-start.7 = (bf16[6,128,128]{2,1,0:T(8,128)(2,1)S(1)}, bf16[6,128,128]{2,1,0:T(8,128)(2,1)}, u32[]{:S(2)}) copy-start(bf16[6,128,128]{2,1,0:T(8,128)(2,1)} %neigh_ref.3) | copy-start | bytes 589828
  41.6 4.3 %collective-permute-start.2 = (bf16[128,128]{1,0:T(8,128)(2,1)S(1)}, bf16[128,128]{1,0:T(8,128)(2,1)S(1)}, u32[]{:S(2)}, u32[]{:S(2)}) collective-permute-start(bf16[128,128]{1,0:T(8,128)(2,1)S(1)} %get-tuple-element.20), channel_id=1, source_target_pairs={{0,1},{1,0},{2,3},{3,2},{4,5},{5,4},{6,7},{7,6},{8,9},{9,8},{10,11... | collective-permute-start | bytes 98312 | tf_op jit(solution)/shard_map/ppermute | solution.py:304
  42.7 7.9 %collective-permute-start.3 = (bf16[128,128]{1,0:T(8,128)(2,1)S(1)}, bf16[128,128]{1,0:T(8,128)(2,1)S(1)}, u32[]{:S(2)}, u32[]{:S(2)}) collective-permute-start(bf16[128,128]{1,0:T(8,128)(2,1)S(1)} %get-tuple-element.20), channel_id=1, source_target_pairs={{1,2},{3,4},{5,6},{2,1},{4,3},{6,5},{9,10},{11,12},{13,14},{10,9},... | collective-permute-start | bytes 98312 | tf_op jit(solution)/shard_map/ppermute | solution.py:304
  75.0 1.3 %collective-permute-start.4 = (f16[4,4,8,128]{3,2,1,0:T(8,128)(2,1)S(1)}, f16[4,4,8,128]{3,2,1,0:T(8,128)(2,1)S(1)}, u32[]{:S(2)}, u32[]{:S(2)}) collective-permute-start(f16[4,4,8,128]{3,2,1,0:T(8,128)(2,1)S(1)} %get-tuple-element.41), channel_id=1, source_target_pairs={{0,8},{8,0},{16,24},{24,16},{32,40},{40,32},{48,56},{56,48},{64,72... | collective-permute-start | bytes 98312 | tf_op jit(solution)/shard_map/ppermute | solution.py:349
  76.4 5.3 %collective-permute-start.5 = (f16[4,4,8,128]{3,2,1,0:T(8,128)(2,1)S(1)}, f16[4,4,8,128]{3,2,1,0:T(8,128)(2,1)S(1)}, u32[]{:S(2)}, u32[]{:S(2)}) collective-permute-start(f16[4,4,8,128]{3,2,1,0:T(8,128)(2,1)S(1)} %get-tuple-element.39), channel_id=1, source_target_pairs={{0,16},{8,24},{16,0},{24,8},{32,48},{40,56},{48,32},{56,40},{64,80... | collective-permute-start | bytes 98312 | tf_op jit(solution)/shard_map/ppermute | solution.py:349
  81.8 7.0 %collective-permute-start.6 = (f16[4,4,8,128]{3,2,1,0:T(8,128)(2,1)S(1)}, f16[4,4,8,128]{3,2,1,0:T(8,128)(2,1)S(1)}, u32[]{:S(2)}, u32[]{:S(2)}) collective-permute-start(f16[4,4,8,128]{3,2,1,0:T(8,128)(2,1)S(1)} %get-tuple-element.37), channel_id=1, source_target_pairs={{0,48},{8,56},{16,32},{24,40},{32,16},{40,24},{48,0},{56,8},{64,11... | collective-permute-start | bytes 98312 | tf_op jit(solution)/shard_map/ppermute | solution.py:349
  89.1 4.0 %collective-permute-start.7 = (f16[4,4,8,128]{3,2,1,0:T(8,128)(2,1)S(1)}, f16[4,4,8,128]{3,2,1,0:T(8,128)(2,1)S(1)}, u32[]{:S(2)}, u32[]{:S(2)}) collective-permute-start(f16[4,4,8,128]{3,2,1,0:T(8,128)(2,1)S(1)} %get-tuple-element.35), channel_id=1, source_target_pairs={{0,64},{8,72},{16,80},{24,88},{32,96},{40,104},{48,112},{56,120},{... | collective-permute-start | bytes 98312 | tf_op jit(solution)/shard_map/ppermute | solution.py:349
  93.2 5.2 %collective-permute-start.8 = (f16[4,4,8,128]{3,2,1,0:T(8,128)(2,1)S(1)}, f16[4,4,8,128]{3,2,1,0:T(8,128)(2,1)S(1)}, u32[]{:S(2)}, u32[]{:S(2)}) collective-permute-start(f16[4,4,8,128]{3,2,1,0:T(8,128)(2,1)S(1)} %add_convert_fusion), channel_id=1, source_target_pairs={{0,192},{8,200},{16,208},{24,216},{32,224},{40,232},{48,240},{56,2... | collective-permute-start | bytes 98312 | tf_op jit(solution)/shard_map/ppermute | solution.py:349

commit v6 on v5

--- a/solution.py
+++ b/solution.py
@@ -38,6 +38,12 @@
 
 def dot_nt(a, b):
     return lax.dot_general(a, b, (((1,), (1,)), ((), ())), preferred_element_type=F32)
+
+
+def twice(block):
+    none = jnp.zeros_like(block)
+    upper = jnp.concatenate([block, none], axis=1)
+    return jnp.concatenate([upper, jnp.concatenate([none, block], axis=1)], axis=0)
 
 
 def grouped(dtype):
@@ -148,7 +154,10 @@
         newest, second, third = pairs
         half = enter_ref[...]
         message = half * jnp.tanh(half) + half
-        moved = dot(jnp.concatenate([message, message], axis=-1), out_ref[second[0]])
+        leave = jnp.concatenate(
+            [twice(out_ref[second[0], :HID]), twice(out_ref[second[0], HID:])], axis=0
+        )
+        moved = dot(jnp.concatenate([message, message], axis=-1), leave)
         enter = jnp.concatenate([self_ref[newest[0]], neigh_ref[newest[0]]], axis=0)
         entered = dot(gather(*newest), enter)
         entered = (entered + bias_ref[newest[0]]).astype(BF16)
@@ -210,7 +219,7 @@
             pltpu.VMEM((2, HELD, NZ, PADDED, HID), BF16),
             pltpu.VMEM((NZ * NY, 2 * HID), BF16),
         ],
-        compiler_params=pltpu.CompilerParams(vmem_limit_bytes=40 * 2**20),
+        compiler_params=pltpu.CompilerParams(vmem_limit_bytes=26 * 2**20),
         cost_estimate=pl.CostEstimate(flops=10**10, bytes_accessed=2**21, transcendentals=10**7),
         name="fine_step",
     )(*args)
@@ -223,11 +232,6 @@
 def halves(value):
     high = value.astype(BF16)
     return high, (value - high.astype(F32)).astype(BF16)
-
-
-def twice(block, none):
-    upper = jnp.concatenate([block, none], axis=1)
-    return jnp.concatenate([upper, jnp.concatenate([none, block], axis=1)], axis=0)
 
 
 def prepare(
@@ -261,9 +265,9 @@
         for x in range(BLOCK):
             enc_ref[:, x * HID : (x + 1) * HID] = jnp.concatenate(spread(rows, x), axis=0).astype(BF16)
     for layer in range(LAYERS):
-        none = jnp.zeros((HID, HID), BF16)
         high, low = halves(centred(out[layer].astype(F32)))
-        leave_ref[layer] = jnp.concatenate([twice(high, none), twice(low, none)], axis=0)
+        leave_ref[layer, :HID, :] = high
+        leave_ref[layer, HID:, :] = low
         bias_ref[layer] = bias[layer : layer + 1, :] * 0.5
         gains_ref[layer] = gain[layer : layer + 1, :] * (0.5 * HID**0.5)
     gains_ref[LAYERS] = dec_gain[...] * HID**0.5
@@ -279,7 +283,7 @@
     shapes = (
         ((FEATURES * BLOCK, BLOCK * HID), BF16),
         ((FEATURES * BLOCK, BLOCK * HID), BF16),
-        ((LAYERS, 4 * HID, 2 * HID), BF16),
+        ((LAYERS, 2 * HID, HID), BF16),
         ((LAYERS, 1, HID), F32),
         ((LAYERS + 1, 1, HID), F32),
         ((BLOCK // 2, CHAN * BLOCK, 2 * HID), BF16),
@@ -291,7 +295,7 @@
         out_specs=(vmem,) * len(shapes),
         scratch_shapes=[pltpu.VMEM(array.shape, array.dtype) for array in arrays]
         + [pltpu.SemaphoreType.DMA((len(arrays),))],
-        compiler_params=pltpu.CompilerParams(vmem_limit_bytes=16 * 2**20),
+        compiler_params=pltpu.CompilerParams(vmem_limit_bytes=8 * 2**20),
         cost_estimate=pl.CostEstimate(flops=10**8, bytes_accessed=2**21, transcendentals=0),
         name="prepare",
     )(plan, rate_values, *arrays)

time: 99.7 us -> 90.4 us (0.907)
  local copies, waits for them, and re-layouts: 10.4 us -> 1.57 us
  Pallas kernels: 48.8 us -> 47.4 us
    unnamed x36 -> x30, local copies, waits for them, and re-layouts: 10.4 us -> 1.57 us
    ppermute x2, starting transfers between devices: 2.63 us -> 0.86 us  [exchange(): lax.ppermute(value, 'space', first)]
    ppermute x2, starting transfers between devices: 6.66 us -> 8.13 us  [exchange(): lax.ppermute(value, 'space', second)]
    pallas_call x2, Pallas kernels: 47.7 us -> 46.3 us  [run_fine_step(): pl.pallas_call(fine_step, out_shape=(jax.ShapeDtypeStruct((CHAN, NZ, BLOC...]
  transfers between devices with their start and end apart: 9 -> 9, of which waited for: 6 -> 8; matrix products, arithmetic and copies ran while one was open for 0% -> 1% of each run, Pallas kernels for 1% -> 1%
where the time goes in v6:
time: 90.4 us; the launch traced here: 89.9 us
  Pallas kernels  47.4 us (52%)
  starting transfers between devices  19.4 us (21%)
  waiting for transfers between devices  17.8 us (20%)
  other arithmetic  3.33 us (4%)
  local copies, waits for them, and re-layouts  1.57 us (2%)
    pallas_call x2, Pallas kernels, run_fine_step(): pl.pallas_call(fine_step, out_shape=(jax.ShapeDtypeStruct((CHAN, NZ, BLOC...  46.3 us
    ppermute x5, waiting for transfers between devices, per_device(): came = lax.ppermute(total.astype(jnp.float16), 'tm', partners).astype(F32)  12.5 us
    ppermute x5, starting transfers between devices, per_device(): came = lax.ppermute(total.astype(jnp.float16), 'tm', partners).astype(F32)  10.4 us
    ppermute x2, starting transfers between devices, exchange(): lax.ppermute(value, 'space', second)  8.13 us
    ppermute x2, waiting for transfers between devices, exchange(): lax.ppermute(value, 'space', second)  5 us
  transfers between devices with their start and end apart: 9, of which 8 were waited for; matrix products, arithmetic and copies ran while one was open for 1% of the time, Pallas kernels for 1%

profile of v6, /device:TPU:56, one launch (start us, length us, event | category | flops | bytes accessed | tf_op | source)
XLA Modules:
  0.0 89.9 jit_solution(16085662586964281826)
XLA Ops:
  0.0 0.8 fusion
  0.8 0.8 convert.8
  1.6 4.2 %collective-permute-start.1 = (bf16[160,128]{1,0:T(8,128)(2,1)S(1)}, bf16[160,128]{1,0:T(8,128)(2,1)S(1)}, u32[]{:S(2)}, u32[]{:S(2)}) collective-permute-start(bf16[160,128]{1,0:T(8,128)(2,1)S(1)} %pad_maximum_fusion), channel_id=1, source_target_pairs={{1,2},{3,4},{5,6},{2,1},{4,3},{6,5},{9,10},{11,12},{13,14},{10,9},... | collective-permute-start | bytes 122888 | tf_op jit(solution)/shard_map/ppermute | solution.py:308
  5.9 0.8 collective-permute-start
  6.7 0.1 pad_add_fusion.where_ref
  6.8 0.5 copy-done.5
  7.4 1.1 %prepare.1 = (bf16[112,1024]{1,0:T(8,128)(2,1)S(1)}, bf16[112,1024]{1,0:T(8,128)(2,1)S(1)}, bf16[6,256,128]{2,1,0:T(8,128)(2,1)S(1)}, f32[6,1,128]{2,1,0:T(1,128...) custom-call(s32[1,2]{1,0:T(1,128)S(1)} %copy-done.10, f32[8]{0:T(128)S(1)} %copy-done.11, ...), custom_call_target="tpu_custom_call" | custom-call | flops 100000000 | bytes 2097152 | tf_op jit(solution)/shard_map/prepare/pallas_call | solution.py:291
  8.5 1.2 %collective-permute-done.1.second_ref.kind_second_ref = bf16[160,128]{1,0:T(8,128)(2,1)S(1)} collective-permute-done((bf16[160,128]{1,0:T(8,128)(2,1)S(1)}, bf16[160,128]{1,0:T(8,128)(2,1)S(1)}, u32[]{:S(2)}, u32[]{:S(2)}) %collective-permute-start.1) | collective-permute-done | bytes 40992 | tf_op jit(solution)/shard_map/ppermute | solution.py:308
  9.6 0.3 collective-permute-done.first_ref.kind_first_ref
  10.0 0.9 %copy-done.4 = bf16[6,128,128]{2,1,0:T(8,128)(2,1)S(1)} copy-done((bf16[6,128,128]{2,1,0:T(8,128)(2,1)S(1)}, bf16[6,128,128]{2,1,0:T(8,128)(2,1)}, u32[]{:S(2)}) %copy-start.4) | copy-done | bytes 196632
  10.9 22.9 %fine_step.2 = (f32[4,4,8,128]{3,2,1,0:T(8,128)S(1)}, bf16[128,128]{1,0:T(8,128)(2,1)S(1)}) custom-call(s32[2]{0:T(128)S(1)} %pad_add_fusion.where_ref, f32[4,4,8,128]{3,2,1,0:T(8,128)S(1)} %bitcast.9, bf16[160,128]{1,0:T(8,128)(2,1)S(1)} %collective-permute-done.first_ref.kind_first_ref, ...), custom_call_target="tpu_custom_call" | custom-call | flops 10000000000 | bytes 2097152 | tf_op jit(solution)/shard_map/fine_step/pallas_call | solution.py:209
  33.7 3.9 %collective-permute-start.3 = (bf16[128,128]{1,0:T(8,128)(2,1)S(1)}, bf16[128,128]{1,0:T(8,128)(2,1)S(1)}, u32[]{:S(2)}, u32[]{:S(2)}) collective-permute-start(bf16[128,128]{1,0:T(8,128)(2,1)S(1)} %get-tuple-element.20), channel_id=1, source_target_pairs={{1,2},{3,4},{5,6},{2,1},{4,3},{6,5},{9,10},{11,12},{13,14},{10,9},... | collective-permute-start | bytes 98312 | tf_op jit(solution)/shard_map/ppermute | solution.py:308
  37.7 0.1 collective-permute-start.2
  37.8 3.8 %collective-permute-done.3.second_ref = bf16[128,128]{1,0:T(8,128)(2,1)S(1)} collective-permute-done((bf16[128,128]{1,0:T(8,128)(2,1)S(1)}, bf16[128,128]{1,0:T(8,128)(2,1)S(1)}, u32[]{:S(2)}, u32[]{:S(2)}) %collective-permute-start.3) | collective-permute-done | bytes 32800 | tf_op jit(solution)/shard_map/ppermute | solution.py:308
  41.7 23.5 %fine_step.3 = (f32[4,4,8,128]{3,2,1,0:T(8,128)S(1)}, bf16[128,128]{1,0:T(8,128)(2,1)}) custom-call(s32[2]{0:T(128)S(1)} %pad_add_fusion.where_ref, f32[4,4,8,128]{3,2,1,0:T(8,128)S(1)} %get-tuple-element.19.own_ref, bf16[128,128]{1,0:T(8,128)(2,1)S(1)} %collective-permute-done.2.first_ref, bf16[128,128]{1,0:T(8,128)(2,1)S(1)} %collective-permute-done.3.second_ref, ...), custom_call_target="tpu_custom_call" | custom-call | flops 10000000000 | bytes 2097152 | tf_op jit(solution)/shard_map/fine_step/pallas_call | solution.py:209
  65.2 0.1 collective-permute-start.4
  65.3 1.2 %collective-permute-done.4 = f16[4,4,8,128]{3,2,1,0:T(8,128)(2,1)S(1)} collective-permute-done((f16[4,4,8,128]{3,2,1,0:T(8,128)(2,1)S(1)}, f16[4,4,8,128]{3,2,1,0:T(8,128)(2,1)S(1)}, u32[]{:S(2)}, u32[]{:S(2)}) %collective-permute-start.4) | collective-permute-done | bytes 32800 | tf_op jit(solution)/shard_map/ppermute | solution.py:353
  66.6 3.4 %collective-permute-start.5 = (f16[4,4,8,128]{3,2,1,0:T(8,128)(2,1)S(1)}, f16[4,4,8,128]{3,2,1,0:T(8,128)(2,1)S(1)}, u32[]{:S(2)}, u32[]{:S(2)}) collective-permute-start(f16[4,4,8,128]{3,2,1,0:T(8,128)(2,1)S(1)} %get-tuple-element.39), channel_id=1, source_target_pairs={{0,16},{8,24},{16,0},{24,8},{32,48},{40,56},{48,32},{56,40},{64,80... | collective-permute-start | bytes 98312 | tf_op jit(solution)/shard_map/ppermute | solution.py:353
  69.9 0.1 multiply_reduce_fusion.5
  70.1 1.9 %collective-permute-done.5 = f16[4,4,8,128]{3,2,1,0:T(8,128)(2,1)S(1)} collective-permute-done((f16[4,4,8,128]{3,2,1,0:T(8,128)(2,1)S(1)}, f16[4,4,8,128]{3,2,1,0:T(8,128)(2,1)S(1)}, u32[]{:S(2)}, u32[]{:S(2)}) %collective-permute-start.5) | collective-permute-done | bytes 32800 | tf_op jit(solution)/shard_map/ppermute | solution.py:353
  72.0 0.1 multiply_reduce_fusion.12
  72.1 5.8 %collective-permute-start.6 = (f16[4,4,8,128]{3,2,1,0:T(8,128)(2,1)S(1)}, f16[4,4,8,128]{3,2,1,0:T(8,128)(2,1)S(1)}, u32[]{:S(2)}, u32[]{:S(2)}) collective-permute-start(f16[4,4,8,128]{3,2,1,0:T(8,128)(2,1)S(1)} %get-tuple-element.37), channel_id=1, source_target_pairs={{0,48},{8,56},{16,32},{24,40},{32,16},{40,24},{48,0},{56,8},{64,11... | collective-permute-start | bytes 98312 | tf_op jit(solution)/shard_map/ppermute | solution.py:353
  77.9 0.2 multiply_reduce_fusion.3
  78.1 1.7 %collective-permute-done.6 = f16[4,4,8,128]{3,2,1,0:T(8,128)(2,1)S(1)} collective-permute-done((f16[4,4,8,128]{3,2,1,0:T(8,128)(2,1)S(1)}, f16[4,4,8,128]{3,2,1,0:T(8,128)(2,1)S(1)}, u32[]{:S(2)}, u32[]{:S(2)}) %collective-permute-start.6) | collective-permute-done | bytes 32800 | tf_op jit(solution)/shard_map/ppermute | solution.py:353
  79.9 0.8 collective-permute-start.7
  80.8 0.2 multiply_reduce_fusion.1
  81.0 2.9 %collective-permute-done.7 = f16[4,4,8,128]{3,2,1,0:T(8,128)(2,1)S(1)} collective-permute-done((f16[4,4,8,128]{3,2,1,0:T(8,128)(2,1)S(1)}, f16[4,4,8,128]{3,2,1,0:T(8,128)(2,1)S(1)}, u32[]{:S(2)}, u32[]{:S(2)}) %collective-permute-start.7) | collective-permute-done | bytes 32800 | tf_op jit(solution)/shard_map/ppermute | solution.py:353
  84.0 0.3 collective-permute-start.8
  84.3 0.1 multiply_reduce_fusion
  84.4 4.8 %collective-permute-done.8 = f16[4,4,8,128]{3,2,1,0:T(8,128)(2,1)S(1)} collective-permute-done((f16[4,4,8,128]{3,2,1,0:T(8,128)(2,1)S(1)}, f16[4,4,8,128]{3,2,1,0:T(8,128)(2,1)S(1)}, u32[]{:S(2)}, u32[]{:S(2)}) %collective-permute-start.8) | collective-permute-done | bytes 32800 | tf_op jit(solution)/shard_map/ppermute | solution.py:353
  89.2 0.1 multiply_reduce_fusion.8
  89.3 0.7 add_bitcast_fusion
  (50 shorter events, 0.5 us)
Async XLA Ops:
  0.0 6.8 %copy-start.2 = (bf16[6,128,128]{2,1,0:T(8,128)(2,1)S(1)}, bf16[6,128,128]{2,1,0:T(8,128)(2,1)}, u32[]{:S(2)}) copy-start(bf16[6,128,128]{2,1,0:T(8,128)(2,1)} %out_hbm.1) | copy-start | bytes 589828
  1.6 5.2 %copy-start.7 = (f32[4,128]{1,0:T(4,128)S(1)}, f32[4,128]{1,0:T(4,128)}, u32[]{:S(2)}) copy-start(f32[4,128]{1,0:T(4,128)} %enc_hbm.1) | copy-start | bytes 6148
  1.6 5.2 %copy-start.8 = (f32[3,128]{1,0:T(4,128)S(1)}, f32[3,128]{1,0:T(4,128)}, u32[]{:S(2)}) copy-start(f32[3,128]{1,0:T(4,128)} %type_hbm.1) | copy-start | bytes 4612
  1.6 8.0 %collective-permute-start.1 = (bf16[160,128]{1,0:T(8,128)(2,1)S(1)}, bf16[160,128]{1,0:T(8,128)(2,1)S(1)}, u32[]{:S(2)}, u32[]{:S(2)}) collective-permute-start(bf16[160,128]{1,0:T(8,128)(2,1)S(1)} %pad_maximum_fusion), channel_id=1, source_target_pairs={{1,2},{3,4},{5,6},{2,1},{4,3},{6,5},{9,10},{11,12},{13,14},{10,9},... | collective-permute-start | bytes 122888 | tf_op jit(solution)/shard_map/ppermute | solution.py:308
  5.9 4.1 %collective-permute-start = (bf16[160,128]{1,0:T(8,128)(2,1)S(1)}, bf16[160,128]{1,0:T(8,128)(2,1)S(1)}, u32[]{:S(2)}, u32[]{:S(2)}) collective-permute-start(bf16[160,128]{1,0:T(8,128)(2,1)S(1)} %pad_maximum_fusion), channel_id=1, source_target_pairs={{0,1},{1,0},{2,3},{3,2},{4,5},{5,4},{6,7},{7,6},{8,9},{9,8},{10,11... | collective-permute-start | bytes 122888 | tf_op jit(solution)/shard_map/ppermute | solution.py:308
  6.6 0.7 copy-start.5
  6.6 0.7 copy-start.6
  6.6 0.7 copy-start.9
  6.6 0.7 copy-start.10
  6.6 0.7 copy-start.11
  6.6 0.7 copy-start.12
  6.7 0.7 copy-start.13
  6.7 3.3 %copy-start.3 = (bf16[6,128,128]{2,1,0:T(8,128)(2,1)S(1)}, bf16[6,128,128]{2,1,0:T(8,128)(2,1)}, u32[]{:S(2)}) copy-start(bf16[6,128,128]{2,1,0:T(8,128)(2,1)} %self_ref.3) | copy-start | bytes 589828
  7.4 2.6 %copy-start = (f32[1,4,4,8,128]{4,3,2,1,0:T(8,128)S(1)}, f32[1,4,4,8,128]{4,3,2,1,0:T(8,128)}, u32[]{:S(2)}) copy-start(f32[1,4,4,8,128]{4,3,2,1,0:T(8,128)} %param.15) | copy-start | bytes 196612
  7.4 2.6 %copy-start.1 = (s32[4,8,128]{2,1,0:T(8,128)S(1)}, s32[4,8,128]{2,1,0:T(8,128)}, u32[]{:S(2)}) copy-start(s32[4,8,128]{2,1,0:T(8,128)} %kind_ref.3) | copy-start | bytes 49156
  10.0 0.9 %copy-start.4 = (bf16[6,128,128]{2,1,0:T(8,128)(2,1)S(1)}, bf16[6,128,128]{2,1,0:T(8,128)(2,1)}, u32[]{:S(2)}) copy-start(bf16[6,128,128]{2,1,0:T(8,128)(2,1)} %neigh_ref.3) | copy-start | bytes 589828
  10.9 26.9 %copy-start.14 = (f32[4,4,4,8,128]{4,3,2,1,0:T(8,128)S(1)}, f32[4,4,4,8,128]{4,3,2,1,0:T(8,128)}, u32[]{:S(2)}) copy-start(f32[4,4,4,8,128]{4,3,2,1,0:T(8,128)} %param.18) | copy-start | bytes 786436
  33.7 7.9 %collective-permute-start.3 = (bf16[128,128]{1,0:T(8,128)(2,1)S(1)}, bf16[128,128]{1,0:T(8,128)(2,1)S(1)}, u32[]{:S(2)}, u32[]{:S(2)}) collective-permute-start(bf16[128,128]{1,0:T(8,128)(2,1)S(1)} %get-tuple-element.20), channel_id=1, source_target_pairs={{1,2},{3,4},{5,6},{2,1},{4,3},{6,5},{9,10},{11,12},{13,14},{10,9},... | collective-permute-start | bytes 98312 | tf_op jit(solution)/shard_map/ppermute | solution.py:308
  37.7 4.0 %collective-permute-start.2 = (bf16[128,128]{1,0:T(8,128)(2,1)S(1)}, bf16[128,128]{1,0:T(8,128)(2,1)S(1)}, u32[]{:S(2)}, u32[]{:S(2)}) collective-permute-start(bf16[128,128]{1,0:T(8,128)(2,1)S(1)} %get-tuple-element.20), channel_id=1, source_target_pairs={{0,1},{1,0},{2,3},{3,2},{4,5},{5,4},{6,7},{7,6},{8,9},{9,8},{10,11... | collective-permute-start | bytes 98312 | tf_op jit(solution)/shard_map/ppermute | solution.py:308
  65.2 1.3 %collective-permute-start.4 = (f16[4,4,8,128]{3,2,1,0:T(8,128)(2,1)S(1)}, f16[4,4,8,128]{3,2,1,0:T(8,128)(2,1)S(1)}, u32[]{:S(2)}, u32[]{:S(2)}) collective-permute-start(f16[4,4,8,128]{3,2,1,0:T(8,128)(2,1)S(1)} %get-tuple-element.41), channel_id=1, source_target_pairs={{0,8},{8,0},{16,24},{24,16},{32,40},{40,32},{48,56},{56,48},{64,72... | collective-permute-start | bytes 98312 | tf_op jit(solution)/shard_map/ppermute | solution.py:353
  66.6 5.4 %collective-permute-start.5 = (f16[4,4,8,128]{3,2,1,0:T(8,128)(2,1)S(1)}, f16[4,4,8,128]{3,2,1,0:T(8,128)(2,1)S(1)}, u32[]{:S(2)}, u32[]{:S(2)}) collective-permute-start(f16[4,4,8,128]{3,2,1,0:T(8,128)(2,1)S(1)} %get-tuple-element.39), channel_id=1, source_target_pairs={{0,16},{8,24},{16,0},{24,8},{32,48},{40,56},{48,32},{56,40},{64,80... | collective-permute-start | bytes 98312 | tf_op jit(solution)/shard_map/ppermute | solution.py:353
  72.1 7.7 %collective-permute-start.6 = (f16[4,4,8,128]{3,2,1,0:T(8,128)(2,1)S(1)}, f16[4,4,8,128]{3,2,1,0:T(8,128)(2,1)S(1)}, u32[]{:S(2)}, u32[]{:S(2)}) collective-permute-start(f16[4,4,8,128]{3,2,1,0:T(8,128)(2,1)S(1)} %get-tuple-element.37), channel_id=1, source_target_pairs={{0,48},{8,56},{16,32},{24,40},{32,16},{40,24},{48,0},{56,8},{64,11... | collective-permute-start | bytes 98312 | tf_op jit(solution)/shard_map/ppermute | solution.py:353
  79.9 4.0 %collective-permute-start.7 = (f16[4,4,8,128]{3,2,1,0:T(8,128)(2,1)S(1)}, f16[4,4,8,128]{3,2,1,0:T(8,128)(2,1)S(1)}, u32[]{:S(2)}, u32[]{:S(2)}) collective-permute-start(f16[4,4,8,128]{3,2,1,0:T(8,128)(2,1)S(1)} %get-tuple-element.35), channel_id=1, source_target_pairs={{0,64},{8,72},{16,80},{24,88},{32,96},{40,104},{48,112},{56,120},{... | collective-permute-start | bytes 98312 | tf_op jit(solution)/shard_map/ppermute | solution.py:353
  84.0 5.2 %collective-permute-start.8 = (f16[4,4,8,128]{3,2,1,0:T(8,128)(2,1)S(1)}, f16[4,4,8,128]{3,2,1,0:T(8,128)(2,1)S(1)}, u32[]{:S(2)}, u32[]{:S(2)}) collective-permute-start(f16[4,4,8,128]{3,2,1,0:T(8,128)(2,1)S(1)} %add_convert_fusion), channel_id=1, source_target_pairs={{0,192},{8,200},{16,208},{24,216},{32,224},{40,232},{48,240},{56,2... | collective-permute-start | bytes 98312 | tf_op jit(solution)/shard_map/ppermute | solution.py:353

commit v7 on v6

--- a/solution.py
+++ b/solution.py
@@ -236,16 +236,16 @@
 
 def prepare(
     plan_ref, rate_ref,
-    enc_hbm, type_hbm, force_hbm, gain_hbm, out_hbm, bias_hbm, dec_gain_hbm, dec_hbm,
-    enc_first_ref, enc_second_ref, leave_ref, bias_ref, gains_ref, dec_out_ref,
+    enc_hbm, type_hbm, force_hbm, gain_hbm, out_hbm, bias_hbm, dec_gain_hbm, dec_hbm, neigh_hbm,
+    enc_first_ref, enc_second_ref, neigh_ref, leave_ref, bias_ref, gains_ref, dec_out_ref,
     enc, kind, force, gain, out, bias, dec_gain, dec, sems,
 ):
-    sources = (enc_hbm, type_hbm, force_hbm, gain_hbm, out_hbm, bias_hbm, dec_gain_hbm, dec_hbm)
-    targets = (enc, kind, force, gain, out, bias, dec_gain, dec)
+    sources = (enc_hbm, type_hbm, force_hbm, gain_hbm, out_hbm, bias_hbm, dec_gain_hbm, dec_hbm, neigh_hbm)
+    targets = (enc, kind, force, gain, out, bias, dec_gain, dec, neigh_ref)
     copies = [pltpu.make_async_copy(a, b, sems.at[n]) for n, (a, b) in enumerate(zip(sources, targets))]
     for copy in copies:
         copy.start()
-    for copy in copies:
+    for copy in copies[:-1]:
         copy.wait()
 
     line = lax.broadcasted_iota(jnp.int32, (BLOCK, HID), 0)
@@ -275,6 +275,7 @@
     for x in range(BLOCK):
         part = jnp.concatenate(spread(rows, x), axis=0).astype(BF16)
         dec_out_ref[x // 2, :, (x % 2) * HID : (x % 2 + 1) * HID] = part
+    copies[-1].wait()
 
 
 def run_prepare(plan, rate_values, *arrays):
@@ -283,6 +284,7 @@
     shapes = (
         ((FEATURES * BLOCK, BLOCK * HID), BF16),
         ((FEATURES * BLOCK, BLOCK * HID), BF16),
+        ((LAYERS, HID, HID), BF16),
         ((LAYERS, 2 * HID, HID), BF16),
         ((LAYERS, 1, HID), F32),
         ((LAYERS + 1, 1, HID), F32),
@@ -293,7 +295,7 @@
         out_shape=tuple(jax.ShapeDtypeStruct(shape, dtype) for shape, dtype in shapes),
         in_specs=[smem] * 2 + [pl.BlockSpec(memory_space=pltpu.HBM)] * len(arrays),
         out_specs=(vmem,) * len(shapes),
-        scratch_shapes=[pltpu.VMEM(array.shape, array.dtype) for array in arrays]
+        scratch_shapes=[pltpu.VMEM(array.shape, array.dtype) for array in arrays[:-1]]
         + [pltpu.SemaphoreType.DMA((len(arrays),))],
         compiler_params=pltpu.CompilerParams(vmem_limit_bytes=8 * 2**20),
         cost_estimate=pl.CostEstimate(flops=10**8, bytes_accessed=2**21, transcendentals=0),
@@ -330,14 +332,14 @@
     kinds = sides = exchange(outgoing)
     enc_first, enc_second, *weights = run_prepare(
         plan, rate_values, enc_weight, type_table, force_vector[None], norm_gain,
-        out_weight, layer_bias, dec_gain[None], dec_weight,
+        out_weight, layer_bias, dec_gain[None], dec_weight, neigh_weight,
     )
 
     state = own
     for step_index in range(STEPS):
         state, outgoing = run_fine_step(
             where, state, *sides, cell_type, *kinds, (enc_first, enc_second)[step_index],
-            self_weight, neigh_weight, *weights,
+            self_weight, *weights,
         )
         if step_index + 1 < STEPS:
             sides = exchange(outgoing)

time: 90.4 us -> 89.2 us (0.987)
  waiting for transfers between devices: 17.8 us -> 16.4 us
    ppermute x2, waiting for transfers between devices: 5 us -> 3.5 us  [exchange(): lax.ppermute(value, 'space', second)]
  transfers between devices with their start and end apart: 9 -> 9, of which waited for: 8 -> 8; matrix products, arithmetic and copies ran while one was open for 1% -> 1% of each run, Pallas kernels for 1% -> 2%
where the time goes in v7:
time: 89.2 us; the launch traced here: 89 us
  Pallas kernels  47.1 us (53%)
  starting transfers between devices  20.1 us (23%)
  waiting for transfers between devices  16.4 us (18%)
  other arithmetic  3.32 us (4%)
  local copies, waits for them, and re-layouts  1.62 us (2%)
    pallas_call x2, Pallas kernels, run_fine_step(): pl.pallas_call(fine_step, out_shape=(jax.ShapeDtypeStruct((CHAN, NZ, BLOC...  45.8 us
    ppermute x5, waiting for transfers between devices, per_device(): came = lax.ppermute(total.astype(jnp.float16), 'tm', partners).astype(F32)  12.3 us
    ppermute x5, starting transfers between devices, per_device(): came = lax.ppermute(total.astype(jnp.float16), 'tm', partners).astype(F32)  10.6 us
    ppermute x2, starting transfers between devices, exchange(): lax.ppermute(value, 'space', second)  8.6 us
    ppermute x2, waiting for transfers between devices, exchange(): lax.ppermute(value, 'space', second)  3.5 us
  transfers between devices with their start and end apart: 9, of which 8 were waited for; matrix products, arithmetic and copies ran while one was open for 1% of the time, Pallas kernels for 2%

profile of v7, /device:TPU:56, one launch (start us, length us, event | category | flops | bytes accessed | tf_op | source)
XLA Modules:
  0.0 89.0 jit_solution(13718798146976370932)
XLA Ops:
  0.0 0.8 fusion
  0.8 0.8 convert.8
  1.7 4.3 %collective-permute-start.1 = (bf16[160,128]{1,0:T(8,128)(2,1)S(1)}, bf16[160,128]{1,0:T(8,128)(2,1)S(1)}, u32[]{:S(2)}, u32[]{:S(2)}) collective-permute-start(bf16[160,128]{1,0:T(8,128)(2,1)S(1)} %pad_maximum_fusion), channel_id=1, source_target_pairs={{1,2},{3,4},{5,6},{2,1},{4,3},{6,5},{9,10},{11,12},{13,14},{10,9},... | collective-permute-start | bytes 122888 | tf_op jit(solution)/shard_map/ppermute | solution.py:310
  6.0 0.8 collective-permute-start
  6.8 0.1 pad_add_fusion.where_ref
  6.9 0.6 copy-done.6
  7.5 0.9 %copy-done.2 = bf16[6,128,128]{2,1,0:T(8,128)(2,1)S(1)} copy-done((bf16[6,128,128]{2,1,0:T(8,128)(2,1)S(1)}, bf16[6,128,128]{2,1,0:T(8,128)(2,1)}, u32[]{:S(2)}) %copy-start.2) | copy-done | bytes 196632
  8.5 1.4 %prepare.1 = (bf16[112,1024]{1,0:T(8,128)(2,1)S(1)}, bf16[112,1024]{1,0:T(8,128)(2,1)S(1)}, bf16[6,128,128]{2,1,0:T(8,128)(2,1)S(1)}, bf16[6,256,128]{2,1,0:T(8,...) custom-call(s32[1,2]{1,0:T(1,128)S(1)} %copy-done.9, ...), custom_call_target="tpu_custom_call" | custom-call | flops 100000000 | bytes 2097152 | tf_op jit(solution)/shard_map/prepare/pallas_call | solution.py:293
  9.9 0.2 collective-permute-done.first_ref.kind_first_ref
  10.1 22.4 %fine_step.2 = (f32[4,4,8,128]{3,2,1,0:T(8,128)S(1)}, bf16[128,128]{1,0:T(8,128)(2,1)S(1)}) custom-call(s32[2]{0:T(128)S(1)} %pad_add_fusion.where_ref, f32[4,4,8,128]{3,2,1,0:T(8,128)S(1)} %bitcast.9, bf16[160,128]{1,0:T(8,128)(2,1)S(1)} %collective-permute-done.first_ref.kind_first_ref, ...), custom_call_target="tpu_custom_call" | custom-call | flops 10000000000 | bytes 2097152 | tf_op jit(solution)/shard_map/fine_step/pallas_call | solution.py:209
  32.5 4.3 %collective-permute-start.3 = (bf16[128,128]{1,0:T(8,128)(2,1)S(1)}, bf16[128,128]{1,0:T(8,128)(2,1)S(1)}, u32[]{:S(2)}, u32[]{:S(2)}) collective-permute-start(bf16[128,128]{1,0:T(8,128)(2,1)S(1)} %get-tuple-element.22), channel_id=1, source_target_pairs={{1,2},{3,4},{5,6},{2,1},{4,3},{6,5},{9,10},{11,12},{13,14},{10,9},... | collective-permute-start | bytes 98312 | tf_op jit(solution)/shard_map/ppermute | solution.py:310
  36.8 0.1 collective-permute-start.2
  36.9 3.5 %collective-permute-done.3.second_ref = bf16[128,128]{1,0:T(8,128)(2,1)S(1)} collective-permute-done((bf16[128,128]{1,0:T(8,128)(2,1)S(1)}, bf16[128,128]{1,0:T(8,128)(2,1)S(1)}, u32[]{:S(2)}, u32[]{:S(2)}) %collective-permute-start.3) | collective-permute-done | bytes 32800 | tf_op jit(solution)/shard_map/ppermute | solution.py:310
  40.4 0.4 collective-permute-done.2.first_ref
  40.8 23.4 %fine_step.3 = (f32[4,4,8,128]{3,2,1,0:T(8,128)S(1)}, bf16[128,128]{1,0:T(8,128)(2,1)}) custom-call(s32[2]{0:T(128)S(1)} %pad_add_fusion.where_ref, f32[4,4,8,128]{3,2,1,0:T(8,128)S(1)} %get-tuple-element.21.own_ref, bf16[128,128]{1,0:T(8,128)(2,1)S(1)} %collective-permute-done.2.first_ref, bf16[128,128]{1,0:T(8,128)(2,1)S(1)} %collective-permute-done.3.second_ref, ...), custom_call_target="tpu_custom_call" | custom-call | flops 10000000000 | bytes 2097152 | tf_op jit(solution)/shard_map/fine_step/pallas_call | solution.py:209
  64.2 0.1 collective-permute-start.4
  64.3 1.2 %collective-permute-done.4 = f16[4,4,8,128]{3,2,1,0:T(8,128)(2,1)S(1)} collective-permute-done((f16[4,4,8,128]{3,2,1,0:T(8,128)(2,1)S(1)}, f16[4,4,8,128]{3,2,1,0:T(8,128)(2,1)S(1)}, u32[]{:S(2)}, u32[]{:S(2)}) %collective-permute-start.4) | collective-permute-done | bytes 32800 | tf_op jit(solution)/shard_map/ppermute | solution.py:355
  65.6 3.0 %collective-permute-start.5 = (f16[4,4,8,128]{3,2,1,0:T(8,128)(2,1)S(1)}, f16[4,4,8,128]{3,2,1,0:T(8,128)(2,1)S(1)}, u32[]{:S(2)}, u32[]{:S(2)}) collective-permute-start(f16[4,4,8,128]{3,2,1,0:T(8,128)(2,1)S(1)} %get-tuple-element.41), channel_id=1, source_target_pairs={{0,16},{8,24},{16,0},{24,8},{32,48},{40,56},{48,32},{56,40},{64,80... | collective-permute-start | bytes 98312 | tf_op jit(solution)/shard_map/ppermute | solution.py:355
  68.6 0.1 multiply_reduce_fusion.5
  68.8 1.7 %collective-permute-done.5 = f16[4,4,8,128]{3,2,1,0:T(8,128)(2,1)S(1)} collective-permute-done((f16[4,4,8,128]{3,2,1,0:T(8,128)(2,1)S(1)}, f16[4,4,8,128]{3,2,1,0:T(8,128)(2,1)S(1)}, u32[]{:S(2)}, u32[]{:S(2)}) %collective-permute-start.5) | collective-permute-done | bytes 32800 | tf_op jit(solution)/shard_map/ppermute | solution.py:355
  70.5 0.1 multiply_reduce_fusion.12
  70.6 6.4 %collective-permute-start.6 = (f16[4,4,8,128]{3,2,1,0:T(8,128)(2,1)S(1)}, f16[4,4,8,128]{3,2,1,0:T(8,128)(2,1)S(1)}, u32[]{:S(2)}, u32[]{:S(2)}) collective-permute-start(f16[4,4,8,128]{3,2,1,0:T(8,128)(2,1)S(1)} %get-tuple-element.39), channel_id=1, source_target_pairs={{0,48},{8,56},{16,32},{24,40},{32,16},{40,24},{48,0},{56,8},{64,11... | collective-permute-start | bytes 98312 | tf_op jit(solution)/shard_map/ppermute | solution.py:355
  77.0 0.2 multiply_reduce_fusion.3
  77.1 1.7 %collective-permute-done.6 = f16[4,4,8,128]{3,2,1,0:T(8,128)(2,1)S(1)} collective-permute-done((f16[4,4,8,128]{3,2,1,0:T(8,128)(2,1)S(1)}, f16[4,4,8,128]{3,2,1,0:T(8,128)(2,1)S(1)}, u32[]{:S(2)}, u32[]{:S(2)}) %collective-permute-start.6) | collective-permute-done | bytes 32800 | tf_op jit(solution)/shard_map/ppermute | solution.py:355
  78.9 0.8 collective-permute-start.7
  79.8 0.2 multiply_reduce_fusion.1
  80.0 2.9 %collective-permute-done.7 = f16[4,4,8,128]{3,2,1,0:T(8,128)(2,1)S(1)} collective-permute-done((f16[4,4,8,128]{3,2,1,0:T(8,128)(2,1)S(1)}, f16[4,4,8,128]{3,2,1,0:T(8,128)(2,1)S(1)}, u32[]{:S(2)}, u32[]{:S(2)}) %collective-permute-start.7) | collective-permute-done | bytes 32800 | tf_op jit(solution)/shard_map/ppermute | solution.py:355
  83.0 0.3 collective-permute-start.8
  83.3 0.1 multiply_reduce_fusion
  83.4 4.8 %collective-permute-done.8 = f16[4,4,8,128]{3,2,1,0:T(8,128)(2,1)S(1)} collective-permute-done((f16[4,4,8,128]{3,2,1,0:T(8,128)(2,1)S(1)}, f16[4,4,8,128]{3,2,1,0:T(8,128)(2,1)S(1)}, u32[]{:S(2)}, u32[]{:S(2)}) %collective-permute-start.8) | collective-permute-done | bytes 32800 | tf_op jit(solution)/shard_map/ppermute | solution.py:355
  88.2 0.1 multiply_reduce_fusion.8
  88.3 0.7 add_bitcast_fusion
  (50 shorter events, 0.5 us)
Async XLA Ops:
  0.0 6.9 %copy-start.1 = (bf16[6,128,128]{2,1,0:T(8,128)(2,1)S(1)}, bf16[6,128,128]{2,1,0:T(8,128)(2,1)}, u32[]{:S(2)}) copy-start(bf16[6,128,128]{2,1,0:T(8,128)(2,1)} %out_hbm.1) | copy-start | bytes 589828
  1.6 5.3 %copy-start.9 = (s32[1,2]{1,0:T(1,128)S(1)}, s32[1,2]{1,0:T(1,128)}, u32[]{:S(2)}) copy-start(s32[1,2]{1,0:T(1,128)} %plan_ref.1) | copy-start | bytes 28
  1.6 5.3 %copy-start.10 = (f32[8]{0:T(128)S(1)}, f32[8]{0:T(128)}, u32[]{:S(2)}) copy-start(f32[8]{0:T(128)} %rate_ref.1) | copy-start | bytes 100
  1.6 5.3 %copy-start.11 = (f32[128]{0:T(128)S(1)}, f32[128]{0:T(128)}, u32[]{:S(2)}) copy-start(f32[128]{0:T(128)} %param.22) | copy-start | bytes 1540
  1.6 5.3 %copy-start.12 = (f32[128]{0:T(128)S(1)}, f32[128]{0:T(128)}, u32[]{:S(2)}) copy-start(f32[128]{0:T(128)} %param.28) | copy-start | bytes 1540
  1.7 8.2 %collective-permute-start.1 = (bf16[160,128]{1,0:T(8,128)(2,1)S(1)}, bf16[160,128]{1,0:T(8,128)(2,1)S(1)}, u32[]{:S(2)}, u32[]{:S(2)}) collective-permute-start(bf16[160,128]{1,0:T(8,128)(2,1)S(1)} %pad_maximum_fusion), channel_id=1, source_target_pairs={{1,2},{3,4},{5,6},{2,1},{4,3},{6,5},{9,10},{11,12},{13,14},{10,9},... | collective-permute-start | bytes 122888 | tf_op jit(solution)/shard_map/ppermute | solution.py:310
  6.0 4.1 %collective-permute-start = (bf16[160,128]{1,0:T(8,128)(2,1)S(1)}, bf16[160,128]{1,0:T(8,128)(2,1)S(1)}, u32[]{:S(2)}, u32[]{:S(2)}) collective-permute-start(bf16[160,128]{1,0:T(8,128)(2,1)S(1)} %pad_maximum_fusion), channel_id=1, source_target_pairs={{0,1},{1,0},{2,3},{3,2},{4,5},{5,4},{6,7},{7,6},{8,9},{9,8},{10,11... | collective-permute-start | bytes 122888 | tf_op jit(solution)/shard_map/ppermute | solution.py:310
  6.8 0.7 copy-start.6
  6.8 0.7 copy-start.7
  6.8 0.7 copy-start.5
  6.8 0.7 copy-start.4
  6.9 0.7 copy-start.8
  7.5 0.9 %copy-start.2 = (bf16[6,128,128]{2,1,0:T(8,128)(2,1)S(1)}, bf16[6,128,128]{2,1,0:T(8,128)(2,1)}, u32[]{:S(2)}) copy-start(bf16[6,128,128]{2,1,0:T(8,128)(2,1)} %neigh_hbm.1) | copy-start | bytes 589828
  8.5 1.6 %copy-start = (f32[1,4,4,8,128]{4,3,2,1,0:T(8,128)S(1)}, f32[1,4,4,8,128]{4,3,2,1,0:T(8,128)}, u32[]{:S(2)}) copy-start(f32[1,4,4,8,128]{4,3,2,1,0:T(8,128)} %param.15) | copy-start | bytes 196612
  8.5 1.6 %copy-start.3 = (s32[4,8,128]{2,1,0:T(8,128)S(1)}, s32[4,8,128]{2,1,0:T(8,128)}, u32[]{:S(2)}) copy-start(s32[4,8,128]{2,1,0:T(8,128)} %kind_ref.3) | copy-start | bytes 49156
  8.5 1.6 %copy-start.13 = (bf16[6,128,128]{2,1,0:T(8,128)(2,1)S(1)}, bf16[6,128,128]{2,1,0:T(8,128)(2,1)}, u32[]{:S(2)}) copy-start(bf16[6,128,128]{2,1,0:T(8,128)(2,1)} %self_ref.3) | copy-start | bytes 589828
  10.1 26.8 %copy-start.14 = (f32[4,4,4,8,128]{4,3,2,1,0:T(8,128)S(1)}, f32[4,4,4,8,128]{4,3,2,1,0:T(8,128)}, u32[]{:S(2)}) copy-start(f32[4,4,4,8,128]{4,3,2,1,0:T(8,128)} %param.18) | copy-start | bytes 786436
  32.5 7.9 %collective-permute-start.3 = (bf16[128,128]{1,0:T(8,128)(2,1)S(1)}, bf16[128,128]{1,0:T(8,128)(2,1)S(1)}, u32[]{:S(2)}, u32[]{:S(2)}) collective-permute-start(bf16[128,128]{1,0:T(8,128)(2,1)S(1)} %get-tuple-element.22), channel_id=1, source_target_pairs={{1,2},{3,4},{5,6},{2,1},{4,3},{6,5},{9,10},{11,12},{13,14},{10,9},... | collective-permute-start | bytes 98312 | tf_op jit(solution)/shard_map/ppermute | solution.py:310
  36.8 4.0 %collective-permute-start.2 = (bf16[128,128]{1,0:T(8,128)(2,1)S(1)}, bf16[128,128]{1,0:T(8,128)(2,1)S(1)}, u32[]{:S(2)}, u32[]{:S(2)}) collective-permute-start(bf16[128,128]{1,0:T(8,128)(2,1)S(1)} %get-tuple-element.22), channel_id=1, source_target_pairs={{0,1},{1,0},{2,3},{3,2},{4,5},{5,4},{6,7},{7,6},{8,9},{9,8},{10,11... | collective-permute-start | bytes 98312 | tf_op jit(solution)/shard_map/ppermute | solution.py:310
  64.2 1.3 %collective-permute-start.4 = (f16[4,4,8,128]{3,2,1,0:T(8,128)(2,1)S(1)}, f16[4,4,8,128]{3,2,1,0:T(8,128)(2,1)S(1)}, u32[]{:S(2)}, u32[]{:S(2)}) collective-permute-start(f16[4,4,8,128]{3,2,1,0:T(8,128)(2,1)S(1)} %get-tuple-element.43), channel_id=1, source_target_pairs={{0,8},{8,0},{16,24},{24,16},{32,40},{40,32},{48,56},{56,48},{64,72... | collective-permute-start | bytes 98312 | tf_op jit(solution)/shard_map/ppermute | solution.py:355
  65.6 4.9 %collective-permute-start.5 = (f16[4,4,8,128]{3,2,1,0:T(8,128)(2,1)S(1)}, f16[4,4,8,128]{3,2,1,0:T(8,128)(2,1)S(1)}, u32[]{:S(2)}, u32[]{:S(2)}) collective-permute-start(f16[4,4,8,128]{3,2,1,0:T(8,128)(2,1)S(1)} %get-tuple-element.41), channel_id=1, source_target_pairs={{0,16},{8,24},{16,0},{24,8},{32,48},{40,56},{48,32},{56,40},{64,80... | collective-permute-start | bytes 98312 | tf_op jit(solution)/shard_map/ppermute | solution.py:355
  70.6 8.3 %collective-permute-start.6 = (f16[4,4,8,128]{3,2,1,0:T(8,128)(2,1)S(1)}, f16[4,4,8,128]{3,2,1,0:T(8,128)(2,1)S(1)}, u32[]{:S(2)}, u32[]{:S(2)}) collective-permute-start(f16[4,4,8,128]{3,2,1,0:T(8,128)(2,1)S(1)} %get-tuple-element.39), channel_id=1, source_target_pairs={{0,48},{8,56},{16,32},{24,40},{32,16},{40,24},{48,0},{56,8},{64,11... | collective-permute-start | bytes 98312 | tf_op jit(solution)/shard_map/ppermute | solution.py:355
  78.9 4.0 %collective-permute-start.7 = (f16[4,4,8,128]{3,2,1,0:T(8,128)(2,1)S(1)}, f16[4,4,8,128]{3,2,1,0:T(8,128)(2,1)S(1)}, u32[]{:S(2)}, u32[]{:S(2)}) collective-permute-start(f16[4,4,8,128]{3,2,1,0:T(8,128)(2,1)S(1)} %get-tuple-element.37), channel_id=1, source_target_pairs={{0,64},{8,72},{16,80},{24,88},{32,96},{40,104},{48,112},{56,120},{... | collective-permute-start | bytes 98312 | tf_op jit(solution)/shard_map/ppermute | solution.py:355
  83.0 5.2 %collective-permute-start.8 = (f16[4,4,8,128]{3,2,1,0:T(8,128)(2,1)S(1)}, f16[4,4,8,128]{3,2,1,0:T(8,128)(2,1)S(1)}, u32[]{:S(2)}, u32[]{:S(2)}) collective-permute-start(f16[4,4,8,128]{3,2,1,0:T(8,128)(2,1)S(1)} %add_convert_fusion), channel_id=1, source_target_pairs={{0,192},{8,200},{16,208},{24,216},{32,224},{40,232},{48,240},{56,2... | collective-permute-start | bytes 98312 | tf_op jit(solution)/shard_map/ppermute | solution.py:355

commit v8 on v7

--- a/solution.py
+++ b/solution.py
@@ -326,9 +326,11 @@
     position = lax.axis_index("space")
     where = jnp.stack([position, lax.axis_size("space") - 1]).astype(jnp.int32)
 
-    outgoing = jnp.concatenate(
-        [own.reshape(ROWS, NY), cell_type.astype(F32).reshape(NZ * BLOCK, NY)], axis=0
-    ).astype(BF16)
+    slabs = CHAN * NZ
+    states = jnp.pad(own.reshape(slabs, BLOCK, NY), ((0, NZ), (0, 0), (0, 0)))
+    types = jnp.pad(cell_type, ((slabs, 0), (0, 0), (0, 0))).astype(F32)
+    slab = lax.broadcasted_iota(jnp.int32, states.shape, 0)
+    outgoing = jnp.where(slab < slabs, states, types).astype(BF16).reshape(ROWS + NZ * BLOCK, NY)
     kinds = sides = exchange(outgoing)
     enc_first, enc_second, *weights = run_prepare(
         plan, rate_values, enc_weight, type_table, force_vector[None], norm_gain,

time: 89.2 us -> 88.5 us (level)
  starting transfers between devices: 20.1 us -> 18.9 us
  local copies, waits for them, and re-layouts: 1.62 us -> 2.56 us
    unnamed x30, local copies, waits for them, and re-layouts: 1.62 us -> 2.56 us
  transfers between devices with their start and end apart: 9 -> 9, of which waited for: 8 -> 6; matrix products, arithmetic and copies ran while one was open for 1% -> 1% of each run, Pallas kernels for 2% -> 2%
where the time goes in v8:
time: 88.5 us; the launch traced here: 88.3 us
  Pallas kernels  47.1 us (53%)
  starting transfers between devices  18.9 us (21%)
  waiting for transfers between devices  16.6 us (19%)
  other arithmetic  2.68 us (3%)
  local copies, waits for them, and re-layouts  2.56 us (3%)
    pallas_call x2, Pallas kernels, run_fine_step(): pl.pallas_call(fine_step, out_shape=(jax.ShapeDtypeStruct((CHAN, NZ, BLOC...  45.7 us
    ppermute x5, waiting for transfers between devices, per_device(): came = lax.ppermute(total.astype(jnp.float16), 'tm', partners).astype(F32)  12.4 us
    ppermute x5, starting transfers between devices, per_device(): came = lax.ppermute(total.astype(jnp.float16), 'tm', partners).astype(F32)  10.3 us
    ppermute x2, starting transfers between devices, exchange(): lax.ppermute(value, 'space', second)  7.77 us
    ppermute x2, waiting for transfers between devices, exchange(): lax.ppermute(value, 'space', second)  4.18 us
    unnamed x30, local copies, waits for them, and re-layouts  2.56 us
  transfers between devices with their start and end apart: 9, of which 6 were waited for; matrix products, arithmetic and copies ran while one was open for 1% of the time, Pallas kernels for 2%

profile of v8, /device:TPU:56, one launch (start us, length us, event | category | flops | bytes accessed | tf_op | source)
XLA Modules:
  0.0 88.3 jit_solution(9606397495776619985)
XLA Ops:
  0.0 1.0 %fusion = bf16[160,128]{1,0:T(8,128)(2,1)S(1)} fusion(s32[4,8,128]{2,1,0:T(8,128)} %kind_ref.3, f32[16,8,128]{2,1,0:T(8,128)} %bitcast.9, pred[20]{0:T(512)(128)(4,1)S(1)} %iota_compare_fusion), kind=kLoop, calls=%fused_computation.26 | loop fusion | flops 40960 | bytes 122900 | tf_op jit(solution)/shard_map/reshape | solution.py:333
  1.0 4.2 %collective-permute-start.1 = (bf16[160,128]{1,0:T(8,128)(2,1)S(1)}, bf16[160,128]{1,0:T(8,128)(2,1)S(1)}, u32[]{:S(2)}, u32[]{:S(2)}) collective-permute-start(bf16[160,128]{1,0:T(8,128)(2,1)S(1)} %fusion), channel_id=1, source_target_pairs={{1,2},{3,4},{5,6},{2,1},{4,3},{6,5},{9,10},{11,12},{13,14},{10,9},... | collective-permute-start | bytes 122888 | tf_op jit(solution)/shard_map/ppermute | solution.py:310
  5.2 0.8 collective-permute-start
  6.0 0.1 pad_add_fusion.where_ref
  6.1 0.6 copy-done.7
  6.7 0.0 copy-done.5
  6.7 0.0 copy-done.8
  6.8 0.9 %copy-done.1 = bf16[6,128,128]{2,1,0:T(8,128)(2,1)S(1)} copy-done((bf16[6,128,128]{2,1,0:T(8,128)(2,1)S(1)}, bf16[6,128,128]{2,1,0:T(8,128)(2,1)}, u32[]{:S(2)}) %copy-start.1) | copy-done | bytes 196632
  7.7 0.9 %copy-done.2 = bf16[6,128,128]{2,1,0:T(8,128)(2,1)S(1)} copy-done((bf16[6,128,128]{2,1,0:T(8,128)(2,1)S(1)}, bf16[6,128,128]{2,1,0:T(8,128)(2,1)}, u32[]{:S(2)}) %copy-start.2) | copy-done | bytes 196632
  8.6 1.4 %prepare.1 = (bf16[112,1024]{1,0:T(8,128)(2,1)S(1)}, bf16[112,1024]{1,0:T(8,128)(2,1)S(1)}, bf16[6,128,128]{2,1,0:T(8,128)(2,1)S(1)}, bf16[6,256,128]{2,1,0:T(8,...) custom-call(s32[1,2]{1,0:T(1,128)S(1)} %copy-done.9, ...), custom_call_target="tpu_custom_call" | custom-call | flops 100000000 | bytes 2097152 | tf_op jit(solution)/shard_map/prepare/pallas_call | solution.py:293
  10.1 22.4 %fine_step.2 = (f32[4,4,8,128]{3,2,1,0:T(8,128)S(1)}, bf16[128,128]{1,0:T(8,128)(2,1)S(1)}) custom-call(s32[2]{0:T(128)S(1)} %pad_add_fusion.where_ref, f32[4,4,8,128]{3,2,1,0:T(8,128)S(1)} %bitcast.10, bf16[160,128]{1,0:T(8,128)(2,1)S(1)} %collective-permute-done.first_ref.kind_first_ref, ...), custom_call_target="tpu_custom_call" | custom-call | flops 10000000000 | bytes 2097152 | tf_op jit(solution)/shard_map/fine_step/pallas_call | solution.py:209
  32.5 3.6 %collective-permute-start.3 = (bf16[128,128]{1,0:T(8,128)(2,1)S(1)}, bf16[128,128]{1,0:T(8,128)(2,1)S(1)}, u32[]{:S(2)}, u32[]{:S(2)}) collective-permute-start(bf16[128,128]{1,0:T(8,128)(2,1)S(1)} %get-tuple-element.22), channel_id=1, source_target_pairs={{1,2},{3,4},{5,6},{2,1},{4,3},{6,5},{9,10},{11,12},{13,14},{10,9},... | collective-permute-start | bytes 98312 | tf_op jit(solution)/shard_map/ppermute | solution.py:310
  36.0 0.1 collective-permute-start.2
  36.2 4.2 %collective-permute-done.3.second_ref = bf16[128,128]{1,0:T(8,128)(2,1)S(1)} collective-permute-done((bf16[128,128]{1,0:T(8,128)(2,1)S(1)}, bf16[128,128]{1,0:T(8,128)(2,1)S(1)}, u32[]{:S(2)}, u32[]{:S(2)}) %collective-permute-start.3) | collective-permute-done | bytes 32800 | tf_op jit(solution)/shard_map/ppermute | solution.py:310
  40.4 23.4 %fine_step.3 = (f32[4,4,8,128]{3,2,1,0:T(8,128)S(1)}, bf16[128,128]{1,0:T(8,128)(2,1)}) custom-call(s32[2]{0:T(128)S(1)} %pad_add_fusion.where_ref, f32[4,4,8,128]{3,2,1,0:T(8,128)S(1)} %get-tuple-element.21.own_ref, bf16[128,128]{1,0:T(8,128)(2,1)S(1)} %collective-permute-done.2.first_ref, bf16[128,128]{1,0:T(8,128)(2,1)S(1)} %collective-permute-done.3.second_ref, ...), custom_call_target="tpu_custom_call" | custom-call | flops 10000000000 | bytes 2097152 | tf_op jit(solution)/shard_map/fine_step/pallas_call | solution.py:209
  63.8 0.1 collective-permute-start.4
  63.9 1.2 %collective-permute-done.4 = f16[4,4,8,128]{3,2,1,0:T(8,128)(2,1)S(1)} collective-permute-done((f16[4,4,8,128]{3,2,1,0:T(8,128)(2,1)S(1)}, f16[4,4,8,128]{3,2,1,0:T(8,128)(2,1)S(1)}, u32[]{:S(2)}, u32[]{:S(2)}) %collective-permute-start.4) | collective-permute-done | bytes 32800 | tf_op jit(solution)/shard_map/ppermute | solution.py:357
  65.1 3.4 %collective-permute-start.5 = (f16[4,4,8,128]{3,2,1,0:T(8,128)(2,1)S(1)}, f16[4,4,8,128]{3,2,1,0:T(8,128)(2,1)S(1)}, u32[]{:S(2)}, u32[]{:S(2)}) collective-permute-start(f16[4,4,8,128]{3,2,1,0:T(8,128)(2,1)S(1)} %get-tuple-element.41), channel_id=1, source_target_pairs={{0,16},{8,24},{16,0},{24,8},{32,48},{40,56},{48,32},{56,40},{64,80... | collective-permute-start | bytes 98312 | tf_op jit(solution)/shard_map/ppermute | solution.py:357
  68.5 0.1 multiply_reduce_fusion.5
  68.7 1.7 %collective-permute-done.5 = f16[4,4,8,128]{3,2,1,0:T(8,128)(2,1)S(1)} collective-permute-done((f16[4,4,8,128]{3,2,1,0:T(8,128)(2,1)S(1)}, f16[4,4,8,128]{3,2,1,0:T(8,128)(2,1)S(1)}, u32[]{:S(2)}, u32[]{:S(2)}) %collective-permute-start.5) | collective-permute-done | bytes 32800 | tf_op jit(solution)/shard_map/ppermute | solution.py:357
  70.4 0.1 multiply_reduce_fusion.12
  70.5 5.8 %collective-permute-start.6 = (f16[4,4,8,128]{3,2,1,0:T(8,128)(2,1)S(1)}, f16[4,4,8,128]{3,2,1,0:T(8,128)(2,1)S(1)}, u32[]{:S(2)}, u32[]{:S(2)}) collective-permute-start(f16[4,4,8,128]{3,2,1,0:T(8,128)(2,1)S(1)} %get-tuple-element.39), channel_id=1, source_target_pairs={{0,48},{8,56},{16,32},{24,40},{32,16},{40,24},{48,0},{56,8},{64,11... | collective-permute-start | bytes 98312 | tf_op jit(solution)/shard_map/ppermute | solution.py:357
  76.3 0.2 multiply_reduce_fusion.3
  76.5 1.7 %collective-permute-done.6 = f16[4,4,8,128]{3,2,1,0:T(8,128)(2,1)S(1)} collective-permute-done((f16[4,4,8,128]{3,2,1,0:T(8,128)(2,1)S(1)}, f16[4,4,8,128]{3,2,1,0:T(8,128)(2,1)S(1)}, u32[]{:S(2)}, u32[]{:S(2)}) %collective-permute-start.6) | collective-permute-done | bytes 32800 | tf_op jit(solution)/shard_map/ppermute | solution.py:357
  78.3 0.8 collective-permute-start.7
  79.1 0.2 multiply_reduce_fusion.1
  79.4 2.9 %collective-permute-done.7 = f16[4,4,8,128]{3,2,1,0:T(8,128)(2,1)S(1)} collective-permute-done((f16[4,4,8,128]{3,2,1,0:T(8,128)(2,1)S(1)}, f16[4,4,8,128]{3,2,1,0:T(8,128)(2,1)S(1)}, u32[]{:S(2)}, u32[]{:S(2)}) %collective-permute-start.7) | collective-permute-done | bytes 32800 | tf_op jit(solution)/shard_map/ppermute | solution.py:357
  82.3 0.2 collective-permute-start.8
  82.6 0.1 multiply_reduce_fusion
  82.7 4.9 %collective-permute-done.8 = f16[4,4,8,128]{3,2,1,0:T(8,128)(2,1)S(1)} collective-permute-done((f16[4,4,8,128]{3,2,1,0:T(8,128)(2,1)S(1)}, f16[4,4,8,128]{3,2,1,0:T(8,128)(2,1)S(1)}, u32[]{:S(2)}, u32[]{:S(2)}) %collective-permute-start.8) | collective-permute-done | bytes 32800 | tf_op jit(solution)/shard_map/ppermute | solution.py:357
  87.6 0.1 multiply_reduce_fusion.8
  87.6 0.7 add_bitcast_fusion
  (49 shorter events, 0.5 us)
Async XLA Ops:
  0.0 6.1 %copy-start.9 = (s32[1,2]{1,0:T(1,128)S(1)}, s32[1,2]{1,0:T(1,128)}, u32[]{:S(2)}) copy-start(s32[1,2]{1,0:T(1,128)} %plan_ref.1) | copy-start | bytes 28
  0.0 6.1 %copy-start.10 = (f32[8]{0:T(128)S(1)}, f32[8]{0:T(128)}, u32[]{:S(2)}) copy-start(f32[8]{0:T(128)} %rate_ref.1) | copy-start | bytes 100
  0.0 6.1 %copy-start.11 = (f32[128]{0:T(128)S(1)}, f32[128]{0:T(128)}, u32[]{:S(2)}) copy-start(f32[128]{0:T(128)} %param.22) | copy-start | bytes 1540
  0.0 6.1 %copy-start.12 = (f32[128]{0:T(128)S(1)}, f32[128]{0:T(128)}, u32[]{:S(2)}) copy-start(f32[128]{0:T(128)} %param.28) | copy-start | bytes 1540
  1.0 9.0 %collective-permute-start.1 = (bf16[160,128]{1,0:T(8,128)(2,1)S(1)}, bf16[160,128]{1,0:T(8,128)(2,1)S(1)}, u32[]{:S(2)}, u32[]{:S(2)}) collective-permute-start(bf16[160,128]{1,0:T(8,128)(2,1)S(1)} %fusion), channel_id=1, source_target_pairs={{1,2},{3,4},{5,6},{2,1},{4,3},{6,5},{9,10},{11,12},{13,14},{10,9},... | collective-permute-start | bytes 122888 | tf_op jit(solution)/shard_map/ppermute | solution.py:310
  5.2 4.8 %collective-permute-start = (bf16[160,128]{1,0:T(8,128)(2,1)S(1)}, bf16[160,128]{1,0:T(8,128)(2,1)S(1)}, u32[]{:S(2)}, u32[]{:S(2)}) collective-permute-start(bf16[160,128]{1,0:T(8,128)(2,1)S(1)} %fusion), channel_id=1, source_target_pairs={{0,1},{1,0},{2,3},{3,2},{4,5},{5,4},{6,7},{7,6},{8,9},{9,8},{10,11... | collective-permute-start | bytes 122888 | tf_op jit(solution)/shard_map/ppermute | solution.py:310
  6.0 0.7 copy-start.7
  6.0 0.7 copy-start.6
  6.0 0.7 copy-start.5
  6.0 0.7 copy-start.4
  6.1 0.7 copy-start.8
  6.8 0.9 %copy-start.1 = (bf16[6,128,128]{2,1,0:T(8,128)(2,1)S(1)}, bf16[6,128,128]{2,1,0:T(8,128)(2,1)}, u32[]{:S(2)}) copy-start(bf16[6,128,128]{2,1,0:T(8,128)(2,1)} %out_hbm.1) | copy-start | bytes 589828
  7.7 0.9 %copy-start.2 = (bf16[6,128,128]{2,1,0:T(8,128)(2,1)S(1)}, bf16[6,128,128]{2,1,0:T(8,128)(2,1)}, u32[]{:S(2)}) copy-start(bf16[6,128,128]{2,1,0:T(8,128)(2,1)} %neigh_hbm.1) | copy-start | bytes 589828
  8.6 1.4 %copy-start = (f32[1,4,4,8,128]{4,3,2,1,0:T(8,128)S(1)}, f32[1,4,4,8,128]{4,3,2,1,0:T(8,128)}, u32[]{:S(2)}) copy-start(f32[1,4,4,8,128]{4,3,2,1,0:T(8,128)} %param.15) | copy-start | bytes 196612
  8.6 1.4 %copy-start.3 = (s32[4,8,128]{2,1,0:T(8,128)S(1)}, s32[4,8,128]{2,1,0:T(8,128)}, u32[]{:S(2)}) copy-start(s32[4,8,128]{2,1,0:T(8,128)} %kind_ref.3) | copy-start | bytes 49156
  8.6 1.4 %copy-start.13 = (bf16[6,128,128]{2,1,0:T(8,128)(2,1)S(1)}, bf16[6,128,128]{2,1,0:T(8,128)(2,1)}, u32[]{:S(2)}) copy-start(bf16[6,128,128]{2,1,0:T(8,128)(2,1)} %self_ref.3) | copy-start | bytes 589828
  10.1 26.1 %copy-start.14 = (f32[4,4,4,8,128]{4,3,2,1,0:T(8,128)S(1)}, f32[4,4,4,8,128]{4,3,2,1,0:T(8,128)}, u32[]{:S(2)}) copy-start(f32[4,4,4,8,128]{4,3,2,1,0:T(8,128)} %param.18) | copy-start | bytes 786436
  32.5 7.9 %collective-permute-start.3 = (bf16[128,128]{1,0:T(8,128)(2,1)S(1)}, bf16[128,128]{1,0:T(8,128)(2,1)S(1)}, u32[]{:S(2)}, u32[]{:S(2)}) collective-permute-start(bf16[128,128]{1,0:T(8,128)(2,1)S(1)} %get-tuple-element.22), channel_id=1, source_target_pairs={{1,2},{3,4},{5,6},{2,1},{4,3},{6,5},{9,10},{11,12},{13,14},{10,9},... | collective-permute-start | bytes 98312 | tf_op jit(solution)/shard_map/ppermute | solution.py:310
  36.0 4.4 %collective-permute-start.2 = (bf16[128,128]{1,0:T(8,128)(2,1)S(1)}, bf16[128,128]{1,0:T(8,128)(2,1)S(1)}, u32[]{:S(2)}, u32[]{:S(2)}) collective-permute-start(bf16[128,128]{1,0:T(8,128)(2,1)S(1)} %get-tuple-element.22), channel_id=1, source_target_pairs={{0,1},{1,0},{2,3},{3,2},{4,5},{5,4},{6,7},{7,6},{8,9},{9,8},{10,11... | collective-permute-start | bytes 98312 | tf_op jit(solution)/shard_map/ppermute | solution.py:310
  63.8 1.3 %collective-permute-start.4 = (f16[4,4,8,128]{3,2,1,0:T(8,128)(2,1)S(1)}, f16[4,4,8,128]{3,2,1,0:T(8,128)(2,1)S(1)}, u32[]{:S(2)}, u32[]{:S(2)}) collective-permute-start(f16[4,4,8,128]{3,2,1,0:T(8,128)(2,1)S(1)} %get-tuple-element.43), channel_id=1, source_target_pairs={{0,8},{8,0},{16,24},{24,16},{32,40},{40,32},{48,56},{56,48},{64,72... | collective-permute-start | bytes 98312 | tf_op jit(solution)/shard_map/ppermute | solution.py:357
  65.1 5.3 %collective-permute-start.5 = (f16[4,4,8,128]{3,2,1,0:T(8,128)(2,1)S(1)}, f16[4,4,8,128]{3,2,1,0:T(8,128)(2,1)S(1)}, u32[]{:S(2)}, u32[]{:S(2)}) collective-permute-start(f16[4,4,8,128]{3,2,1,0:T(8,128)(2,1)S(1)} %get-tuple-element.41), channel_id=1, source_target_pairs={{0,16},{8,24},{16,0},{24,8},{32,48},{40,56},{48,32},{56,40},{64,80... | collective-permute-start | bytes 98312 | tf_op jit(solution)/shard_map/ppermute | solution.py:357
  70.5 7.7 %collective-permute-start.6 = (f16[4,4,8,128]{3,2,1,0:T(8,128)(2,1)S(1)}, f16[4,4,8,128]{3,2,1,0:T(8,128)(2,1)S(1)}, u32[]{:S(2)}, u32[]{:S(2)}) collective-permute-start(f16[4,4,8,128]{3,2,1,0:T(8,128)(2,1)S(1)} %get-tuple-element.39), channel_id=1, source_target_pairs={{0,48},{8,56},{16,32},{24,40},{32,16},{40,24},{48,0},{56,8},{64,11... | collective-permute-start | bytes 98312 | tf_op jit(solution)/shard_map/ppermute | solution.py:357
  78.3 4.0 %collective-permute-start.7 = (f16[4,4,8,128]{3,2,1,0:T(8,128)(2,1)S(1)}, f16[4,4,8,128]{3,2,1,0:T(8,128)(2,1)S(1)}, u32[]{:S(2)}, u32[]{:S(2)}) collective-permute-start(f16[4,4,8,128]{3,2,1,0:T(8,128)(2,1)S(1)} %get-tuple-element.37), channel_id=1, source_target_pairs={{0,64},{8,72},{16,80},{24,88},{32,96},{40,104},{48,112},{56,120},{... | collective-permute-start | bytes 98312 | tf_op jit(solution)/shard_map/ppermute | solution.py:357
  82.3 5.2 %collective-permute-start.8 = (f16[4,4,8,128]{3,2,1,0:T(8,128)(2,1)S(1)}, f16[4,4,8,128]{3,2,1,0:T(8,128)(2,1)S(1)}, u32[]{:S(2)}, u32[]{:S(2)}) collective-permute-start(f16[4,4,8,128]{3,2,1,0:T(8,128)(2,1)S(1)} %add_convert_fusion), channel_id=1, source_target_pairs={{0,192},{8,200},{16,208},{24,216},{32,224},{40,232},{48,240},{56,2... | collective-permute-start | bytes 98312 | tf_op jit(solution)/shard_map/ppermute | solution.py:357

commit v9 on v8

--- a/solution.py
+++ b/solution.py
@@ -150,33 +150,42 @@
                 rows.append(jnp.concatenate([mid, along_x + along_y + along_z], axis=-1))
         return jnp.concatenate(rows, axis=0)
 
-    def turn(_, pairs):
-        newest, second, third = pairs
-        half = enter_ref[...]
-        message = half * jnp.tanh(half) + half
-        leave = jnp.concatenate(
-            [twice(out_ref[second[0], :HID]), twice(out_ref[second[0], HID:])], axis=0
-        )
-        moved = dot(jnp.concatenate([message, message], axis=-1), leave)
-        enter = jnp.concatenate([self_ref[newest[0]], neigh_ref[newest[0]]], axis=0)
-        entered = dot(gather(*newest), enter)
-        entered = (entered + bias_ref[newest[0]]).astype(BF16)
-        for at, (d, z) in enumerate(tiles):
-            enter_ref[z * NY : (z + 1) * NY, d * HID : (d + 1) * HID] = entered[at * NY : (at + 1) * NY]
-        outside = jnp.logical_and(at_right, third[1] + 1 == 2 * BLOCK)
-        slot = (third[0] + 1) % 2
-        for d, z in tiles:
-            row = third[1] if d == 0 else jnp.where(outside, SPARE, third[1] + 1)
-            normalize(third[0] + 1, hidden_ref[third[1] + d, z], norm_ref.at[slot, row, z])
-        for d, z in tiles:
-            hidden_ref[second[1] + d, z] += moved[z * NY : (z + 1) * NY, d * HID : (d + 1) * HID]
-        layer, x = newest
+    def work(newest, second, third):
+        if second is not None:
+            half = enter_ref[...]
+            message = half * jnp.tanh(half) + half
+            leave = jnp.concatenate(
+                [twice(out_ref[second[0], :HID]), twice(out_ref[second[0], HID:])], axis=0
+            )
+            moved = dot(jnp.concatenate([message, message], axis=-1), leave)
+        if newest is not None:
+            enter = jnp.concatenate([self_ref[newest[0]], neigh_ref[newest[0]]], axis=0)
+            entered = dot(gather(*newest), enter)
+            entered = (entered + bias_ref[newest[0]]).astype(BF16)
+            for at, (d, z) in enumerate(tiles):
+                enter_ref[z * NY : (z + 1) * NY, d * HID : (d + 1) * HID] = entered[at * NY : (at + 1) * NY]
+        if third is not None:
+            outside = jnp.logical_and(at_right, third[1] + 1 == 2 * BLOCK)
+            slot = (third[0] + 1) % 2
+            for d, z in tiles:
+                row = third[1] if d == 0 else jnp.where(outside, SPARE, third[1] + 1)
+                normalize(third[0] + 1, hidden_ref[third[1] + d, z], norm_ref.at[slot, row, z])
+        if second is not None:
+            for d, z in tiles:
+                hidden_ref[second[1] + d, z] += moved[z * NY : (z + 1) * NY, d * HID : (d + 1) * HID]
+
+    def after(pair):
+        layer, x = pair
         ends = x + 2 >= rows_of(layer)[1]
         next_layer = jnp.where(ends, layer + 1, layer)
         next_x = jnp.where(ends, rows_of(layer + 1)[0], x + 2)
         done = next_layer >= LAYERS
-        following = (jnp.where(done, 0, next_layer), jnp.where(done, SPARE, next_x))
-        return following, newest, second
+        return (jnp.where(done, 0, next_layer), jnp.where(done, SPARE, next_x))
+
+    def turn(_, pairs):
+        newest, second, third = pairs
+        work(newest, second, third)
+        return after(newest), newest, second
 
     def count(layer):
         low, high = rows_of(layer)
@@ -185,7 +194,10 @@
     total = sum(count(layer) for layer in range(LAYERS))
     none = (jnp.int32(0), jnp.int32(SPARE))
     start = (jnp.int32(0), rows_of(0)[0])
-    lax.fori_loop(0, total + 2, turn, (start, none, none))
+    work(start, None, None)
+    _, second, third = lax.fori_loop(0, total - 1, turn, (after(start), start, none))
+    work(None, second, third)
+    work(None, None, second)
 
     found = []
     for z in range(NZ):

time: 88.5 us -> 87.7 us (level)
  Pallas kernels: 47.1 us -> 46.1 us
    pallas_call x2, Pallas kernels: 45.7 us -> 44.7 us  [run_fine_step(): pl.pallas_call(fine_step, out_shape=(jax.ShapeDtypeStruct((CHAN, NZ, BLOC...]
where the time goes in v9:
time: 87.7 us; the launch traced here: 86.9 us
  Pallas kernels  46.1 us (53%)
  starting transfers between devices  19 us (22%)
  waiting for transfers between devices  16.2 us (18%)
  other arithmetic  2.68 us (3%)
  local copies, waits for them, and re-layouts  2.56 us (3%)
    pallas_call x2, Pallas kernels, run_fine_step(): pl.pallas_call(fine_step, out_shape=(jax.ShapeDtypeStruct((CHAN, NZ, BLOC...  44.7 us
    ppermute x5, waiting for transfers between devices, per_device(): came = lax.ppermute(total.astype(jnp.float16), 'tm', partners).astype(F32)  12 us
    ppermute x5, starting transfers between devices, per_device(): came = lax.ppermute(total.astype(jnp.float16), 'tm', partners).astype(F32)  10.3 us
    ppermute x2, starting transfers between devices, exchange(): lax.ppermute(value, 'space', second)  7.74 us
    ppermute x2, waiting for transfers between devices, exchange(): lax.ppermute(value, 'space', second)  4.2 us
    unnamed x30, local copies, waits for them, and re-layouts  2.56 us
  transfers between devices with their start and end apart: 9, of which 6 were waited for; matrix products, arithmetic and copies ran while one was open for 1% of the time, Pallas kernels for 2%

profile of v9, /device:TPU:56, one launch (start us, length us, event | category | flops | bytes accessed | tf_op | source)
XLA Modules:
  0.0 86.9 jit_solution(2749421298696865527)
XLA Ops:
  0.0 1.0 %fusion = bf16[160,128]{1,0:T(8,128)(2,1)S(1)} fusion(s32[4,8,128]{2,1,0:T(8,128)} %kind_ref.3, f32[16,8,128]{2,1,0:T(8,128)} %bitcast.9, pred[20]{0:T(512)(128)(4,1)S(1)} %iota_compare_fusion), kind=kLoop, calls=%fused_computation.26 | loop fusion | flops 40960 | bytes 122900 | tf_op jit(solution)/shard_map/reshape | solution.py:345
  1.0 4.2 %collective-permute-start.1 = (bf16[160,128]{1,0:T(8,128)(2,1)S(1)}, bf16[160,128]{1,0:T(8,128)(2,1)S(1)}, u32[]{:S(2)}, u32[]{:S(2)}) collective-permute-start(bf16[160,128]{1,0:T(8,128)(2,1)S(1)} %fusion), channel_id=1, source_target_pairs={{1,2},{3,4},{5,6},{2,1},{4,3},{6,5},{9,10},{11,12},{13,14},{10,9},... | collective-permute-start | bytes 122888 | tf_op jit(solution)/shard_map/ppermute | solution.py:322
  5.2 0.8 collective-permute-start
  6.0 0.1 pad_add_fusion.where_ref
  6.1 0.6 copy-done.7
  6.7 0.0 copy-done.5
  6.7 0.0 copy-done.8
  6.8 0.9 %copy-done.1 = bf16[6,128,128]{2,1,0:T(8,128)(2,1)S(1)} copy-done((bf16[6,128,128]{2,1,0:T(8,128)(2,1)S(1)}, bf16[6,128,128]{2,1,0:T(8,128)(2,1)}, u32[]{:S(2)}) %copy-start.1) | copy-done | bytes 196632
  7.7 0.9 %copy-done.2 = bf16[6,128,128]{2,1,0:T(8,128)(2,1)S(1)} copy-done((bf16[6,128,128]{2,1,0:T(8,128)(2,1)S(1)}, bf16[6,128,128]{2,1,0:T(8,128)(2,1)}, u32[]{:S(2)}) %copy-start.2) | copy-done | bytes 196632
  8.6 1.4 %prepare.1 = (bf16[112,1024]{1,0:T(8,128)(2,1)S(1)}, bf16[112,1024]{1,0:T(8,128)(2,1)S(1)}, bf16[6,128,128]{2,1,0:T(8,128)(2,1)S(1)}, bf16[6,256,128]{2,1,0:T(8,...) custom-call(s32[1,2]{1,0:T(1,128)S(1)} %copy-done.9, ...), custom_call_target="tpu_custom_call" | custom-call | flops 100000000 | bytes 2097152 | tf_op jit(solution)/shard_map/prepare/pallas_call | solution.py:305
  10.1 21.9 %fine_step.2 = (f32[4,4,8,128]{3,2,1,0:T(8,128)S(1)}, bf16[128,128]{1,0:T(8,128)(2,1)S(1)}) custom-call(s32[2]{0:T(128)S(1)} %pad_add_fusion.where_ref, f32[4,4,8,128]{3,2,1,0:T(8,128)S(1)} %bitcast.10, bf16[160,128]{1,0:T(8,128)(2,1)S(1)} %collective-permute-done.first_ref.kind_first_ref, ...), custom_call_target="tpu_custom_call" | custom-call | flops 10000000000 | bytes 2097152 | tf_op jit(solution)/shard_map/fine_step/pallas_call | solution.py:221
  32.0 3.5 %collective-permute-start.3 = (bf16[128,128]{1,0:T(8,128)(2,1)S(1)}, bf16[128,128]{1,0:T(8,128)(2,1)S(1)}, u32[]{:S(2)}, u32[]{:S(2)}) collective-permute-start(bf16[128,128]{1,0:T(8,128)(2,1)S(1)} %get-tuple-element.22), channel_id=1, source_target_pairs={{1,2},{3,4},{5,6},{2,1},{4,3},{6,5},{9,10},{11,12},{13,14},{10,9},... | collective-permute-start | bytes 98312 | tf_op jit(solution)/shard_map/ppermute | solution.py:322
  35.5 0.1 collective-permute-start.2
  35.7 4.2 %collective-permute-done.3.second_ref = bf16[128,128]{1,0:T(8,128)(2,1)S(1)} collective-permute-done((bf16[128,128]{1,0:T(8,128)(2,1)S(1)}, bf16[128,128]{1,0:T(8,128)(2,1)S(1)}, u32[]{:S(2)}, u32[]{:S(2)}) %collective-permute-start.3) | collective-permute-done | bytes 32800 | tf_op jit(solution)/shard_map/ppermute | solution.py:322
  39.9 22.8 %fine_step.3 = (f32[4,4,8,128]{3,2,1,0:T(8,128)S(1)}, bf16[128,128]{1,0:T(8,128)(2,1)}) custom-call(s32[2]{0:T(128)S(1)} %pad_add_fusion.where_ref, f32[4,4,8,128]{3,2,1,0:T(8,128)S(1)} %get-tuple-element.21.own_ref, bf16[128,128]{1,0:T(8,128)(2,1)S(1)} %collective-permute-done.2.first_ref, bf16[128,128]{1,0:T(8,128)(2,1)S(1)} %collective-permute-done.3.second_ref, ...), custom_call_target="tpu_custom_call" | custom-call | flops 10000000000 | bytes 2097152 | tf_op jit(solution)/shard_map/fine_step/pallas_call | solution.py:221
  62.7 0.1 collective-permute-start.4
  62.9 1.2 %collective-permute-done.4 = f16[4,4,8,128]{3,2,1,0:T(8,128)(2,1)S(1)} collective-permute-done((f16[4,4,8,128]{3,2,1,0:T(8,128)(2,1)S(1)}, f16[4,4,8,128]{3,2,1,0:T(8,128)(2,1)S(1)}, u32[]{:S(2)}, u32[]{:S(2)}) %collective-permute-start.4) | collective-permute-done | bytes 32800 | tf_op jit(solution)/shard_map/ppermute | solution.py:369
  64.1 3.7 %collective-permute-start.5 = (f16[4,4,8,128]{3,2,1,0:T(8,128)(2,1)S(1)}, f16[4,4,8,128]{3,2,1,0:T(8,128)(2,1)S(1)}, u32[]{:S(2)}, u32[]{:S(2)}) collective-permute-start(f16[4,4,8,128]{3,2,1,0:T(8,128)(2,1)S(1)} %get-tuple-element.41), channel_id=1, source_target_pairs={{0,16},{8,24},{16,0},{24,8},{32,48},{40,56},{48,32},{56,40},{64,80... | collective-permute-start | bytes 98312 | tf_op jit(solution)/shard_map/ppermute | solution.py:369
  67.8 0.1 multiply_reduce_fusion.5
  68.0 1.7 %collective-permute-done.5 = f16[4,4,8,128]{3,2,1,0:T(8,128)(2,1)S(1)} collective-permute-done((f16[4,4,8,128]{3,2,1,0:T(8,128)(2,1)S(1)}, f16[4,4,8,128]{3,2,1,0:T(8,128)(2,1)S(1)}, u32[]{:S(2)}, u32[]{:S(2)}) %collective-permute-start.5) | collective-permute-done | bytes 32800 | tf_op jit(solution)/shard_map/ppermute | solution.py:369
  69.7 0.1 multiply_reduce_fusion.12
  69.8 5.1 %collective-permute-start.6 = (f16[4,4,8,128]{3,2,1,0:T(8,128)(2,1)S(1)}, f16[4,4,8,128]{3,2,1,0:T(8,128)(2,1)S(1)}, u32[]{:S(2)}, u32[]{:S(2)}) collective-permute-start(f16[4,4,8,128]{3,2,1,0:T(8,128)(2,1)S(1)} %get-tuple-element.39), channel_id=1, source_target_pairs={{0,48},{8,56},{16,32},{24,40},{32,16},{40,24},{48,0},{56,8},{64,11... | collective-permute-start | bytes 98312 | tf_op jit(solution)/shard_map/ppermute | solution.py:369
  74.9 0.2 multiply_reduce_fusion.3
  75.1 1.7 %collective-permute-done.6 = f16[4,4,8,128]{3,2,1,0:T(8,128)(2,1)S(1)} collective-permute-done((f16[4,4,8,128]{3,2,1,0:T(8,128)(2,1)S(1)}, f16[4,4,8,128]{3,2,1,0:T(8,128)(2,1)S(1)}, u32[]{:S(2)}, u32[]{:S(2)}) %collective-permute-start.6) | collective-permute-done | bytes 32800 | tf_op jit(solution)/shard_map/ppermute | solution.py:369
  76.9 0.8 collective-permute-start.7
  77.8 0.2 multiply_reduce_fusion.1
  78.0 2.9 %collective-permute-done.7 = f16[4,4,8,128]{3,2,1,0:T(8,128)(2,1)S(1)} collective-permute-done((f16[4,4,8,128]{3,2,1,0:T(8,128)(2,1)S(1)}, f16[4,4,8,128]{3,2,1,0:T(8,128)(2,1)S(1)}, u32[]{:S(2)}, u32[]{:S(2)}) %collective-permute-start.7) | collective-permute-done | bytes 32800 | tf_op jit(solution)/shard_map/ppermute | solution.py:369
  81.0 0.6 collective-permute-start.8
  81.6 0.1 multiply_reduce_fusion
  81.7 4.5 %collective-permute-done.8 = f16[4,4,8,128]{3,2,1,0:T(8,128)(2,1)S(1)} collective-permute-done((f16[4,4,8,128]{3,2,1,0:T(8,128)(2,1)S(1)}, f16[4,4,8,128]{3,2,1,0:T(8,128)(2,1)S(1)}, u32[]{:S(2)}, u32[]{:S(2)}) %collective-permute-start.8) | collective-permute-done | bytes 32800 | tf_op jit(solution)/shard_map/ppermute | solution.py:369
  86.2 0.1 multiply_reduce_fusion.8
  86.2 0.7 add_bitcast_fusion
  (49 shorter events, 0.5 us)
Async XLA Ops:
  0.0 6.1 %copy-start.9 = (s32[1,2]{1,0:T(1,128)S(1)}, s32[1,2]{1,0:T(1,128)}, u32[]{:S(2)}) copy-start(s32[1,2]{1,0:T(1,128)} %plan_ref.1) | copy-start | bytes 28
  0.0 6.1 %copy-start.10 = (f32[8]{0:T(128)S(1)}, f32[8]{0:T(128)}, u32[]{:S(2)}) copy-start(f32[8]{0:T(128)} %rate_ref.1) | copy-start | bytes 100
  0.0 6.1 %copy-start.11 = (f32[128]{0:T(128)S(1)}, f32[128]{0:T(128)}, u32[]{:S(2)}) copy-start(f32[128]{0:T(128)} %param.22) | copy-start | bytes 1540
  0.0 6.1 %copy-start.12 = (f32[128]{0:T(128)S(1)}, f32[128]{0:T(128)}, u32[]{:S(2)}) copy-start(f32[128]{0:T(128)} %param.28) | copy-start | bytes 1540
  1.0 9.0 %collective-permute-start.1 = (bf16[160,128]{1,0:T(8,128)(2,1)S(1)}, bf16[160,128]{1,0:T(8,128)(2,1)S(1)}, u32[]{:S(2)}, u32[]{:S(2)}) collective-permute-start(bf16[160,128]{1,0:T(8,128)(2,1)S(1)} %fusion), channel_id=1, source_target_pairs={{1,2},{3,4},{5,6},{2,1},{4,3},{6,5},{9,10},{11,12},{13,14},{10,9},... | collective-permute-start | bytes 122888 | tf_op jit(solution)/shard_map/ppermute | solution.py:322
  5.2 4.8 %collective-permute-start = (bf16[160,128]{1,0:T(8,128)(2,1)S(1)}, bf16[160,128]{1,0:T(8,128)(2,1)S(1)}, u32[]{:S(2)}, u32[]{:S(2)}) collective-permute-start(bf16[160,128]{1,0:T(8,128)(2,1)S(1)} %fusion), channel_id=1, source_target_pairs={{0,1},{1,0},{2,3},{3,2},{4,5},{5,4},{6,7},{7,6},{8,9},{9,8},{10,11... | collective-permute-start | bytes 122888 | tf_op jit(solution)/shard_map/ppermute | solution.py:322
  6.0 0.7 copy-start.7
  6.0 0.7 copy-start.6
  6.0 0.7 copy-start.5
  6.0 0.7 copy-start.4
  6.1 0.7 copy-start.8
  6.8 0.9 %copy-start.1 = (bf16[6,128,128]{2,1,0:T(8,128)(2,1)S(1)}, bf16[6,128,128]{2,1,0:T(8,128)(2,1)}, u32[]{:S(2)}) copy-start(bf16[6,128,128]{2,1,0:T(8,128)(2,1)} %out_hbm.1) | copy-start | bytes 589828
  7.7 0.9 %copy-start.2 = (bf16[6,128,128]{2,1,0:T(8,128)(2,1)S(1)}, bf16[6,128,128]{2,1,0:T(8,128)(2,1)}, u32[]{:S(2)}) copy-start(bf16[6,128,128]{2,1,0:T(8,128)(2,1)} %neigh_hbm.1) | copy-start | bytes 589828
  8.6 1.4 %copy-start = (f32[1,4,4,8,128]{4,3,2,1,0:T(8,128)S(1)}, f32[1,4,4,8,128]{4,3,2,1,0:T(8,128)}, u32[]{:S(2)}) copy-start(f32[1,4,4,8,128]{4,3,2,1,0:T(8,128)} %param.15) | copy-start | bytes 196612
  8.6 1.4 %copy-start.3 = (s32[4,8,128]{2,1,0:T(8,128)S(1)}, s32[4,8,128]{2,1,0:T(8,128)}, u32[]{:S(2)}) copy-start(s32[4,8,128]{2,1,0:T(8,128)} %kind_ref.3) | copy-start | bytes 49156
  8.6 1.4 %copy-start.13 = (bf16[6,128,128]{2,1,0:T(8,128)(2,1)S(1)}, bf16[6,128,128]{2,1,0:T(8,128)(2,1)}, u32[]{:S(2)}) copy-start(bf16[6,128,128]{2,1,0:T(8,128)(2,1)} %self_ref.3) | copy-start | bytes 589828
  10.1 25.6 %copy-start.14 = (f32[4,4,4,8,128]{4,3,2,1,0:T(8,128)S(1)}, f32[4,4,4,8,128]{4,3,2,1,0:T(8,128)}, u32[]{:S(2)}) copy-start(f32[4,4,4,8,128]{4,3,2,1,0:T(8,128)} %param.18) | copy-start | bytes 786436
  32.0 7.9 %collective-permute-start.3 = (bf16[128,128]{1,0:T(8,128)(2,1)S(1)}, bf16[128,128]{1,0:T(8,128)(2,1)S(1)}, u32[]{:S(2)}, u32[]{:S(2)}) collective-permute-start(bf16[128,128]{1,0:T(8,128)(2,1)S(1)} %get-tuple-element.22), channel_id=1, source_target_pairs={{1,2},{3,4},{5,6},{2,1},{4,3},{6,5},{9,10},{11,12},{13,14},{10,9},... | collective-permute-start | bytes 98312 | tf_op jit(solution)/shard_map/ppermute | solution.py:322
  35.5 4.4 %collective-permute-start.2 = (bf16[128,128]{1,0:T(8,128)(2,1)S(1)}, bf16[128,128]{1,0:T(8,128)(2,1)S(1)}, u32[]{:S(2)}, u32[]{:S(2)}) collective-permute-start(bf16[128,128]{1,0:T(8,128)(2,1)S(1)} %get-tuple-element.22), channel_id=1, source_target_pairs={{0,1},{1,0},{2,3},{3,2},{4,5},{5,4},{6,7},{7,6},{8,9},{9,8},{10,11... | collective-permute-start | bytes 98312 | tf_op jit(solution)/shard_map/ppermute | solution.py:322
  62.7 1.3 %collective-permute-start.4 = (f16[4,4,8,128]{3,2,1,0:T(8,128)(2,1)S(1)}, f16[4,4,8,128]{3,2,1,0:T(8,128)(2,1)S(1)}, u32[]{:S(2)}, u32[]{:S(2)}) collective-permute-start(f16[4,4,8,128]{3,2,1,0:T(8,128)(2,1)S(1)} %get-tuple-element.43), channel_id=1, source_target_pairs={{0,8},{8,0},{16,24},{24,16},{32,40},{40,32},{48,56},{56,48},{64,72... | collective-permute-start | bytes 98312 | tf_op jit(solution)/shard_map/ppermute | solution.py:369
  64.1 5.6 %collective-permute-start.5 = (f16[4,4,8,128]{3,2,1,0:T(8,128)(2,1)S(1)}, f16[4,4,8,128]{3,2,1,0:T(8,128)(2,1)S(1)}, u32[]{:S(2)}, u32[]{:S(2)}) collective-permute-start(f16[4,4,8,128]{3,2,1,0:T(8,128)(2,1)S(1)} %get-tuple-element.41), channel_id=1, source_target_pairs={{0,16},{8,24},{16,0},{24,8},{32,48},{40,56},{48,32},{56,40},{64,80... | collective-permute-start | bytes 98312 | tf_op jit(solution)/shard_map/ppermute | solution.py:369
  69.8 7.0 %collective-permute-start.6 = (f16[4,4,8,128]{3,2,1,0:T(8,128)(2,1)S(1)}, f16[4,4,8,128]{3,2,1,0:T(8,128)(2,1)S(1)}, u32[]{:S(2)}, u32[]{:S(2)}) collective-permute-start(f16[4,4,8,128]{3,2,1,0:T(8,128)(2,1)S(1)} %get-tuple-element.39), channel_id=1, source_target_pairs={{0,48},{8,56},{16,32},{24,40},{32,16},{40,24},{48,0},{56,8},{64,11... | collective-permute-start | bytes 98312 | tf_op jit(solution)/shard_map/ppermute | solution.py:369
  76.9 4.0 %collective-permute-start.7 = (f16[4,4,8,128]{3,2,1,0:T(8,128)(2,1)S(1)}, f16[4,4,8,128]{3,2,1,0:T(8,128)(2,1)S(1)}, u32[]{:S(2)}, u32[]{:S(2)}) collective-permute-start(f16[4,4,8,128]{3,2,1,0:T(8,128)(2,1)S(1)} %get-tuple-element.37), channel_id=1, source_target_pairs={{0,64},{8,72},{16,80},{24,88},{32,96},{40,104},{48,112},{56,120},{... | collective-permute-start | bytes 98312 | tf_op jit(solution)/shard_map/ppermute | solution.py:369
  81.0 5.2 %collective-permute-start.8 = (f16[4,4,8,128]{3,2,1,0:T(8,128)(2,1)S(1)}, f16[4,4,8,128]{3,2,1,0:T(8,128)(2,1)S(1)}, u32[]{:S(2)}, u32[]{:S(2)}) collective-permute-start(f16[4,4,8,128]{3,2,1,0:T(8,128)(2,1)S(1)} %add_convert_fusion), channel_id=1, source_target_pairs={{0,192},{8,200},{16,208},{24,216},{32,224},{40,232},{48,240},{56,2... | collective-permute-start | bytes 98312 | tf_op jit(solution)/shard_map/ppermute | solution.py:369
